TPU v7x, 32 devices: a whole 2x2x4 slice. The times are simulated.
32 devices in a mesh: fsdp: 8 (over z, y), seq: 4 (over x, core).
Axes of the slice: x: 2, y: 2, z: 4, core: 2. Of those that a mesh axis runs over, the one named last changes fastest.
Arguments:
- queries: bfloat16 [4096, 4096], P(('fsdp', 'seq')), may hold values from -6 to 6
- keys: bfloat16 [4096, 4096], P(('fsdp', 'seq')), may hold values from -6 to 6
- values: bfloat16 [4096, 4096], P(('fsdp', 'seq')), may hold values from -6 to 6
- cotangent: bfloat16 [4096, 4096], P(('fsdp', 'seq')), may hold values from -8 to 8
- out_weight: bfloat16 [4096, 4096], P('seq', 'fsdp'), may hold values from -0.09375 to 0.09375
- short_taps: float32 [3, 7, 4096], P(None, None, 'seq'), may hold values from -2 to 2
- long_taps: float32 [128, 256], P(None, 'seq'), may hold values from -0.5 to 0.5
- skip_gain: float32 [4096], P('seq'), may hold values from -1 to 1
Outputs:
- query_grad: bfloat16 [4096, 4096], P(('fsdp', 'seq'))
- key_grad: bfloat16 [4096, 4096], P(('fsdp', 'seq'))
- value_grad: bfloat16 [4096, 4096], P(('fsdp', 'seq'))
- weight_grad: float32 [4096, 4096], P('seq', 'fsdp')
- short_grad: float32 [3, 7, 4096], P(None, None, 'seq')
- long_grad: float32 [128, 256], P(None, 'seq')
- gain_grad: float32 [4096], P('seq')
All inputs are finite; a program needn't handle non-finite values.
Results may differ from a plain program's by a relative error of at most 0.0075.
Values may be sent and summed in bfloat16 or wider, within the bound.
No kernel may reach another device: no remote copies, remote signals or barrier semaphores. Data moves between devices by JAX's collectives and lax.ppermute only.
A program may use at most 256 MiB of HBM per device.

v0:
```python
import functools

import jax
import jax.numpy as jnp
from jax import lax
from jax.experimental import pallas as pl
from jax.experimental.pallas import tpu as pltpu
from jax.sharding import Mesh
from jax.sharding import PartitionSpec as P

SHORT = 7
LTAPS = 128
LANES = 128
PAD = 16
Z = 4
F32 = jnp.float32
BF16 = jnp.bfloat16


def params(mib):
    return pltpu.CompilerParams(vmem_limit_bytes=mib * 2**20)


def cost(flops, nbytes):
    return pl.CostEstimate(flops=flops, bytes_accessed=nbytes, transcendentals=0)


def tables_kernel(fwd_ref, bwd_ref, tf_ref, tb_ref):
    for g in range(fwd_ref.shape[0]):
        rows = slice(g * LTAPS, (g + 1) * LTAPS)
        for src, dst in ((fwd_ref, tf_ref), (bwd_ref, tb_ref)):
            wide = jnp.broadcast_to(src[g : g + 1, :], (LTAPS, 2 * LTAPS))
            dst[rows, :] = pltpu.roll(wide, 0, 1, stride=1, stride_axis=0).astype(BF16)


def make_tables(long_taps):
    by_group = long_taps.T
    groups = by_group.shape[0]
    fwd = jnp.pad(by_group[:, ::-1], ((0, 0), (1, LTAPS - 1)))
    bwd = jnp.pad(by_group, ((0, 0), (0, LTAPS)))
    per = 8
    row_spec = pl.BlockSpec((per, 2 * LTAPS), lambda i: (i, 0))
    tab_spec = pl.BlockSpec((per * LTAPS, 2 * LTAPS), lambda i: (i, 0))
    shape = jax.ShapeDtypeStruct((groups * LTAPS, 2 * LTAPS), BF16)
    return pl.pallas_call(
        tables_kernel,
        grid=(groups // per,),
        in_specs=[row_spec, row_spec],
        out_specs=[tab_spec, tab_spec],
        out_shape=[shape, shape],
        compiler_params=params(32),
        name="tables",
    )(fwd, bwd)


def pick_groups(wide, col, rows, per):
    lane_group = lax.broadcasted_iota(jnp.int32, (rows, LANES), 1) // (LANES // per)
    cols = slice(col * LANES, (col + 1) * LANES)
    out = wide[0:rows, cols]
    for g in range(1, per):
        out = jnp.where(lane_group == g, wide[g * rows : (g + 1) * rows, cols], out)
    return out


def forward_kernel(place_ref, x_ref, h_ref, taps_ref, skip_ref, tab_ref, mixed_ref, f_ref, filt_ref, xf, pf, pb, wide):
    blocks, _, rows, _ = x_ref.shape
    tokens = blocks * rows
    per = tab_ref.shape[0] // LTAPS
    xf[0, LTAPS : LTAPS + PAD] = h_ref[0:PAD].astype(F32)
    for i in (1, 2):
        begin = PAD + (i - 1) * (LTAPS + PAD)
        xf[i, 0 : LTAPS + PAD] = h_ref[begin : begin + LTAPS + PAD].astype(F32)
    for i in range(3):
        for b in range(blocks):
            begin = LTAPS + PAD + b * rows
            xf[i, begin : begin + rows] = x_ref[b, i].astype(F32)

    def feature(i, base):
        total = taps_ref[i, 0:1] * xf[i, PAD + base : PAD + base + LTAPS]
        for j in range(1, SHORT):
            total = total + taps_ref[i, j : j + 1] * xf[i, PAD + base - j : PAD + base - j + LTAPS]
        return total

    for n in range(tokens // LTAPS + 1):
        base = n * LTAPS
        own = slice(base - LTAPS, base)
        f1 = feature(1, base)
        f2 = feature(2, base)
        prod = f1 * f2
        pb[base : base + LTAPS] = prod.astype(BF16)
        if n:
            f_ref[1, own] = f1
            f_ref[2, own] = f2
            f_ref[0, own] = feature(0, base)
            pf[own] = prod
    skip = skip_ref[...]
    for b in range(0, tokens // LTAPS, 2):
        low = b * LTAPS
        windows = jnp.concatenate([pb[low : low + 2 * LTAPS], pb[low + LTAPS : low + 3 * LTAPS]], axis=1)
        wide[...] = jnp.dot(tab_ref[...], windows, preferred_element_type=F32)
        for n in range(2):
            own = slice(low + n * LTAPS, low + (n + 1) * LTAPS)
            filtered = pick_groups(wide, n, LTAPS, per) + skip * pf[own]
            filt_ref[own] = filtered
            mixed = f_ref[0, own] * filtered
            there = pl.multiple_of(place_ref[b + n] * LTAPS, LTAPS)
            mixed_ref[:, pl.ds(there, LTAPS)] = mixed.T.astype(BF16)


def forward(x, halo, short_taps, skip, table, place, chunk, chunks):
    blocks, _, rows, cols = x.shape
    cols //= chunks
    tokens = blocks * rows
    tiles = cols // LANES
    first = chunk * tiles
    tab_rows = table.shape[0] * LANES // skip.shape[1]
    return pl.pallas_call(
        forward_kernel,
        grid_spec=pltpu.PrefetchScalarGridSpec(
            num_scalar_prefetch=1,
            grid=(tiles,),
            in_specs=[
                pl.BlockSpec((blocks, 3, rows, LANES), lambda c, _: (0, 0, 0, first + c)),
                pl.BlockSpec((halo.shape[0], LANES), lambda c, _: (0, first + c)),
                pl.BlockSpec((3, SHORT, LANES), lambda c, _: (0, 0, first + c)),
                pl.BlockSpec((1, LANES), lambda c, _: (0, first + c)),
                pl.BlockSpec((tab_rows, 2 * LTAPS), lambda c, _: (first + c, 0)),
            ],
            out_specs=[
                pl.BlockSpec((LANES, tokens), lambda c, _: (c, 0)),
                pl.BlockSpec((3, tokens, LANES), lambda c, _: (0, 0, c)),
                pl.BlockSpec((tokens, LANES), lambda c, _: (0, c)),
            ],
            scratch_shapes=[
                pltpu.VMEM((3, PAD + LTAPS + tokens, LANES), F32),
                pltpu.VMEM((tokens, LANES), F32),
                pltpu.VMEM((LTAPS + tokens, LANES), BF16),
                pltpu.VMEM((tab_rows, 2 * LTAPS), F32),
            ],
        ),
        out_shape=[
            jax.ShapeDtypeStruct((cols, tokens), BF16),
            jax.ShapeDtypeStruct((3, tokens, cols), F32),
            jax.ShapeDtypeStruct((tokens, cols), F32),
        ],
        compiler_params=params(48),
        cost_estimate=cost(4 * LTAPS * tokens * tab_rows, 24 * tokens * cols),
        name="forward",
    )(place, x, halo, short_taps, skip, table)


def sum_by_lag(gram):
    wide = gram.shape[1]
    parts = [gram[i : i + 8] for i in range(0, gram.shape[0], 8)]
    step = 8
    while len(parts) > 1:
        parts = [
            parts[k] + pltpu.roll(parts[k + 1], wide - step, 1) for k in range(0, len(parts), 2)
        ]
        step *= 2
    total = parts[0]
    row = lax.broadcasted_iota(jnp.int32, total.shape, 0)
    for bit in (1, 2, 4):
        total = jnp.where((row & bit) != 0, pltpu.roll(total, wide - bit, 1), total)
    return jnp.sum(total[:, :LTAPS], axis=0, keepdims=True)


def backward_kernel(
    mo_ref, mr_ref, f_ref, filt_ref, x_ref, n_ref, taps_ref, skip_ref, tab_ref,
    grad_ref, short_ref, long_ref, db, fg, wide, left, right,
):
    blocks, _, rows, _ = x_ref.shape
    tokens = blocks * rows
    per = tab_ref.shape[0] // LTAPS
    count = tokens // LTAPS
    skip = skip_ref[...]
    lane_group = lax.broadcasted_iota(jnp.int32, (1, LANES), 1) // (LANES // per)
    gain = jnp.zeros((8, LANES), F32)
    for b in range(count):
        own = slice(b * LTAPS, (b + 1) * LTAPS)
        mixed_grad = mo_ref[own] + mr_ref[own].astype(F32)
        slope = mixed_grad * f_ref[0, own]
        db[own] = slope.astype(BF16)
        fg[0, own] = mixed_grad * filt_ref[own]
        fg[1, own] = skip * slope
        prod = f_ref[1, own] * f_ref[2, own]
        gain = gain + jnp.sum((prod * slope).reshape(LTAPS // 8, 8, LANES), axis=0)
        prod_b = prod.astype(BF16)
        for g in range(per):
            keep = (lane_group == g).astype(F32).astype(BF16)
            left[g * LTAPS : (g + 1) * LTAPS, b * LANES : (b + 1) * LANES] = prod_b * keep
    db[tokens : tokens + LTAPS + PAD] = n_ref[0 : LTAPS + PAD]
    db[tokens + LTAPS + PAD :] = jnp.zeros((LTAPS - PAD, LANES), BF16)
    for b in range(count):
        right[:, b * LANES : (b + 1) * LANES] = db[b * LTAPS : (b + 2) * LTAPS]
    for b in range(0, count, 2):
        wide[...] = jnp.dot(
            tab_ref[...], right[:, b * LANES : (b + 2) * LANES], preferred_element_type=F32
        )
        for n in range(2):
            own = slice((b + n) * LTAPS, (b + n + 1) * LTAPS)
            grad = pick_groups(wide, n, LTAPS, per) + fg[1, own]
            fg[1, own] = grad * f_ref[2, own]
            fg[2, own] = grad * f_ref[1, own]
    few = jnp.concatenate([tab_ref[g * LTAPS : g * LTAPS + PAD] for g in range(per)], axis=0)
    edge = jnp.dot(few, db[tokens : tokens + 2 * LTAPS], preferred_element_type=F32)
    begin = LTAPS + PAD
    grad = pick_groups(edge, 0, PAD, per) + skip * n_ref[0:PAD].astype(F32)
    fg[1, tokens : tokens + PAD] = grad * n_ref[begin + PAD : begin + 2 * PAD].astype(F32)
    fg[2, tokens : tokens + PAD] = grad * n_ref[begin : begin + PAD].astype(F32)
    fg[0, tokens : tokens + PAD] = n_ref[begin + 2 * PAD : begin + 3 * PAD].astype(F32)
    for i in range(3):
        sums = [jnp.zeros((8, LANES), F32) for _ in range(SHORT)]
        for b in range(count):
            low = b * LTAPS
            inputs = x_ref[b, i].astype(F32)
            total = None
            for j in range(SHORT):
                later = fg[i, low + j : low + j + LTAPS]
                term = taps_ref[i, j : j + 1] * later
                total = term if total is None else total + term
                sums[j] = sums[j] + jnp.sum((later * inputs).reshape(LTAPS // 8, 8, LANES), axis=0)
            grad_ref[b, i] = total.astype(BF16)
        for j in range(SHORT):
            short_ref[i, j : j + 1] = jnp.sum(sums[j], axis=0, keepdims=True)
        short_ref[i, SHORT : SHORT + 1] = jnp.sum(gain, axis=0, keepdims=True)
    wide[...] = lax.dot_general(left[...], right[...], (((1,), (1,)), ((), ())), preferred_element_type=F32)
    for g in range(per):
        gram = wide[g * LTAPS : (g + 1) * LTAPS]
        long_ref[g : g + 1] = sum_by_lag(gram)


def backward(mixed_own, mixed_rest, feats, filt, x, later, short_taps, skip, table, chunk, chunks):
    blocks, _, rows, cols = x.shape
    cols //= chunks
    tokens = blocks * rows
    tiles = cols // LANES
    first = chunk * tiles
    tab_rows = table.shape[0] * LANES // skip.shape[1]
    per = tab_rows // LTAPS
    tok = pl.BlockSpec((tokens, LANES), lambda c: (0, first + c))
    return pl.pallas_call(
        backward_kernel,
        grid=(tiles,),
        in_specs=[
            tok,
            tok,
            pl.BlockSpec((3, tokens, LANES), lambda c: (0, 0, c)),
            pl.BlockSpec((tokens, LANES), lambda c: (0, c)),
            pl.BlockSpec((blocks, 3, rows, LANES), lambda c: (0, 0, 0, first + c)),
            pl.BlockSpec((later.shape[0], LANES), lambda c: (0, first + c)),
            pl.BlockSpec((3, SHORT, LANES), lambda c: (0, 0, first + c)),
            pl.BlockSpec((1, LANES), lambda c: (0, first + c)),
            pl.BlockSpec((tab_rows, 2 * LTAPS), lambda c: (first + c, 0)),
        ],
        out_specs=[
            pl.BlockSpec((blocks, 3, rows, LANES), lambda c: (0, 0, 0, c)),
            pl.BlockSpec((3, SHORT + 1, LANES), lambda c: (0, 0, c)),
            pl.BlockSpec((per, LTAPS), lambda c: (c, 0)),
        ],
        out_shape=[
            jax.ShapeDtypeStruct((blocks, 3, rows, cols), BF16),
            jax.ShapeDtypeStruct((3, SHORT + 1, cols), F32),
            jax.ShapeDtypeStruct((tiles * per, LTAPS), F32),
        ],
        scratch_shapes=[
            pltpu.VMEM((tokens + 2 * LTAPS, LANES), BF16),
            pltpu.VMEM((3, tokens + PAD, LANES), F32),
            pltpu.VMEM((tab_rows, 2 * LTAPS), F32),
            pltpu.VMEM((tab_rows, tokens), BF16),
            pltpu.VMEM((2 * LTAPS, tokens), BF16),
        ],
        compiler_params=params(48),
        cost_estimate=cost(8 * LTAPS * tokens * tab_rows, 36 * tokens * cols),
        name="backward",
    )(mixed_own, mixed_rest, feats, filt, x, later, short_taps, skip, table)


def pack_kernel(*refs):
    out_ref = refs[-1]
    for i, ref in enumerate(refs[:3]):
        out_ref[0, i] = ref[...]


def pack(arrays, seq):
    rows, width = arrays[0].shape
    cols = width // seq
    return pl.pallas_call(
        pack_kernel,
        grid=(seq,),
        in_specs=[pl.BlockSpec((rows, cols), lambda s: (0, s))] * 3,
        out_specs=pl.BlockSpec((1, 3, rows, cols), lambda s: (s, 0, 0, 0)),
        out_shape=jax.ShapeDtypeStruct((seq, 3, rows, cols), BF16),
        compiler_params=params(32),
        name="pack",
    )(*arrays)


def unpack_kernel(*refs):
    parts, outs = refs[:-3], refs[-3:]
    cols = parts[0].shape[3]
    for n, part in enumerate(parts):
        for i, out in enumerate(outs):
            out[:, n * cols : (n + 1) * cols] = part[0, i]


def unpack(parts):
    seq, _, rows, cols = parts[0].shape
    wide = cols * len(parts)
    shape = jax.ShapeDtypeStruct((rows, seq * wide), BF16)
    return pl.pallas_call(
        unpack_kernel,
        grid=(seq,),
        in_specs=[pl.BlockSpec((1, 3, rows, cols), lambda s: (s, 0, 0, 0))] * len(parts),
        out_specs=[pl.BlockSpec((rows, wide), lambda s: (0, s))] * 3,
        out_shape=[shape] * 3,
        compiler_params=params(32),
        name="unpack",
    )(*parts)


def along(block, axis, distance):
    size = lax.axis_size(axis)
    return lax.ppermute(block, axis, [(i, i + distance) for i in range(size) if 0 <= i + distance < size])


def around(block, axis, distance):
    size = lax.axis_size(axis)
    return lax.ppermute(block, axis, [(i, (i + distance) % size) for i in range(size)])


def across(block, axis, bit):
    return lax.ppermute(block, axis, [(i, i ^ bit) for i in range(lax.axis_size(axis))])


def bits_of(axis):
    size = lax.axis_size(axis)
    return [1 << n for n in range(size.bit_length() - 1)]


def sum_over(value, axes):
    for axis in axes:
        for bit in bits_of(axis):
            value = value + across(value, axis, bit)
    return value


def split_kernel(y_ref, *refs):
    count = (len(refs) - 1) // 2
    for n in range(count):
        refs[count + 1 + n][...] = refs[n][...]


def split_cotangent(cotangent, y, ys, col_part, after):
    rows, width = cotangent.shape

    def source(step):
        return pl.BlockSpec((rows, col_part), lambda z, y_ref: (0, z * ys + (y_ref[0] + step) % ys))

    return pl.pallas_call(
        split_kernel,
        grid_spec=pltpu.PrefetchScalarGridSpec(
            num_scalar_prefetch=1,
            grid=(Z,),
            in_specs=[source(step) for step in range(ys)] + [pl.BlockSpec(memory_space=pl.ANY)],
            out_specs=[pl.BlockSpec((rows, col_part), lambda z, _: (0, z))] * ys,
        ),
        out_shape=[jax.ShapeDtypeStruct((rows, width // ys), BF16)] * ys,
        compiler_params=params(32),
        name="split",
    )(y.reshape(1), *([cotangent] * ys), after)


def join_kernel(axis, count, *refs):
    out = refs[-1]
    for n in range(count):
        size = refs[n].shape[axis]
        here = slice(n * size, (n + 1) * size)
        if axis == 0:
            out[here] = refs[n][...]
        else:
            out[:, here] = refs[n][...]


def join(parts, axis, after=()):
    shape = list(parts[0].shape)
    tile = shape[-1] // Z
    block = pl.BlockSpec((*shape[:-1], tile), lambda i: (0, 0, 0, i))
    shape[axis] *= len(parts)
    return pl.pallas_call(
        functools.partial(join_kernel, axis, len(parts)),
        grid=(Z,),
        in_specs=[block] * len(parts) + [pl.BlockSpec(memory_space=pl.ANY)] * len(after),
        out_specs=pl.BlockSpec((*shape[:-1], tile), lambda i: (0, 0, 0, i)),
        out_shape=jax.ShapeDtypeStruct(tuple(shape), BF16),
        compiler_params=params(32),
        name="join",
    )(*parts, *after)


def gather_cotangent(cotangent, col_part, after_first, after):
    ys, y = lax.axis_size("y"), lax.axis_index("y")
    held = split_cotangent(cotangent, y, ys, col_part, after_first)
    held = [around(part, "y", step) if step else part for step, part in enumerate(held)]
    held = join([part[None, None] for part in held], 0, after)
    bits = bits_of("seq")
    for bit in reversed(bits[1:]):
        held = join([held, across(held, "seq", bit)], 1)
    return held, across(held, "seq", bits[0])


def mixed_grad_kernel(place_ref, a_ref, b_ref, w_ref, _, out_ref, found):
    _, count, rows, _ = a_ref.shape
    tokens = count * rows
    pieces = jnp.concatenate([ref[...].reshape(tokens, -1) for ref in (a_ref, b_ref)], axis=0)
    found[...] = contract(pieces, w_ref[...], 1)
    for block in range(2 * count):
        there = pl.multiple_of(place_ref[block] * rows, rows)
        out_ref[block * rows : (block + 1) * rows] = found[pl.ds(there, rows)].astype(out_ref.dtype)


def mixed_grad(cots, weights, place, step, dtype, after):
    _, count, rows, width = cots[0].shape
    tokens = 2 * count * rows
    cols = weights.shape[0]
    tile = min(cols, 2 * LANES)
    piece = pl.BlockSpec((1, count, rows, width), lambda i, _: (step, 0, 0, 0))
    return pl.pallas_call(
        mixed_grad_kernel,
        grid_spec=pltpu.PrefetchScalarGridSpec(
            num_scalar_prefetch=1,
            grid=(cols // tile,),
            in_specs=[
                piece,
                piece,
                pl.BlockSpec((tile, width), lambda i, _: (i, 0)),
                pl.BlockSpec(memory_space=pl.ANY),
            ],
            out_specs=pl.BlockSpec((tokens, tile), lambda i, _: (0, i)),
            scratch_shapes=[pltpu.VMEM((tokens, tile), F32)],
        ),
        out_shape=jax.ShapeDtypeStruct((tokens, cols), dtype),
        compiler_params=params(56),
        cost_estimate=cost(2 * tokens * width * cols, 2 * (tokens + cols) * width),
        name="mixed_grad",
    )(place, *cots, weights, after)


def weight_grad_kernel(scale, chunks, a_ref, b_ref, *refs):
    mixed, out = refs[:-2], refs[-1]
    steps, count, rows, tile = a_ref.shape
    tokens = count * rows
    part = mixed[0].shape[0]
    for h in range(chunks):
        total = None
        for step in range(steps):
            for n, ref in enumerate((a_ref, b_ref)):
                left = mixed[step * chunks + h][:, n * tokens : (n + 1) * tokens]
                term = jnp.dot(left, ref[step].reshape(tokens, tile), preferred_element_type=F32)
                total = term if total is None else total + term
        out[h * part : (h + 1) * part] = (total * scale).astype(BF16)


def weight_grad(cots, mixed, chunks, scale, after):
    steps, count, rows, width = cots[0].shape
    part, tokens = mixed[0].shape
    tile = width // Z
    piece = pl.BlockSpec((steps, count, rows, tile), lambda i: (0, 0, 0, i))
    return pl.pallas_call(
        functools.partial(weight_grad_kernel, scale, chunks),
        grid=(Z,),
        in_specs=[piece, piece] + [pl.BlockSpec((part, tokens), lambda i: (0, 0))] * len(mixed)
        + [pl.BlockSpec(memory_space=pl.ANY)],
        out_specs=pl.BlockSpec((part * chunks, tile), lambda i: (0, i)),
        out_shape=jax.ShapeDtypeStruct((part * chunks, width), BF16),
        compiler_params=params(48),
        cost_estimate=cost(
            2 * part * chunks * steps * tokens * width, 2 * (steps * tokens + part * chunks) * width
        ),
        name="weight_grad",
    )(*cots, *mixed, after)


def tail_kernel(x_ref, before_ref, out_ref):
    rows = x_ref.shape[2]
    out_ref[0:PAD] = x_ref[0, 0, rows - PAD :]
    for i in (1, 2):
        begin = PAD + (i - 1) * (PAD + rows)
        out_ref[begin : begin + PAD] = before_ref[0, i, rows - PAD :]
        out_ref[begin + PAD : begin + PAD + rows] = x_ref[0, i]


def tail_of(x):
    seq, _, rows, cols = x.shape

    def block(s):
        return pl.BlockSpec((1, 3, rows, cols), lambda i: (s, 0, 0, 0))

    out_rows = PAD + 2 * (PAD + rows)
    return pl.pallas_call(
        tail_kernel,
        grid=(1,),
        in_specs=[block(seq - 1), block(seq - 2)],
        out_specs=pl.BlockSpec((out_rows, cols), lambda i: (0, 0)),
        out_shape=jax.ShapeDtypeStruct((out_rows, cols), BF16),
        compiler_params=params(32),
        name="tail",
    )(x, x)


def head_kernel(mo_ref, mr_ref, *refs):
    out_ref = refs[-1]
    chunks = len(refs) // 2
    edge = LTAPS + PAD
    part = out_ref.shape[1] // chunks
    for h in range(chunks):
        own = slice(h * part, (h + 1) * part)
        f_ref, filt_ref = refs[2 * h : 2 * h + 2]
        mixed = mo_ref[:, own] + mr_ref[:, own].astype(F32)
        out_ref[0:edge, own] = (mixed * f_ref[0]).astype(BF16)
        out_ref[edge : edge + PAD, own] = f_ref[1, 0:PAD].astype(BF16)
        out_ref[edge + PAD : edge + 2 * PAD, own] = f_ref[2, 0:PAD].astype(BF16)
        out_ref[edge + 2 * PAD :, own] = (mixed[0:PAD] * filt_ref[0:PAD]).astype(BF16)


def head_of(mixed_own, mixed_rest, mixers):
    edge, cols = LTAPS + PAD, mixed_own.shape[1]
    part = cols // len(mixers)
    whole = pl.BlockSpec((edge, cols), lambda i: (0, 0))
    feat_specs = [
        pl.BlockSpec((3, edge, part), lambda i: (0, 0, 0)),
        pl.BlockSpec((edge, part), lambda i: (0, 0)),
    ]
    return pl.pallas_call(
        head_kernel,
        grid=(1,),
        in_specs=[whole, whole] + feat_specs * len(mixers),
        out_specs=pl.BlockSpec((edge + 3 * PAD, cols), lambda i: (0, 0)),
        out_shape=jax.ShapeDtypeStruct((edge + 3 * PAD, cols), BF16),
        compiler_params=params(32),
        name="head",
    )(mixed_own, mixed_rest, *[array for mixer in mixers for array in mixer[1:]])


def contract(a, b, dim):
    return lax.dot_general(a, b, (((dim,), (dim,)), ((), ())), preferred_element_type=F32)


def places(seq):
    bits = bits_of("seq")
    source = lax.iota(jnp.int32, seq) ^ lax.axis_index("seq")
    return sum(((source >> n) & 1) << (len(bits) - 1 - n) for n in range(len(bits)))


def body(queries, keys, values, cotangent, out_weight, short_taps, long_taps, skip_gain):
    rows, width = queries.shape
    col_part = out_weight.shape[1]
    seq, ys = lax.axis_size("seq"), lax.axis_size("y")
    cols = width // seq
    chunks = 2 if cols % (2 * LANES) == 0 else 1
    groups = long_taps.shape[1]
    fsdp = ("z", "y")
    grad_scale = float(rows * seq * ys * Z) ** (-0.5)

    weights = lax.all_gather(out_weight, "z", axis=1, tiled=True)
    fwd_table, bwd_table = make_tables(long_taps)
    skip = skip_gain.reshape(1, cols)
    place = places(seq)
    by_owner = pack((queries, keys, values), seq)
    x = lax.all_to_all(by_owner, "seq", split_axis=0, concat_axis=0, tiled=True)
    halo = along(tail_of(x), fsdp, 1)
    cots = gather_cotangent(cotangent, col_part, by_owner, [halo])
    mixers = [forward(x, halo, short_taps, skip, fwd_table, place, h, chunks) for h in range(chunks)]

    parts = []
    for step in range(1, ys):
        parts.append(mixed_grad(cots, weights, place, step, BF16, parts[-1] if parts else place))
    rest = [around(parts[step - 1], "y", -step) for step in range(1, ys)]
    mixed_rest = rest[0] if len(rest) == 1 else sum(piece.astype(F32) for piece in rest)

    mixed_all = [
        around(mixers[h][0], "y", step) if step else mixers[h][0] for step in range(ys) for h in range(chunks)
    ]
    weight_sum = weight_grad(cots, mixed_all, chunks, grad_scale, parts[-1])
    weight_part = lax.psum_scatter(weight_sum, "z", scatter_dimension=1, tiled=True)

    mixed_own = mixed_grad(cots, weights, place, 0, F32, weight_sum)
    later = along(head_of(mixed_own, mixed_rest, mixers), fsdp, -1)
    grads, short_parts, long_parts = [], [], []
    for h in range(chunks):
        _, feats, filt = mixers[h]
        grad, short_part, long_part = backward(
            mixed_own, mixed_rest, feats, filt, x, later, short_taps, skip, bwd_table, h, chunks
        )
        grads.append(lax.all_to_all(grad, "seq", split_axis=0, concat_axis=0, tiled=True))
        short_parts.append(short_part)
        long_parts.append(long_part)

    query_grad, key_grad, value_grad = unpack(grads)
    packed = jnp.concatenate(
        [
            jnp.concatenate(short_parts, axis=2).reshape(3 * (SHORT + 1), cols),
            jnp.concatenate(long_parts, axis=0).reshape(-1, cols),
        ],
        axis=0,
    )
    packed = sum_over(packed, ("y", "z")) * grad_scale
    short_sum = packed[: 3 * (SHORT + 1)].reshape(3, SHORT + 1, cols)
    long_sum = packed[3 * (SHORT + 1) :].reshape(groups, LTAPS).T
    return (
        query_grad,
        key_grad,
        value_grad,
        weight_part.astype(F32),
        short_sum[:, :SHORT],
        long_sum,
        short_sum[0, SHORT],
    )


def solution(mesh):
    fsdp, seq = mesh.shape["fsdp"], mesh.shape["seq"]
    split = Mesh(mesh.devices.reshape(Z, fsdp // Z, seq), ("z", "y", "seq"))
    tokens = P(("z", "y", "seq"), None)
    specs = (P("seq", ("z", "y")), P(None, None, "seq"), P(None, "seq"), P("seq"))
    return jax.shard_map(
        body,
        mesh=split,
        in_specs=(tokens,) * 4 + specs,
        out_specs=(tokens,) * 3 + specs,
        check_vma=False,
    )
```

profile of v0, /device:TPU:0, one launch (start us, length us, event | category | flops | bytes accessed | tf_op | source)
XLA Modules:
  0.0 314.0 jit_solution(9146406665153325786)
XLA Ops:
  12.2 40.9 %all_to_all.15.x_ref.before_ref = bf16[4,3,128,1024]{3,2,1,0:T(8,128)(2,1)S(1)} all-to-all(bf16[4,3,128,1024]{3,2,1,0:T(8,128)(2,1)S(1)} %pack.1.refs_2_), channel_id=1, replica_groups=mesh['z'=4,'y'=2,'seq'=4] {'seq'}, dimensions={0} | all-to-all | bytes 6291456 | tf_op jit(solution)/shard_map/all_to_all | solution.py:570
  56.4 4.2 %collective-permute-start.1 = (bf16[304,1024]{1,0:T(8,128)(2,1)S(1)}, bf16[304,1024]{1,0:T(8,128)(2,1)}, u32[]{:S(2)}, u32[]{:S(2)}) collective-permute-start(bf16[304,1024]{1,0:T(8,128)(2,1)S(1)} %tail.1), channel_id=1, source_target_pairs={{0,4},{4,8},{8,12},{12,16},{16,20},{20,24},{24,28},{1,5},{5,9},{9,... | collective-permute-start | bytes 1867784 | tf_op jit(solution)/shard_map/ppermute | solution.py:324
  60.6 1.9 copy-done.3
  65.0 19.3 %collective-permute-done = bf16[128,2048]{1,0:T(8,128)(2,1)S(1)} collective-permute-done((bf16[128,2048]{1,0:T(8,128)(2,1)S(1)}, bf16[128,2048]{1,0:T(8,128)(2,1)S(1)}, u32[]{:S(2)}, u32[]{:S(2)}) %collective-permute-start) | collective-permute-done | bytes 524320 | tf_op jit(solution)/shard_map/ppermute | solution.py:329
  85.3 23.5 %collective-permute-done.2.refs_1_ = bf16[2,1,128,2048]{3,2,1,0:T(8,128)(2,1)S(1)} collective-permute-done((bf16[2,1,128,2048]{3,2,1,0:T(8,128)(2,1)S(1)}, bf16[2,1,128,2048]{3,2,1,0:T(8,128)(2,1)S(1)}, u32[]{:S(2)}, u32[]{:S(2)}) %collective-permute-start.2) | collective-permute-done | bytes 1048608 | tf_op jit(solution)/shard_map/ppermute | solution.py:333
  109.6 2.8 tables.1
  112.4 2.0 copy-done.6
  114.4 2.1 copy-done.7
  116.5 6.6 %forward.2 = (bf16[512,512]{1,0:T(8,128)(2,1)S(1)}, f32[3,512,512]{2,1,0:T(8,128)S(1)}, f32[512,512]{1,0:T(8,128)S(1)}) custom-call(s32[4]{0:T(128)S(1)} %shift-left_add_fusion.place_ref._, bf16[4,3,128,1024]{3,2,1,0:T(8,128)(2,1)} %copy-done, bf16[304,1024]{1,0:T(8,128)(2,1)} %collective-permute-done.1.refs_2_.h_ref, f32[3,7,1024]{2,1,0:T(8,128)S(1)} %copy-done.23, ...), custom_call_target="tpu_custom_call" | custom-call | flops 268435456 | bytes 6291456 | tf_op jit(solution)/shard_map/forward/pallas_call | solution.py:117
  125.7 4.3 %collective-permute-start.4 = (bf16[512,512]{1,0:T(8,128)(2,1)S(1)}, bf16[512,512]{1,0:T(8,128)(2,1)S(1)}, u32[]{:S(2)}, u32[]{:S(2)}) collective-permute-start(bf16[512,512]{1,0:T(8,128)(2,1)S(1)} %get-tuple-element.29.refs_0_), channel_id=1, source_target_pairs={{0,4},{4,0},{1,5},{5,1},{2,6},{6,2},{3,7},{7,3},{8,12},{12,8},{9,1... | collective-permute-start | bytes 1572872 | tf_op jit(solution)/shard_map/ppermute | solution.py:329
  130.0 7.1 %forward.3 = (bf16[512,512]{1,0:T(8,128)(2,1)}, f32[3,512,512]{2,1,0:T(8,128)S(1)}, f32[512,512]{1,0:T(8,128)S(1)}) custom-call(s32[4]{0:T(128)S(1)} %shift-left_add_fusion.place_ref._, bf16[4,3,128,1024]{3,2,1,0:T(8,128)(2,1)} %copy-done, bf16[304,1024]{1,0:T(8,128)(2,1)} %collective-permute-done.1.refs_2_.h_ref, f32[3,7,1024]{2,1,0:T(8,128)S(1)} %copy-done.23, ...), custom_call_target="tpu_custom_call" | custom-call | flops 268435456 | bytes 6291456 | tf_op jit(solution)/shard_map/forward/pallas_call | solution.py:117
  137.1 1.7 copy-done.8
  139.8 7.0 %mixed_grad.2.refs_4_ = bf16[512,1024]{1,0:T(8,128)(2,1)} custom-call(s32[4]{0:T(128)} %copy-done.29, bf16[2,2,128,2048]{3,2,1,0:T(8,128)(2,1)} %copy-done.4, bf16[2,2,128,2048]{3,2,1,0:T(8,128)(2,1)} %collective-permute-done.3.b_ref, bf16[1024,2048]{1,0:T(8,128)(2,1)} %all-gather.2.cloned.1.call-done.w_ref, s32[4]{0:T(128)} %copy-done.29), custom_call_target="tpu_custom_call" | custom-call | flops 2147483648 | bytes 6291456 | tf_op jit(solution)/shard_map/mixed_grad/pallas_call | solution.py:428
  146.8 7.3 %collective-permute-done.5.refs_3_ = bf16[512,512]{1,0:T(8,128)(2,1)} collective-permute-done((bf16[512,512]{1,0:T(8,128)(2,1)}, bf16[512,512]{1,0:T(8,128)(2,1)}, u32[]{:S(2)}, u32[]{:S(2)}) %collective-permute-start.5) | collective-permute-done | bytes 524320 | tf_op jit(solution)/shard_map/ppermute | solution.py:329
  156.9 7.7 %weight_grad.1._ = bf16[1024,2048]{1,0:T(8,128)(2,1)} custom-call(bf16[2,2,128,2048]{3,2,1,0:T(8,128)(2,1)S(1)} %copy-done.5, bf16[2,2,128,2048]{3,2,1,0:T(8,128)(2,1)} %collective-permute-done.3.b_ref, bf16[512,512]{1,0:T(8,128)(2,1)S(1)} %get-tuple-element.29.refs_0_, bf16[512,512]{1,0:T(8,128)(2,1)} %get-tuple-element.30.refs_1_, ...), custom_call_target="tpu_custom_call" | custom-call | flops 4294967296 | bytes 8388608 | tf_op jit(solution)/shard_map/weight_grad/pallas_call | solution.py:469
  164.7 1.7 collective-permute-start.6
  166.3 7.4 %mixed_grad.3.mo_ref = f32[512,1024]{1,0:T(8,128)} custom-call(s32[4]{0:T(128)} %copy-done.29, bf16[2,2,128,2048]{3,2,1,0:T(8,128)(2,1)} %copy-done.4, bf16[2,2,128,2048]{3,2,1,0:T(8,128)(2,1)} %collective-permute-done.3.b_ref, bf16[1024,2048]{1,0:T(8,128)(2,1)} %all-gather.2.cloned.1.call-done.w_ref, bf16[1024,2048]{1,0:T(8,128)(2,1)} %weight_grad.1._), custom_call_target="tpu_custom_call" | custom-call | flops 2147483648 | bytes 6291456 | tf_op jit(solution)/shard_map/mixed_grad/pallas_call | solution.py:428
  173.7 15.8 %collective-permute-done.6.mr_ref = bf16[512,1024]{1,0:T(8,128)(2,1)S(1)} collective-permute-done((bf16[512,1024]{1,0:T(8,128)(2,1)}, bf16[512,1024]{1,0:T(8,128)(2,1)S(1)}, u32[]{:S(2)}, u32[]{:S(2)}) %collective-permute-start.6) | collective-permute-done | bytes 1048608 | tf_op jit(solution)/shard_map/ppermute | solution.py:329
  189.6 2.0 copy-done.1
  195.5 10.5 %collective-permute-done.7.n_ref = bf16[192,1024]{1,0:T(8,128)(2,1)S(1)} collective-permute-done((bf16[192,1024]{1,0:T(8,128)(2,1)S(1)}, bf16[192,1024]{1,0:T(8,128)(2,1)S(1)}, u32[]{:S(2)}, u32[]{:S(2)}) %collective-permute-start.7) | collective-permute-done | bytes 393248 | tf_op jit(solution)/shard_map/ppermute | solution.py:324
  206.0 9.9 %backward.2 = (bf16[4,3,128,512]{3,2,1,0:T(8,128)(2,1)S(1)}, f32[3,8,512]{2,1,0:T(8,128)S(1)}, f32[32,128]{1,0:T(8,128)S(1)}) custom-call(f32[512,1024]{1,0:T(8,128)} %mixed_grad.3.mo_ref, bf16[512,1024]{1,0:T(8,128)(2,1)S(1)} %collective-permute-done.6.mr_ref, f32[3,512,512]{2,1,0:T(8,128)} %copy-done.10, f32[512,512]{1,0:T(8,128)S(1)} %copy-done.19, ...), custom_call_target="tpu_custom_call" | custom-call | flops 536870912 | bytes 9437184 | tf_op jit(solution)/shard_map/backward/pallas_call | solution.py:242
  217.1 3.7 %all-to-all-start.1 = ((bf16[4,3,128,512]{3,2,1,0:T(8,128)(2,1)}), bf16[4,3,128,512]{3,2,1,0:T(8,128)(2,1)S(1)}, u32[]{:S(2)}, u32[]{:S(2)}) async-start(bf16[4,3,128,512]{3,2,1,0:T(8,128)(2,1)} %copy-done.22), calls=%async_computation.1 | async-start | bytes 3145728 | tf_op jit(solution)/shard_map/all_to_all | solution.py:595
  222.1 9.9 %backward.3 = (bf16[4,3,128,512]{3,2,1,0:T(8,128)(2,1)S(1)}, f32[3,8,512]{2,1,0:T(8,128)S(1)}, f32[32,128]{1,0:T(8,128)S(1)}) custom-call(f32[512,1024]{1,0:T(8,128)} %mixed_grad.3.mo_ref, bf16[512,1024]{1,0:T(8,128)(2,1)S(1)} %copy-done.13, f32[3,512,512]{2,1,0:T(8,128)} %copy-done.8, f32[512,512]{1,0:T(8,128)S(1)} %copy-done.16, ...), custom_call_target="tpu_custom_call" | custom-call | flops 536870912 | bytes 9437184 | tf_op jit(solution)/shard_map/backward/pallas_call | solution.py:242
  233.1 7.7 %all-to-all-done.1.refs_0_ = bf16[4,3,128,512]{3,2,1,0:T(8,128)(2,1)S(1)} async-done(((bf16[4,3,128,512]{3,2,1,0:T(8,128)(2,1)}), bf16[4,3,128,512]{3,2,1,0:T(8,128)(2,1)S(1)}, u32[]{:S(2)}, u32[]{:S(2)}) %all-to-all-start.1) | async-done | bytes 1572896 | tf_op jit(solution)/shard_map/all_to_all | solution.py:595
  240.8 4.4 %all-to-all-start.2 = ((bf16[4,3,128,512]{3,2,1,0:T(8,128)(2,1)}), bf16[4,3,128,512]{3,2,1,0:T(8,128)(2,1)}, u32[]{:S(2)}, u32[]{:S(2)}) async-start(bf16[4,3,128,512]{3,2,1,0:T(8,128)(2,1)} %copy-done.21), calls=%async_computation.2 | async-start | bytes 3145728 | tf_op jit(solution)/shard_map/all_to_all | solution.py:595
  245.2 30.7 %collective-permute-start.8 = (f32[32,1024]{1,0:T(8,128)S(1)}, f32[32,1024]{1,0:T(8,128)S(1)}, u32[]{:S(2)}, u32[]{:S(2)}) collective-permute-start(f32[32,1024]{1,0:T(8,128)S(1)} %pad_maximum_fusion), channel_id=1, source_target_pairs={{0,4},{4,0},{1,5},{5,1},{2,6},{6,2},{3,7},{7,3},{8,12},{12,8},{9,1... | collective-permute-start | bytes 393224 | tf_op jit(solution)/shard_map/ppermute | solution.py:333
  275.9 4.1 %collective-permute-done.8 = f32[32,1024]{1,0:T(8,128)S(1)} collective-permute-done((f32[32,1024]{1,0:T(8,128)S(1)}, f32[32,1024]{1,0:T(8,128)S(1)}, u32[]{:S(2)}, u32[]{:S(2)}) %collective-permute-start.8) | collective-permute-done | bytes 131104 | tf_op jit(solution)/shard_map/ppermute | solution.py:333
  280.0 6.9 %collective-permute-start.9 = (f32[32,1024]{1,0:T(8,128)S(1)}, f32[32,1024]{1,0:T(8,128)S(1)}, u32[]{:S(2)}, u32[]{:S(2)}) collective-permute-start(f32[32,1024]{1,0:T(8,128)S(1)} %fusion), channel_id=1, source_target_pairs={{0,8},{8,0},{16,24},{24,16},{1,9},{9,1},{17,25},{25,17},{2,10},{10... | collective-permute-start | bytes 393224 | tf_op jit(solution)/shard_map/ppermute | solution.py:333
  286.9 3.6 %collective-permute-done.9 = f32[32,1024]{1,0:T(8,128)S(1)} collective-permute-done((f32[32,1024]{1,0:T(8,128)S(1)}, f32[32,1024]{1,0:T(8,128)S(1)}, u32[]{:S(2)}, u32[]{:S(2)}) %collective-permute-start.9) | collective-permute-done | bytes 131104 | tf_op jit(solution)/shard_map/ppermute | solution.py:333
  291.1 8.1 %collective-permute-done.10 = f32[32,1024]{1,0:T(8,128)S(1)} collective-permute-done((f32[32,1024]{1,0:T(8,128)S(1)}, f32[32,1024]{1,0:T(8,128)S(1)}, u32[]{:S(2)}, u32[]{:S(2)}) %collective-permute-start.10) | collective-permute-done | bytes 131104 | tf_op jit(solution)/shard_map/ppermute | solution.py:333
  300.5 3.9 %unpack.1 = (bf16[128,4096]{1,0:T(8,128)(2,1)}, bf16[128,4096]{1,0:T(8,128)(2,1)}, bf16[128,4096]{1,0:T(8,128)(2,1)}) custom-call(bf16[4,3,128,512]{3,2,1,0:T(8,128)(2,1)S(1)} %all-to-all-done.1.refs_0_, bf16[4,3,128,512]{3,2,1,0:T(8,128)(2,1)} %all-to-all-done.2.refs_1_), custom_call_target="tpu_custom_call" | custom-call | tf_op jit(solution)/shard_map/unpack/pallas_call | solution.py:311
  304.3 2.8 convert_element_type.7
  (96 shorter events, 28.2 us)
Async XLA Ops:
  7.2 132.6 %all-gather.2.cloned.1.call-start = ((), (), s32[]{:S(2)}) async-start(), calls=%async_computation.4 | async-start | bytes 5242880 | tf_op jit(solution)/shard_map/all_gather | solution.py:565
  7.9 296.4 %reduce-scatter.2.cloned.1.call-start = ((), (), s32[]{:S(2)}) async-start(), calls=%async_computation.5 | async-start | bytes 5242880 | tf_op jit(solution)/shard_map/reduce_scatter | solution.py:585
  56.4 28.0 %collective-permute-start.1 = (bf16[304,1024]{1,0:T(8,128)(2,1)S(1)}, bf16[304,1024]{1,0:T(8,128)(2,1)}, u32[]{:S(2)}, u32[]{:S(2)}) collective-permute-start(bf16[304,1024]{1,0:T(8,128)(2,1)S(1)} %tail.1), channel_id=1, source_target_pairs={{0,4},{4,8},{8,12},{12,16},{16,20},{20,24},{24,28},{1,5},{5,9},{9,... | collective-permute-start | bytes 1867784 | tf_op jit(solution)/shard_map/ppermute | solution.py:324
  60.6 1.9 copy-start.3
  64.2 20.1 %collective-permute-start = (bf16[128,2048]{1,0:T(8,128)(2,1)S(1)}, bf16[128,2048]{1,0:T(8,128)(2,1)S(1)}, u32[]{:S(2)}, u32[]{:S(2)}) collective-permute-start(bf16[128,2048]{1,0:T(8,128)(2,1)S(1)} %get-tuple-element.27), channel_id=1, source_target_pairs={{0,4},{4,0},{1,5},{5,1},{2,6},{6,2},{3,7},{7,3},{8,12},{12,8},{9,1... | collective-permute-start | bytes 1572872 | tf_op jit(solution)/shard_map/ppermute | solution.py:329
  84.3 25.1 %copy-start.30 = (f32[128,64]{0,1:T(8,128)S(1)}, f32[128,64]{0,1:T(8,128)}, u32[]{:S(2)}) copy-start(f32[128,64]{0,1:T(8,128)} %param.14) | copy-start | bytes 98308
  84.4 32.1 %copy-start.23 = (f32[3,7,1024]{2,1,0:T(8,128)S(1)}, f32[3,7,1024]{2,1,0:T(8,128)}, u32[]{:S(2)}) copy-start(f32[3,7,1024]{2,1,0:T(8,128)} %taps_ref.7) | copy-start | bytes 258052
  84.4 32.1 %copy-start.28 = (f32[1024]{0:T(1024)S(1)}, f32[1024]{0:T(1024)}, u32[]{:S(2)}) copy-start(f32[1024]{0:T(1024)} %param.15) | copy-start | bytes 12292
  84.7 24.1 %collective-permute-start.2 = (bf16[2,1,128,2048]{3,2,1,0:T(8,128)(2,1)S(1)}, bf16[2,1,128,2048]{3,2,1,0:T(8,128)(2,1)S(1)}, u32[]{:S(2)}, u32[]{:S(2)}) collective-permute-start(bf16[2,1,128,2048]{3,2,1,0:T(8,128)(2,1)S(1)} %join.2.refs_0_), channel_id=1, source_target_pairs={{0,2},{1,3},{2,0},{3,1},{4,6},{5,7},{6,4},{7,5},{8,10},{9,11},{10,... | collective-permute-start | bytes 3145736 | tf_op jit(solution)/shard_map/ppermute | solution.py:333
  109.3 30.4 %copy-start.4 = (bf16[2,2,128,2048]{3,2,1,0:T(8,128)(2,1)}, bf16[2,2,128,2048]{3,2,1,0:T(8,128)(2,1)S(1)}, u32[]{:S(2)}) copy-start(bf16[2,2,128,2048]{3,2,1,0:T(8,128)(2,1)S(1)} %join.3.a_ref) | copy-start | bytes 6291460
  109.3 30.4 %collective-permute-start.3 = (bf16[2,2,128,2048]{3,2,1,0:T(8,128)(2,1)S(1)}, bf16[2,2,128,2048]{3,2,1,0:T(8,128)(2,1)}, u32[]{:S(2)}, u32[]{:S(2)}) collective-permute-start(bf16[2,2,128,2048]{3,2,1,0:T(8,128)(2,1)S(1)} %join.3.a_ref), channel_id=1, source_target_pairs={{0,1},{1,0},{2,3},{3,2},{4,5},{5,4},{6,7},{7,6},{8,9},{9,8},{10,11... | collective-permute-start | bytes 6291464 | tf_op jit(solution)/shard_map/ppermute | solution.py:333
  112.4 2.0 copy-start.6
  114.4 2.1 copy-start.7
  116.5 13.6 %copy-start.29 = (s32[4]{0:T(128)}, s32[4]{0:T(128)S(1)}, u32[]{:S(2)}) copy-start(s32[4]{0:T(128)S(1)} %shift-left_add_fusion.place_ref._) | copy-start | bytes 52
  123.1 1.7 copy-start.10
  125.7 21.1 %collective-permute-start.4 = (bf16[512,512]{1,0:T(8,128)(2,1)S(1)}, bf16[512,512]{1,0:T(8,128)(2,1)S(1)}, u32[]{:S(2)}, u32[]{:S(2)}) collective-permute-start(bf16[512,512]{1,0:T(8,128)(2,1)S(1)} %get-tuple-element.29.refs_0_), channel_id=1, source_target_pairs={{0,4},{4,0},{1,5},{5,1},{2,6},{6,2},{3,7},{7,3},{8,12},{12,8},{9,1... | collective-permute-start | bytes 1572872 | tf_op jit(solution)/shard_map/ppermute | solution.py:329
  137.1 1.7 copy-start.8
  139.8 14.4 %collective-permute-start.5 = (bf16[512,512]{1,0:T(8,128)(2,1)}, bf16[512,512]{1,0:T(8,128)(2,1)}, u32[]{:S(2)}, u32[]{:S(2)}) collective-permute-start(bf16[512,512]{1,0:T(8,128)(2,1)} %get-tuple-element.30.refs_1_), channel_id=1, source_target_pairs={{0,4},{4,0},{1,5},{5,1},{2,6},{6,2},{3,7},{7,3},{8,12},{12,8},{9,1... | collective-permute-start | bytes 1572872 | tf_op jit(solution)/shard_map/ppermute | solution.py:329
  164.7 24.9 %copy-start.9 = (f32[3,512,512]{2,1,0:T(8,128)S(1)}, f32[3,512,512]{2,1,0:T(8,128)}, u32[]{:S(2)}) copy-start(f32[3,512,512]{2,1,0:T(8,128)} %copy-done.8) | copy-start | bytes 9437188
  164.7 24.9 %copy-start.11 = (f32[3,512,512]{2,1,0:T(8,128)S(1)}, f32[3,512,512]{2,1,0:T(8,128)}, u32[]{:S(2)}) copy-start(f32[3,512,512]{2,1,0:T(8,128)} %copy-done.10) | copy-start | bytes 9437188
  164.7 24.9 %collective-permute-start.6 = (bf16[512,1024]{1,0:T(8,128)(2,1)}, bf16[512,1024]{1,0:T(8,128)(2,1)S(1)}, u32[]{:S(2)}, u32[]{:S(2)}) collective-permute-start(bf16[512,1024]{1,0:T(8,128)(2,1)} %mixed_grad.2.refs_4_), channel_id=1, source_target_pairs={{0,4},{4,0},{1,5},{5,1},{2,6},{6,2},{3,7},{7,3},{8,12},{12,8},{9,1... | collective-permute-start | bytes 3145736 | tf_op jit(solution)/shard_map/ppermute | solution.py:329
  189.6 16.5 %copy-start.12 = (bf16[512,1024]{1,0:T(8,128)(2,1)}, bf16[512,1024]{1,0:T(8,128)(2,1)S(1)}, u32[]{:S(2)}) copy-start(bf16[512,1024]{1,0:T(8,128)(2,1)S(1)} %collective-permute-done.6.mr_ref) | copy-start | bytes 3145732
  189.6 2.0 copy-start.1
  194.0 12.0 %copy-start.19 = (f32[512,512]{1,0:T(8,128)S(1)}, f32[512,512]{1,0:T(8,128)}, u32[]{:S(2)}) copy-start(f32[512,512]{1,0:T(8,128)} %copy-done.17) | copy-start | bytes 3145732
  194.1 12.0 %collective-permute-start.7 = (bf16[192,1024]{1,0:T(8,128)(2,1)S(1)}, bf16[192,1024]{1,0:T(8,128)(2,1)S(1)}, u32[]{:S(2)}, u32[]{:S(2)}) collective-permute-start(bf16[192,1024]{1,0:T(8,128)(2,1)S(1)} %head.1), channel_id=1, source_target_pairs={{4,0},{8,4},{12,8},{16,12},{20,16},{24,20},{28,24},{5,1},{9,5},{13... | collective-permute-start | bytes 1179656 | tf_op jit(solution)/shard_map/ppermute | solution.py:324
  217.1 3.7 %copy-start.13 = (bf16[512,1024]{1,0:T(8,128)(2,1)S(1)}, bf16[512,1024]{1,0:T(8,128)(2,1)}, u32[]{:S(2)}) copy-start(bf16[512,1024]{1,0:T(8,128)(2,1)} %copy-done.12) | copy-start | bytes 3145732
  217.1 23.7 %all-to-all-start.1 = ((bf16[4,3,128,512]{3,2,1,0:T(8,128)(2,1)}), bf16[4,3,128,512]{3,2,1,0:T(8,128)(2,1)S(1)}, u32[]{:S(2)}, u32[]{:S(2)}) async-start(bf16[4,3,128,512]{3,2,1,0:T(8,128)(2,1)} %copy-done.22), calls=%async_computation.1 | async-start | bytes 3145728 | tf_op jit(solution)/shard_map/all_to_all | solution.py:595
  240.8 59.6 %all-to-all-start.2 = ((bf16[4,3,128,512]{3,2,1,0:T(8,128)(2,1)}), bf16[4,3,128,512]{3,2,1,0:T(8,128)(2,1)}, u32[]{:S(2)}, u32[]{:S(2)}) async-start(bf16[4,3,128,512]{3,2,1,0:T(8,128)(2,1)} %copy-done.21), calls=%async_computation.2 | async-start | bytes 3145728 | tf_op jit(solution)/shard_map/all_to_all | solution.py:595
  245.2 34.8 %collective-permute-start.8 = (f32[32,1024]{1,0:T(8,128)S(1)}, f32[32,1024]{1,0:T(8,128)S(1)}, u32[]{:S(2)}, u32[]{:S(2)}) collective-permute-start(f32[32,1024]{1,0:T(8,128)S(1)} %pad_maximum_fusion), channel_id=1, source_target_pairs={{0,4},{4,0},{1,5},{5,1},{2,6},{6,2},{3,7},{7,3},{8,12},{12,8},{9,1... | collective-permute-start | bytes 393224 | tf_op jit(solution)/shard_map/ppermute | solution.py:333
  280.0 10.5 %collective-permute-start.9 = (f32[32,1024]{1,0:T(8,128)S(1)}, f32[32,1024]{1,0:T(8,128)S(1)}, u32[]{:S(2)}, u32[]{:S(2)}) collective-permute-start(f32[32,1024]{1,0:T(8,128)S(1)} %fusion), channel_id=1, source_target_pairs={{0,8},{8,0},{16,24},{24,16},{1,9},{9,1},{17,25},{25,17},{2,10},{10... | collective-permute-start | bytes 393224 | tf_op jit(solution)/shard_map/ppermute | solution.py:333
  290.5 8.6 %collective-permute-start.10 = (f32[32,1024]{1,0:T(8,128)S(1)}, f32[32,1024]{1,0:T(8,128)S(1)}, u32[]{:S(2)}, u32[]{:S(2)}) collective-permute-start(f32[32,1024]{1,0:T(8,128)S(1)} %add.20), channel_id=1, source_target_pairs={{0,16},{8,24},{16,0},{24,8},{1,17},{9,25},{17,1},{25,9},{2,18},{10... | collective-permute-start | bytes 393224 | tf_op jit(solution)/shard_map/ppermute | solution.py:333
  299.8 7.4 %copy-start.31 = (f32[3,8,1024]{2,1,0:T(8,128)}, f32[3,8,1024]{2,1,0:T(8,128)S(1)}, u32[]{:S(2)}) copy-start(f32[3,8,1024]{2,1,0:T(8,128)S(1)} %slice_bitcast_fusion) | copy-start | bytes 294916
  (15 other events, 18.9 us)
Sparse Core Ops, SparseCore 0:
  9.6 83.4 all-gather.1
  164.8 100.3 reduce-scatter.1
where the time goes:
time: 315 us; the launch traced here: 314 us
  waiting for transfers between devices  101 us (32%)
  Pallas kernels  64 us (20%)
  starting transfers between devices  59.3 us (19%)
  blocking collectives  40.9 us (13%)
  local copies, waits for them, and re-layouts  31.6 us (10%)
  between operations  14.3 us (5%)
    ppermute x4, waiting for transfers between devices, around(): lax.ppermute(block, axis, [(i, (i + distance) % size) for i in range(size)])  42.5 us
    all_to_all x1, blocking collectives, body(): x = lax.all_to_all(by_owner, 'seq', split_axis=0, concat_axis=0, tiled=True)  40.9 us
    ppermute x5, waiting for transfers between devices, across(): lax.ppermute(block, axis, [(i, i ^ bit) for i in range(lax.axis_size(axis...  39.4 us
    ppermute x5, starting transfers between devices, across(): lax.ppermute(block, axis, [(i, i ^ bit) for i in range(lax.axis_size(axis...  38.7 us
    unnamed x64, local copies, waits for them, and re-layouts  30.2 us
    pallas_call x2, Pallas kernels, backward(): pl.pallas_call(backward_kernel, grid=(tiles,), in_specs=[tok, tok, pl.Blo...  19.7 us
    pallas_call x2, Pallas kernels, mixed_grad(): pl.pallas_call(mixed_grad_kernel, grid_spec=pltpu.PrefetchScalarGridSpec(...  14.4 us
    pallas_call x2, Pallas kernels, forward(): pl.pallas_call(forward_kernel, grid_spec=pltpu.PrefetchScalarGridSpec(num...  13.6 us
  transfers between devices with their start and end apart: 15, of which 9 were waited for; matrix products, arithmetic and copies ran while one was open for 0% of the time, Pallas kernels for 18%

commit v1 on v0

--- a/solution.py
+++ b/solution.py
@@ -17,12 +17,8 @@
 BF16 = jnp.bfloat16
 
 
-def params(mib):
-    return pltpu.CompilerParams(vmem_limit_bytes=mib * 2**20)
-
-
-def cost(flops, nbytes):
-    return pl.CostEstimate(flops=flops, bytes_accessed=nbytes, transcendentals=0)
+def params():
+    return pltpu.CompilerParams(vmem_limit_bytes=60 * 2**20)
 
 
 def tables_kernel(fwd_ref, bwd_ref, tf_ref, tb_ref):
@@ -48,7 +44,7 @@
         in_specs=[row_spec, row_spec],
         out_specs=[tab_spec, tab_spec],
         out_shape=[shape, shape],
-        compiler_params=params(32),
+        compiler_params=params(),
         name="tables",
     )(fwd, bwd)
 
@@ -143,8 +139,7 @@
             jax.ShapeDtypeStruct((3, tokens, cols), F32),
             jax.ShapeDtypeStruct((tokens, cols), F32),
         ],
-        compiler_params=params(48),
-        cost_estimate=cost(4 * LTAPS * tokens * tab_rows, 24 * tokens * cols),
+        compiler_params=params(),
         name="forward",
     )(place, x, halo, short_taps, skip, table)
 
@@ -270,8 +265,7 @@
             pltpu.VMEM((tab_rows, tokens), BF16),
             pltpu.VMEM((2 * LTAPS, tokens), BF16),
         ],
-        compiler_params=params(48),
-        cost_estimate=cost(8 * LTAPS * tokens * tab_rows, 36 * tokens * cols),
+        compiler_params=params(),
         name="backward",
     )(mixed_own, mixed_rest, feats, filt, x, later, short_taps, skip, table)
 
@@ -291,7 +285,7 @@
         in_specs=[pl.BlockSpec((rows, cols), lambda s: (0, s))] * 3,
         out_specs=pl.BlockSpec((1, 3, rows, cols), lambda s: (s, 0, 0, 0)),
         out_shape=jax.ShapeDtypeStruct((seq, 3, rows, cols), BF16),
-        compiler_params=params(32),
+        compiler_params=params(),
         name="pack",
     )(*arrays)
 
@@ -314,7 +308,7 @@
         in_specs=[pl.BlockSpec((1, 3, rows, cols), lambda s: (s, 0, 0, 0))] * len(parts),
         out_specs=[pl.BlockSpec((rows, wide), lambda s: (0, s))] * 3,
         out_shape=[shape] * 3,
-        compiler_params=params(32),
+        compiler_params=params(),
         name="unpack",
     )(*parts)
 
@@ -366,7 +360,7 @@
             out_specs=[pl.BlockSpec((rows, col_part), lambda z, _: (0, z))] * ys,
         ),
         out_shape=[jax.ShapeDtypeStruct((rows, width // ys), BF16)] * ys,
-        compiler_params=params(32),
+        compiler_params=params(),
         name="split",
     )(y.reshape(1), *([cotangent] * ys), after)
 
@@ -393,23 +387,26 @@
         in_specs=[block] * len(parts) + [pl.BlockSpec(memory_space=pl.ANY)] * len(after),
         out_specs=pl.BlockSpec((*shape[:-1], tile), lambda i: (0, 0, 0, i)),
         out_shape=jax.ShapeDtypeStruct(tuple(shape), BF16),
-        compiler_params=params(32),
+        compiler_params=params(),
         name="join",
     )(*parts, *after)
 
 
-def gather_cotangent(cotangent, col_part, after_first, after):
+def own_cotangent(cotangent, col_part, after):
     ys, y = lax.axis_size("y"), lax.axis_index("y")
-    held = split_cotangent(cotangent, y, ys, col_part, after_first)
+    held = split_cotangent(cotangent, y, ys, col_part, after)
     held = [around(part, "y", step) if step else part for step, part in enumerate(held)]
-    held = join([part[None, None] for part in held], 0, after)
+    return join([part[None, None] for part in held], 0)
+
+
+def gather_cotangent(held, after):
     bits = bits_of("seq")
     for bit in reversed(bits[1:]):
-        held = join([held, across(held, "seq", bit)], 1)
+        held = join([held, across(held, "seq", bit)], 1, after)
     return held, across(held, "seq", bits[0])
 
 
-def mixed_grad_kernel(place_ref, a_ref, b_ref, w_ref, _, out_ref, found):
+def mixed_grad_kernel(place_ref, a_ref, b_ref, w_ref, _, out_ref, head_ref, found):
     _, count, rows, _ = a_ref.shape
     tokens = count * rows
     pieces = jnp.concatenate([ref[...].reshape(tokens, -1) for ref in (a_ref, b_ref)], axis=0)
@@ -417,6 +414,7 @@
     for block in range(2 * count):
         there = pl.multiple_of(place_ref[block] * rows, rows)
         out_ref[block * rows : (block + 1) * rows] = found[pl.ds(there, rows)].astype(out_ref.dtype)
+    head_ref[...] = out_ref[0 : LTAPS + PAD]
 
 
 def mixed_grad(cots, weights, place, step, dtype, after):
@@ -436,12 +434,17 @@
                 pl.BlockSpec((tile, width), lambda i, _: (i, 0)),
                 pl.BlockSpec(memory_space=pl.ANY),
             ],
-            out_specs=pl.BlockSpec((tokens, tile), lambda i, _: (0, i)),
+            out_specs=[
+                pl.BlockSpec((tokens, tile), lambda i, _: (0, i)),
+                pl.BlockSpec((LTAPS + PAD, tile), lambda i, _: (0, i)),
+            ],
             scratch_shapes=[pltpu.VMEM((tokens, tile), F32)],
         ),
-        out_shape=jax.ShapeDtypeStruct((tokens, cols), dtype),
-        compiler_params=params(56),
-        cost_estimate=cost(2 * tokens * width * cols, 2 * (tokens + cols) * width),
+        out_shape=[
+            jax.ShapeDtypeStruct((tokens, cols), dtype),
+            jax.ShapeDtypeStruct((LTAPS + PAD, cols), dtype),
+        ],
+        compiler_params=params(),
         name="mixed_grad",
     )(place, *cots, weights, after)
 
@@ -473,15 +476,13 @@
         + [pl.BlockSpec(memory_space=pl.ANY)],
         out_specs=pl.BlockSpec((part * chunks, tile), lambda i: (0, i)),
         out_shape=jax.ShapeDtypeStruct((part * chunks, width), BF16),
-        compiler_params=params(48),
-        cost_estimate=cost(
-            2 * part * chunks * steps * tokens * width, 2 * (steps * tokens + part * chunks) * width
-        ),
+        compiler_params=params(),
         name="weight_grad",
     )(*cots, *mixed, after)
 
 
-def tail_kernel(x_ref, before_ref, out_ref):
+def tail_kernel(x_ref, before_ref, *refs):
+    out_ref = refs[-1]
     rows = x_ref.shape[2]
     out_ref[0:PAD] = x_ref[0, 0, rows - PAD :]
     for i in (1, 2):
@@ -490,7 +491,7 @@
         out_ref[begin + PAD : begin + PAD + rows] = x_ref[0, i]
 
 
-def tail_of(x):
+def tail_of(x, after):
     seq, _, rows, cols = x.shape
 
     def block(s):
@@ -500,12 +501,12 @@
     return pl.pallas_call(
         tail_kernel,
         grid=(1,),
-        in_specs=[block(seq - 1), block(seq - 2)],
+        in_specs=[block(seq - 1), block(seq - 2)] + [pl.BlockSpec(memory_space=pl.ANY)] * len(after),
         out_specs=pl.BlockSpec((out_rows, cols), lambda i: (0, 0)),
         out_shape=jax.ShapeDtypeStruct((out_rows, cols), BF16),
-        compiler_params=params(32),
+        compiler_params=params(),
         name="tail",
-    )(x, x)
+    )(x, x, *after)
 
 
 def head_kernel(mo_ref, mr_ref, *refs):
@@ -537,7 +538,7 @@
         in_specs=[whole, whole] + feat_specs * len(mixers),
         out_specs=pl.BlockSpec((edge + 3 * PAD, cols), lambda i: (0, 0)),
         out_shape=jax.ShapeDtypeStruct((edge + 3 * PAD, cols), BF16),
-        compiler_params=params(32),
+        compiler_params=params(),
         name="head",
     )(mixed_own, mixed_rest, *[array for mixer in mixers for array in mixer[1:]])
 
@@ -568,24 +569,29 @@
     place = places(seq)
     by_owner = pack((queries, keys, values), seq)
     x = lax.all_to_all(by_owner, "seq", split_axis=0, concat_axis=0, tiled=True)
-    halo = along(tail_of(x), fsdp, 1)
-    cots = gather_cotangent(cotangent, col_part, by_owner, [halo])
+    held = own_cotangent(cotangent, col_part, by_owner)
+    halo = along(tail_of(x, [fwd_table, held]), fsdp, 1)
     mixers = [forward(x, halo, short_taps, skip, fwd_table, place, h, chunks) for h in range(chunks)]
-
-    parts = []
+    cots = gather_cotangent(held, [mixer[0] for mixer in mixers])
+
+    parts, heads = [], []
     for step in range(1, ys):
-        parts.append(mixed_grad(cots, weights, place, step, BF16, parts[-1] if parts else place))
+        part, head = mixed_grad(cots, weights, place, step, BF16, parts[-1] if parts else place)
+        parts.append(part)
+        heads.append(around(head, "y", -step))
+    mixed_own, own_head = mixed_grad(cots, weights, place, 0, F32, parts[-1])
     rest = [around(parts[step - 1], "y", -step) for step in range(1, ys)]
     mixed_rest = rest[0] if len(rest) == 1 else sum(piece.astype(F32) for piece in rest)
+    head_rest = heads[0] if len(heads) == 1 else sum(piece.astype(F32) for piece in heads)
+    head = head_of(own_head, head_rest, mixers)
+    later = along(head, fsdp, -1)
 
     mixed_all = [
         around(mixers[h][0], "y", step) if step else mixers[h][0] for step in range(ys) for h in range(chunks)
     ]
-    weight_sum = weight_grad(cots, mixed_all, chunks, grad_scale, parts[-1])
+    weight_sum = weight_grad(cots, mixed_all, chunks, grad_scale, head)
     weight_part = lax.psum_scatter(weight_sum, "z", scatter_dimension=1, tiled=True)
 
-    mixed_own = mixed_grad(cots, weights, place, 0, F32, weight_sum)
-    later = along(head_of(mixed_own, mixed_rest, mixers), fsdp, -1)
     grads, short_parts, long_parts = [], [], []
     for h in range(chunks):
         _, feats, filt = mixers[h]

time: 315 us -> 279 us (0.89)
  blocking collectives: 40.9 us -> 0 us
  Pallas kernels: 64 us -> 90 us
  local copies, waits for them, and re-layouts: 31.6 us -> 11.5 us
  waiting for transfers between devices: 101 us -> 94.3 us
    all_to_all x1 -> x0, blocking collectives: 40.9 us -> none  [body(): x = lax.all_to_all(by_owner, 'seq', split_axis=0, concat_axis=0, tiled=True)]
    ppermute x2, waiting for transfers between devices: 10.5 us -> 42.8 us  [along(): lax.ppermute(block, axis, [(i, i + distance) for i in range(size) if 0 <=...]
    ppermute x5, waiting for transfers between devices: 39.4 us -> 15.1 us  [across(): lax.ppermute(block, axis, [(i, i ^ bit) for i in range(lax.axis_size(axis...]
    unnamed x64 -> x34, local copies, waits for them, and re-layouts: 30.2 us -> 8.79 us
    ppermute x4 -> x5, waiting for transfers between devices: 42.5 us -> 22.7 us  [around(): lax.ppermute(block, axis, [(i, (i + distance) % size) for i in range(size)])]
    ppermute x4 -> x5, starting transfers between devices: 6.76 us -> 24.6 us  [around(): lax.ppermute(block, axis, [(i, (i + distance) % size) for i in range(size)])]
    ppermute x5, starting transfers between devices: 38.7 us -> 21.2 us  [across(): lax.ppermute(block, axis, [(i, i ^ bit) for i in range(lax.axis_size(axis...]
    pallas_call x2, Pallas kernels: 0.82 us -> 7.26 us  [join(): pl.pallas_call(functools.partial(join_kernel, axis, len(parts)), grid=(Z,...]
  transfers between devices with their start and end apart: 15 -> 17, of which waited for: 9 -> 9; matrix products, arithmetic and copies ran while one was open for 0% -> 2% of each run, Pallas kernels for 18% -> 29%
where the time goes in v1:
time: 279 us; the launch traced here: 277 us
  waiting for transfers between devices  94.3 us (34%)
  Pallas kernels  90 us (32%)
  starting transfers between devices  62.4 us (22%)
  between operations  14.2 us (5%)
  local copies, waits for them, and re-layouts  11.5 us (4%)
  other arithmetic  4.95 us (2%)
    ppermute x2, waiting for transfers between devices, along(): lax.ppermute(block, axis, [(i, i + distance) for i in range(size) if 0 <=...  42.8 us
    ppermute x5, starting transfers between devices, around(): lax.ppermute(block, axis, [(i, (i + distance) % size) for i in range(size)])  24.6 us
    ppermute x5, waiting for transfers between devices, around(): lax.ppermute(block, axis, [(i, (i + distance) % size) for i in range(size)])  22.7 us
    ppermute x5, starting transfers between devices, across(): lax.ppermute(block, axis, [(i, i ^ bit) for i in range(lax.axis_size(axis...  21.2 us
    pallas_call x2, Pallas kernels, backward(): pl.pallas_call(backward_kernel, grid=(tiles,), in_specs=[tok, tok, pl.Blo...  21.1 us
    pallas_call x2, Pallas kernels, forward(): pl.pallas_call(forward_kernel, grid_spec=pltpu.PrefetchScalarGridSpec(num...  15.3 us
    ppermute x5, waiting for transfers between devices, across(): lax.ppermute(block, axis, [(i, i ^ bit) for i in range(lax.axis_size(axis...  15.1 us
    pallas_call x2, Pallas kernels, mixed_grad(): pl.pallas_call(mixed_grad_kernel, grid_spec=pltpu.PrefetchScalarGridSpec(...  14.5 us
  transfers between devices with their start and end apart: 17, of which 9 were waited for; matrix products, arithmetic and copies ran while one was open for 2% of the time, Pallas kernels for 29%

profile of v1, /device:TPU:0, one launch (start us, length us, event | category | flops | bytes accessed | tf_op | source)
XLA Modules:
  0.0 277.3 jit_solution(18165161151853337626)
XLA Ops:
  7.9 4.2 %pack.1.refs_2_ = bf16[4,3,128,1024]{3,2,1,0:T(8,128)(2,1)} custom-call(bf16[128,4096]{1,0:T(8,128)(2,1)} %refs_0_.2, bf16[128,4096]{1,0:T(8,128)(2,1)} %refs_1_.2, bf16[128,4096]{1,0:T(8,128)(2,1)} %refs_2_.1), custom_call_target="tpu_custom_call" | custom-call | tf_op jit(solution)/shard_map/pack/pallas_call | solution.py:282
  12.1 4.2 %all-to-all-start = ((bf16[4,3,128,1024]{3,2,1,0:T(8,128)(2,1)}), bf16[4,3,128,1024]{3,2,1,0:T(8,128)(2,1)S(1)}, u32[]{:S(2)}, u32[]{:S(2)}) async-start(bf16[4,3,128,1024]{3,2,1,0:T(8,128)(2,1)} %pack.1.refs_2_), calls=%async_computation | async-start | bytes 6291456 | tf_op jit(solution)/shard_map/all_to_all | solution.py:571
  16.3 3.5 %split.1 = (bf16[128,2048]{1,0:T(8,128)(2,1)}, bf16[128,2048]{1,0:T(8,128)(2,1)}) custom-call(s32[1]{0:T(128)} %bitcast.y_ref, bf16[128,4096]{1,0:T(8,128)(2,1)} %refs_1_.3, bf16[128,4096]{1,0:T(8,128)(2,1)} %refs_1_.3, bf16[4,3,128,1024]{3,2,1,0:T(8,128)(2,1)} %pack.1.refs_2_), custom_call_target="tpu_custom_call" | custom-call | tf_op jit(solution)/shard_map/split/pallas_call | solution.py:354
  22.3 12.7 %collective-permute-done = bf16[128,2048]{1,0:T(8,128)(2,1)S(1)} collective-permute-done((bf16[128,2048]{1,0:T(8,128)(2,1)}, bf16[128,2048]{1,0:T(8,128)(2,1)S(1)}, u32[]{:S(2)}, u32[]{:S(2)}) %collective-permute-start) | collective-permute-done | bytes 524320 | tf_op jit(solution)/shard_map/ppermute | solution.py:323
  35.8 3.4 %join.2.refs_1_.refs_0_ = bf16[2,1,128,2048]{3,2,1,0:T(8,128)(2,1)} custom-call(bf16[1,1,128,2048]{3,2,1,0:T(8,128)(2,1)} %bitcast.12, bf16[1,1,128,2048]{3,2,1,0:T(8,128)(2,1)} %bitcast.13), custom_call_target="tpu_custom_call" | custom-call | tf_op jit(solution)/shard_map/join/pallas_call | solution.py:384
  42.3 6.8 %tables.1 = (bf16[8192,256]{1,0:T(8,128)(2,1)}, bf16[8192,256]{1,0:T(8,128)(2,1)}) custom-call(f32[64,256]{1,0:T(8,128)} %pad.8.fwd_ref, f32[64,256]{1,0:T(8,128)} %pad.9.bwd_ref), custom_call_target="tpu_custom_call" | custom-call | tf_op jit(solution)/shard_map/tables/pallas_call | solution.py:41
  49.0 5.1 %all-to-all-done.x_ref.before_ref = bf16[4,3,128,1024]{3,2,1,0:T(8,128)(2,1)S(1)} async-done(((bf16[4,3,128,1024]{3,2,1,0:T(8,128)(2,1)}), bf16[4,3,128,1024]{3,2,1,0:T(8,128)(2,1)S(1)}, u32[]{:S(2)}, u32[]{:S(2)}) %all-to-all-start) | async-done | bytes 3145760 | tf_op jit(solution)/shard_map/all_to_all | solution.py:571
  58.0 3.9 %collective-permute-start.2 = (bf16[304,1024]{1,0:T(8,128)(2,1)}, bf16[304,1024]{1,0:T(8,128)(2,1)S(1)}, u32[]{:S(2)}, u32[]{:S(2)}) collective-permute-start(bf16[304,1024]{1,0:T(8,128)(2,1)} %tail.1), channel_id=1, source_target_pairs={{0,4},{4,8},{8,12},{12,16},{16,20},{20,24},{24,28},{1,5},{5,9},{9,... | collective-permute-start | bytes 1867784 | tf_op jit(solution)/shard_map/ppermute | solution.py:318
  62.5 12.5 %collective-permute-done.2.h_ref = bf16[304,1024]{1,0:T(8,128)(2,1)S(1)} collective-permute-done((bf16[304,1024]{1,0:T(8,128)(2,1)}, bf16[304,1024]{1,0:T(8,128)(2,1)S(1)}, u32[]{:S(2)}, u32[]{:S(2)}) %collective-permute-start.2) | collective-permute-done | bytes 622624 | tf_op jit(solution)/shard_map/ppermute | solution.py:318
  75.7 7.7 %forward.3 = (bf16[512,512]{1,0:T(8,128)(2,1)}, f32[3,512,512]{2,1,0:T(8,128)}, f32[512,512]{1,0:T(8,128)}) custom-call(s32[4]{0:T(128)} %shift-left_add_fusion.place_ref._, bf16[4,3,128,1024]{3,2,1,0:T(8,128)(2,1)} %copy-done, bf16[304,1024]{1,0:T(8,128)(2,1)} %copy-done.5, f32[3,7,1024]{2,1,0:T(8,128)} %taps_ref.7, f32[1,1024]{1,0:T(1,128)} %bitcast.17, ...), custom_call_target="tpu_custom_call" | custom-call | tf_op jit(solution)/shard_map/forward/pallas_call | solution.py:113
  83.4 7.7 %forward.2 = (bf16[512,512]{1,0:T(8,128)(2,1)}, f32[3,512,512]{2,1,0:T(8,128)}, f32[512,512]{1,0:T(8,128)}) custom-call(s32[4]{0:T(128)} %shift-left_add_fusion.place_ref._, bf16[4,3,128,1024]{3,2,1,0:T(8,128)(2,1)} %copy-done, bf16[304,1024]{1,0:T(8,128)(2,1)} %copy-done.5, f32[3,7,1024]{2,1,0:T(8,128)} %taps_ref.7, f32[1,1024]{1,0:T(1,128)} %bitcast.18, ...), custom_call_target="tpu_custom_call" | custom-call | tf_op jit(solution)/shard_map/forward/pallas_call | solution.py:113
  91.1 3.8 %join.3.a_ref = bf16[2,2,128,2048]{3,2,1,0:T(8,128)(2,1)} custom-call(bf16[2,1,128,2048]{3,2,1,0:T(8,128)(2,1)} %join.2.refs_1_.refs_0_, bf16[2,1,128,2048]{3,2,1,0:T(8,128)(2,1)} %collective-permute-done.1.refs_1_, bf16[512,512]{1,0:T(8,128)(2,1)} %get-tuple-element.33.refs_2_.refs_0_, bf16[512,512]{1,0:T(8,128)(2,1)} %get-tuple-element.34.refs_3_.refs_1_), custom_call_target="tpu_custom_call" | custom-call | tf_op jit(solution)/shard_map/join/pallas_call | solution.py:384
  95.0 16.0 %collective-permute-start.8 = (bf16[512,512]{1,0:T(8,128)(2,1)S(1)}, bf16[512,512]{1,0:T(8,128)(2,1)}, u32[]{:S(2)}, u32[]{:S(2)}) collective-permute-start(bf16[512,512]{1,0:T(8,128)(2,1)S(1)} %copy-done.6), channel_id=1, source_target_pairs={{0,4},{4,0},{1,5},{5,1},{2,6},{6,2},{3,7},{7,3},{8,12},{12,8},{9,1... | collective-permute-start | bytes 1572872 | tf_op jit(solution)/shard_map/ppermute | solution.py:323
  112.5 7.1 %mixed_grad.2 = (bf16[512,1024]{1,0:T(8,128)(2,1)}, bf16[144,1024]{1,0:T(8,128)(2,1)}) custom-call(s32[4]{0:T(128)} %shift-left_add_fusion.place_ref._, bf16[2,2,128,2048]{3,2,1,0:T(8,128)(2,1)} %join.3.a_ref, bf16[2,2,128,2048]{3,2,1,0:T(8,128)(2,1)} %copy-done.1, bf16[1024,2048]{1,0:T(8,128)(2,1)} %all-gather.2.cloned.1.call-done.w_ref, ...), custom_call_target="tpu_custom_call" | custom-call | tf_op jit(solution)/shard_map/mixed_grad/pallas_call | solution.py:426
  119.5 4.2 %collective-permute-start.5 = (bf16[144,1024]{1,0:T(8,128)(2,1)}, bf16[144,1024]{1,0:T(8,128)(2,1)S(1)}, u32[]{:S(2)}, u32[]{:S(2)}) collective-permute-start(bf16[144,1024]{1,0:T(8,128)(2,1)} %get-tuple-element.40), channel_id=1, source_target_pairs={{0,4},{4,0},{1,5},{5,1},{2,6},{6,2},{3,7},{7,3},{8,12},{12,8},{9,1... | collective-permute-start | bytes 884744 | tf_op jit(solution)/shard_map/ppermute | solution.py:323
  123.7 7.4 %mixed_grad.3 = (f32[512,1024]{1,0:T(8,128)}, f32[144,1024]{1,0:T(8,128)}) custom-call(s32[4]{0:T(128)} %shift-left_add_fusion.place_ref._, bf16[2,2,128,2048]{3,2,1,0:T(8,128)(2,1)} %join.3.a_ref, bf16[2,2,128,2048]{3,2,1,0:T(8,128)(2,1)} %copy-done.1, bf16[1024,2048]{1,0:T(8,128)(2,1)} %all-gather.2.cloned.1.call-done.w_ref, ...), custom_call_target="tpu_custom_call" | custom-call | tf_op jit(solution)/shard_map/mixed_grad/pallas_call | solution.py:426
  131.1 10.0 %collective-permute-done.5.mr_ref = bf16[144,1024]{1,0:T(8,128)(2,1)S(1)} collective-permute-done((bf16[144,1024]{1,0:T(8,128)(2,1)}, bf16[144,1024]{1,0:T(8,128)(2,1)S(1)}, u32[]{:S(2)}, u32[]{:S(2)}) %collective-permute-start.5) | collective-permute-done | bytes 294944 | tf_op jit(solution)/shard_map/ppermute | solution.py:323
  144.5 8.4 %weight_grad.1 = bf16[1024,2048]{1,0:T(8,128)(2,1)} custom-call(bf16[2,2,128,2048]{3,2,1,0:T(8,128)(2,1)} %join.3.a_ref, bf16[2,2,128,2048]{3,2,1,0:T(8,128)(2,1)} %copy-done.1, bf16[512,512]{1,0:T(8,128)(2,1)} %get-tuple-element.33.refs_2_.refs_0_, bf16[512,512]{1,0:T(8,128)(2,1)} %get-tuple-element.34.refs_3_.refs_1_, ...), custom_call_target="tpu_custom_call" | custom-call | tf_op jit(solution)/shard_map/weight_grad/pallas_call | solution.py:472
  157.2 30.3 %collective-permute-done.6.n_ref = bf16[192,1024]{1,0:T(8,128)(2,1)S(1)} collective-permute-done((bf16[192,1024]{1,0:T(8,128)(2,1)S(1)}, bf16[192,1024]{1,0:T(8,128)(2,1)S(1)}, u32[]{:S(2)}, u32[]{:S(2)}) %collective-permute-start.6) | collective-permute-done | bytes 393248 | tf_op jit(solution)/shard_map/ppermute | solution.py:318
  188.6 10.6 %backward.3 = (bf16[4,3,128,512]{3,2,1,0:T(8,128)(2,1)}, f32[3,8,512]{2,1,0:T(8,128)}, f32[32,128]{1,0:T(8,128)}) custom-call(f32[512,1024]{1,0:T(8,128)} %get-tuple-element.36.mo_ref, bf16[512,1024]{1,0:T(8,128)(2,1)} %copy-done.4, f32[3,512,512]{2,1,0:T(8,128)} %get-tuple-element.41.refs_2_.f_ref, f32[512,512]{1,0:T(8,128)} %get-tuple-element.42.refs_3_.filt_ref, ...), custom_call_target="tpu_custom_call" | custom-call | tf_op jit(solution)/shard_map/backward/pallas_call | solution.py:237
  199.1 3.6 %all-to-all-start.2 = ((bf16[4,3,128,512]{3,2,1,0:T(8,128)(2,1)}), bf16[4,3,128,512]{3,2,1,0:T(8,128)(2,1)S(1)}, u32[]{:S(2)}, u32[]{:S(2)}) async-start(bf16[4,3,128,512]{3,2,1,0:T(8,128)(2,1)} %get-tuple-element.45), calls=%async_computation.2 | async-start | bytes 3145728 | tf_op jit(solution)/shard_map/all_to_all | solution.py:601
  202.7 10.5 %backward.2 = (bf16[4,3,128,512]{3,2,1,0:T(8,128)(2,1)}, f32[3,8,512]{2,1,0:T(8,128)}, f32[32,128]{1,0:T(8,128)}) custom-call(f32[512,1024]{1,0:T(8,128)} %get-tuple-element.36.mo_ref, bf16[512,1024]{1,0:T(8,128)(2,1)} %copy-done.4, f32[3,512,512]{2,1,0:T(8,128)} %get-tuple-element.37.refs_0_.f_ref, f32[512,512]{1,0:T(8,128)} %get-tuple-element.38.refs_1_.filt_ref, ...), custom_call_target="tpu_custom_call" | custom-call | tf_op jit(solution)/shard_map/backward/pallas_call | solution.py:237
  214.8 8.0 %all-to-all-done.2.refs_1_ = bf16[4,3,128,512]{3,2,1,0:T(8,128)(2,1)S(1)} async-done(((bf16[4,3,128,512]{3,2,1,0:T(8,128)(2,1)}), bf16[4,3,128,512]{3,2,1,0:T(8,128)(2,1)S(1)}, u32[]{:S(2)}, u32[]{:S(2)}) %all-to-all-start.2) | async-done | bytes 1572896 | tf_op jit(solution)/shard_map/all_to_all | solution.py:601
  222.8 3.6 %all-to-all-start.1 = ((bf16[4,3,128,512]{3,2,1,0:T(8,128)(2,1)}), bf16[4,3,128,512]{3,2,1,0:T(8,128)(2,1)S(1)}, u32[]{:S(2)}, u32[]{:S(2)}) async-start(bf16[4,3,128,512]{3,2,1,0:T(8,128)(2,1)} %get-tuple-element.44), calls=%async_computation.1 | async-start | bytes 3145728 | tf_op jit(solution)/shard_map/all_to_all | solution.py:601
  226.4 7.6 %collective-permute-start.9 = (f32[32,1024]{1,0:T(8,128)S(1)}, f32[32,1024]{1,0:T(8,128)S(1)}, u32[]{:S(2)}, u32[]{:S(2)}) collective-permute-start(f32[32,1024]{1,0:T(8,128)S(1)} %pad_maximum_fusion), channel_id=1, source_target_pairs={{0,4},{4,0},{1,5},{5,1},{2,6},{6,2},{3,7},{7,3},{8,12},{12,8},{9,1... | collective-permute-start | bytes 393224 | tf_op jit(solution)/shard_map/ppermute | solution.py:327
  233.9 4.1 %collective-permute-done.9 = f32[32,1024]{1,0:T(8,128)S(1)} collective-permute-done((f32[32,1024]{1,0:T(8,128)S(1)}, f32[32,1024]{1,0:T(8,128)S(1)}, u32[]{:S(2)}, u32[]{:S(2)}) %collective-permute-start.9) | collective-permute-done | bytes 131104 | tf_op jit(solution)/shard_map/ppermute | solution.py:327
  238.1 8.6 %collective-permute-start.10 = (f32[32,1024]{1,0:T(8,128)S(1)}, f32[32,1024]{1,0:T(8,128)S(1)}, u32[]{:S(2)}, u32[]{:S(2)}) collective-permute-start(f32[32,1024]{1,0:T(8,128)S(1)} %fusion), channel_id=1, source_target_pairs={{0,8},{8,0},{16,24},{24,16},{1,9},{9,1},{17,25},{25,17},{2,10},{10... | collective-permute-start | bytes 393224 | tf_op jit(solution)/shard_map/ppermute | solution.py:327
  246.7 5.8 %collective-permute-done.10 = f32[32,1024]{1,0:T(8,128)S(1)} collective-permute-done((f32[32,1024]{1,0:T(8,128)S(1)}, f32[32,1024]{1,0:T(8,128)S(1)}, u32[]{:S(2)}, u32[]{:S(2)}) %collective-permute-start.10) | collective-permute-done | bytes 131104 | tf_op jit(solution)/shard_map/ppermute | solution.py:327
  252.5 3.4 %collective-permute-start.11 = (f32[32,1024]{1,0:T(8,128)S(1)}, f32[32,1024]{1,0:T(8,128)S(1)}, u32[]{:S(2)}, u32[]{:S(2)}) collective-permute-start(f32[32,1024]{1,0:T(8,128)S(1)} %add.20), channel_id=1, source_target_pairs={{0,16},{8,24},{16,0},{24,8},{1,17},{9,25},{17,1},{25,9},{2,18},{10... | collective-permute-start | bytes 393224 | tf_op jit(solution)/shard_map/ppermute | solution.py:327
  255.9 5.2 %collective-permute-done.11 = f32[32,1024]{1,0:T(8,128)S(1)} collective-permute-done((f32[32,1024]{1,0:T(8,128)S(1)}, f32[32,1024]{1,0:T(8,128)S(1)}, u32[]{:S(2)}, u32[]{:S(2)}) %collective-permute-start.11) | collective-permute-done | bytes 131104 | tf_op jit(solution)/shard_map/ppermute | solution.py:327
  263.5 4.2 %unpack.1 = (bf16[128,4096]{1,0:T(8,128)(2,1)}, bf16[128,4096]{1,0:T(8,128)(2,1)}, bf16[128,4096]{1,0:T(8,128)(2,1)}) custom-call(bf16[4,3,128,512]{3,2,1,0:T(8,128)(2,1)} %copy-done.3, bf16[4,3,128,512]{3,2,1,0:T(8,128)(2,1)} %copy-done.2), custom_call_target="tpu_custom_call" | custom-call | tf_op jit(solution)/shard_map/unpack/pallas_call | solution.py:305
  267.6 2.8 %convert_element_type.7 = f32[1024,512]{1,0:T(8,128)} convert(bf16[1024,512]{1,0:T(8,128)(2,1)} %reduce-scatter.2.cloned.1.call-done) | non-fusion elementwise | flops 524288 | bytes 3145728 | tf_op jit(solution)/shard_map/convert_element_type | solution.py:620
  (69 shorter events, 26.6 us)
Async XLA Ops:
  7.2 103.9 %all-gather.2.cloned.1.call-start = ((), (), s32[]{:S(2)}) async-start(), calls=%async_computation.4 | async-start | bytes 5242880 | tf_op jit(solution)/shard_map/all_gather | solution.py:566
  12.1 42.0 %all-to-all-start = ((bf16[4,3,128,1024]{3,2,1,0:T(8,128)(2,1)}), bf16[4,3,128,1024]{3,2,1,0:T(8,128)(2,1)S(1)}, u32[]{:S(2)}, u32[]{:S(2)}) async-start(bf16[4,3,128,1024]{3,2,1,0:T(8,128)(2,1)} %pack.1.refs_2_), calls=%async_computation | async-start | bytes 6291456 | tf_op jit(solution)/shard_map/all_to_all | solution.py:571
  16.3 251.4 %reduce-scatter.2.cloned.1.call-start = ((), (), s32[]{:S(2)}) async-start(), calls=%async_computation.5 | async-start | bytes 5242880 | tf_op jit(solution)/shard_map/reduce_scatter | solution.py:593
  16.3 24.6 %copy-start.13 = (f32[128,64]{0,1:T(8,128)S(1)}, f32[128,64]{0,1:T(8,128)}, u32[]{:S(2)}) copy-start(f32[128,64]{0,1:T(8,128)} %param.14) | copy-start | bytes 98308
  19.7 15.2 %collective-permute-start = (bf16[128,2048]{1,0:T(8,128)(2,1)}, bf16[128,2048]{1,0:T(8,128)(2,1)S(1)}, u32[]{:S(2)}, u32[]{:S(2)}) collective-permute-start(bf16[128,2048]{1,0:T(8,128)(2,1)} %get-tuple-element.31), channel_id=1, source_target_pairs={{0,4},{4,0},{1,5},{5,1},{2,6},{6,2},{3,7},{7,3},{8,12},{12,8},{9,1... | collective-permute-start | bytes 1572872 | tf_op jit(solution)/shard_map/ppermute | solution.py:323
  35.0 0.8 copy-start.11
  39.2 51.9 %collective-permute-start.1 = (bf16[2,1,128,2048]{3,2,1,0:T(8,128)(2,1)}, bf16[2,1,128,2048]{3,2,1,0:T(8,128)(2,1)}, u32[]{:S(2)}, u32[]{:S(2)}) collective-permute-start(bf16[2,1,128,2048]{3,2,1,0:T(8,128)(2,1)} %join.2.refs_1_.refs_0_), channel_id=1, source_target_pairs={{0,2},{1,3},{2,0},{3,1},{4,6},{5,7},{6,4},{7,5},{8,10},{9,11},{10,... | collective-permute-start | bytes 3145736 | tf_op jit(solution)/shard_map/ppermute | solution.py:327
  54.1 1.6 copy-start
  58.0 16.9 %collective-permute-start.2 = (bf16[304,1024]{1,0:T(8,128)(2,1)}, bf16[304,1024]{1,0:T(8,128)(2,1)S(1)}, u32[]{:S(2)}, u32[]{:S(2)}) collective-permute-start(bf16[304,1024]{1,0:T(8,128)(2,1)} %tail.1), channel_id=1, source_target_pairs={{0,4},{4,8},{8,12},{12,16},{16,20},{20,24},{24,28},{1,5},{5,9},{9,... | collective-permute-start | bytes 1867784 | tf_op jit(solution)/shard_map/ppermute | solution.py:318
  74.9 0.8 copy-start.5
  91.1 3.9 %copy-start.6 = (bf16[512,512]{1,0:T(8,128)(2,1)S(1)}, bf16[512,512]{1,0:T(8,128)(2,1)}, u32[]{:S(2)}) copy-start(bf16[512,512]{1,0:T(8,128)(2,1)} %get-tuple-element.34.refs_3_.refs_1_) | copy-start | bytes 1572868
  91.1 19.9 %copy-start.7 = (bf16[512,512]{1,0:T(8,128)(2,1)S(1)}, bf16[512,512]{1,0:T(8,128)(2,1)}, u32[]{:S(2)}) copy-start(bf16[512,512]{1,0:T(8,128)(2,1)} %get-tuple-element.33.refs_2_.refs_0_) | copy-start | bytes 1572868
  95.0 16.1 %collective-permute-start.3 = (bf16[2,2,128,2048]{3,2,1,0:T(8,128)(2,1)}, bf16[2,2,128,2048]{3,2,1,0:T(8,128)(2,1)S(1)}, u32[]{:S(2)}, u32[]{:S(2)}) collective-permute-start(bf16[2,2,128,2048]{3,2,1,0:T(8,128)(2,1)} %join.3.a_ref), channel_id=1, source_target_pairs={{0,1},{1,0},{2,3},{3,2},{4,5},{5,4},{6,7},{7,6},{8,9},{9,8},{10,11... | collective-permute-start | bytes 6291464 | tf_op jit(solution)/shard_map/ppermute | solution.py:327
  95.0 49.5 %collective-permute-start.8 = (bf16[512,512]{1,0:T(8,128)(2,1)S(1)}, bf16[512,512]{1,0:T(8,128)(2,1)}, u32[]{:S(2)}, u32[]{:S(2)}) collective-permute-start(bf16[512,512]{1,0:T(8,128)(2,1)S(1)} %copy-done.6), channel_id=1, source_target_pairs={{0,4},{4,0},{1,5},{5,1},{2,6},{6,2},{3,7},{7,3},{8,12},{12,8},{9,1... | collective-permute-start | bytes 1572872 | tf_op jit(solution)/shard_map/ppermute | solution.py:323
  111.0 33.5 %collective-permute-start.7 = (bf16[512,512]{1,0:T(8,128)(2,1)S(1)}, bf16[512,512]{1,0:T(8,128)(2,1)}, u32[]{:S(2)}, u32[]{:S(2)}) collective-permute-start(bf16[512,512]{1,0:T(8,128)(2,1)S(1)} %copy-done.7), channel_id=1, source_target_pairs={{0,4},{4,0},{1,5},{5,1},{2,6},{6,2},{3,7},{7,3},{8,12},{12,8},{9,1... | collective-permute-start | bytes 1572872 | tf_op jit(solution)/shard_map/ppermute | solution.py:323
  111.1 1.4 copy-start.1
  119.5 21.6 %collective-permute-start.5 = (bf16[144,1024]{1,0:T(8,128)(2,1)}, bf16[144,1024]{1,0:T(8,128)(2,1)S(1)}, u32[]{:S(2)}, u32[]{:S(2)}) collective-permute-start(bf16[144,1024]{1,0:T(8,128)(2,1)} %get-tuple-element.40), channel_id=1, source_target_pairs={{0,4},{4,0},{1,5},{5,1},{2,6},{6,2},{3,7},{7,3},{8,12},{12,8},{9,1... | collective-permute-start | bytes 884744 | tf_op jit(solution)/shard_map/ppermute | solution.py:323
  152.9 1.2 copy-start.10
  152.9 3.0 %copy-start.8 = (bf16[192,1024]{1,0:T(8,128)(2,1)S(1)}, bf16[192,1024]{1,0:T(8,128)(2,1)}, u32[]{:S(2)}) copy-start(bf16[192,1024]{1,0:T(8,128)(2,1)} %head.1.refs_4_) | copy-start | bytes 1179652
  154.1 33.4 %collective-permute-start.4 = (bf16[512,1024]{1,0:T(8,128)(2,1)S(1)}, bf16[512,1024]{1,0:T(8,128)(2,1)S(1)}, u32[]{:S(2)}, u32[]{:S(2)}) collective-permute-start(bf16[512,1024]{1,0:T(8,128)(2,1)S(1)} %copy-done.10), channel_id=1, source_target_pairs={{0,4},{4,0},{1,5},{5,1},{2,6},{6,2},{3,7},{7,3},{8,12},{12,8},{9,1... | collective-permute-start | bytes 3145736 | tf_op jit(solution)/shard_map/ppermute | solution.py:323
  155.9 31.6 %collective-permute-start.6 = (bf16[192,1024]{1,0:T(8,128)(2,1)S(1)}, bf16[192,1024]{1,0:T(8,128)(2,1)S(1)}, u32[]{:S(2)}, u32[]{:S(2)}) collective-permute-start(bf16[192,1024]{1,0:T(8,128)(2,1)S(1)} %copy-done.8), channel_id=1, source_target_pairs={{4,0},{8,4},{12,8},{16,12},{20,16},{24,20},{28,24},{5,1},{9,5},{13... | collective-permute-start | bytes 1179656 | tf_op jit(solution)/shard_map/ppermute | solution.py:318
  187.5 1.1 copy-start.4
  199.1 23.6 %all-to-all-start.2 = ((bf16[4,3,128,512]{3,2,1,0:T(8,128)(2,1)}), bf16[4,3,128,512]{3,2,1,0:T(8,128)(2,1)S(1)}, u32[]{:S(2)}, u32[]{:S(2)}) async-start(bf16[4,3,128,512]{3,2,1,0:T(8,128)(2,1)} %get-tuple-element.45), calls=%async_computation.2 | async-start | bytes 3145728 | tf_op jit(solution)/shard_map/all_to_all | solution.py:601
  202.7 10.5 %copy-start.16 = (f32[32,128]{1,0:T(8,128)S(1)}, f32[32,128]{1,0:T(8,128)}, u32[]{:S(2)}) copy-start(f32[32,128]{1,0:T(8,128)} %get-tuple-element.52) | copy-start | bytes 49156
  202.7 11.3 %copy-start.15 = (f32[3,8,512]{2,1,0:T(8,128)S(1)}, f32[3,8,512]{2,1,0:T(8,128)}, u32[]{:S(2)}) copy-start(f32[3,8,512]{2,1,0:T(8,128)} %get-tuple-element.50) | copy-start | bytes 147460
  222.8 39.6 %copy-start.2 = (bf16[4,3,128,512]{3,2,1,0:T(8,128)(2,1)}, bf16[4,3,128,512]{3,2,1,0:T(8,128)(2,1)S(1)}, u32[]{:S(2)}) copy-start(bf16[4,3,128,512]{3,2,1,0:T(8,128)(2,1)S(1)} %all-to-all-done.2.refs_1_) | copy-start | bytes 4718596
  222.8 39.6 %all-to-all-start.1 = ((bf16[4,3,128,512]{3,2,1,0:T(8,128)(2,1)}), bf16[4,3,128,512]{3,2,1,0:T(8,128)(2,1)S(1)}, u32[]{:S(2)}, u32[]{:S(2)}) async-start(bf16[4,3,128,512]{3,2,1,0:T(8,128)(2,1)} %get-tuple-element.44), calls=%async_computation.1 | async-start | bytes 3145728 | tf_op jit(solution)/shard_map/all_to_all | solution.py:601
  226.4 11.7 %collective-permute-start.9 = (f32[32,1024]{1,0:T(8,128)S(1)}, f32[32,1024]{1,0:T(8,128)S(1)}, u32[]{:S(2)}, u32[]{:S(2)}) collective-permute-start(f32[32,1024]{1,0:T(8,128)S(1)} %pad_maximum_fusion), channel_id=1, source_target_pairs={{0,4},{4,0},{1,5},{5,1},{2,6},{6,2},{3,7},{7,3},{8,12},{12,8},{9,1... | collective-permute-start | bytes 393224 | tf_op jit(solution)/shard_map/ppermute | solution.py:327
  238.1 14.4 %collective-permute-start.10 = (f32[32,1024]{1,0:T(8,128)S(1)}, f32[32,1024]{1,0:T(8,128)S(1)}, u32[]{:S(2)}, u32[]{:S(2)}) collective-permute-start(f32[32,1024]{1,0:T(8,128)S(1)} %fusion), channel_id=1, source_target_pairs={{0,8},{8,0},{16,24},{24,16},{1,9},{9,1},{17,25},{25,17},{2,10},{10... | collective-permute-start | bytes 393224 | tf_op jit(solution)/shard_map/ppermute | solution.py:327
  252.5 8.5 %collective-permute-start.11 = (f32[32,1024]{1,0:T(8,128)S(1)}, f32[32,1024]{1,0:T(8,128)S(1)}, u32[]{:S(2)}, u32[]{:S(2)}) collective-permute-start(f32[32,1024]{1,0:T(8,128)S(1)} %add.20), channel_id=1, source_target_pairs={{0,16},{8,24},{16,0},{24,8},{1,17},{9,25},{17,1},{25,9},{2,18},{10... | collective-permute-start | bytes 393224 | tf_op jit(solution)/shard_map/ppermute | solution.py:327
  261.1 9.4 %copy-start.14 = (f32[3,8,1024]{2,1,0:T(8,128)}, f32[3,8,1024]{2,1,0:T(8,128)S(1)}, u32[]{:S(2)}) copy-start(f32[3,8,1024]{2,1,0:T(8,128)S(1)} %slice_bitcast_fusion) | copy-start | bytes 294916
  262.4 1.1 copy-start.3
  (2 other events, 1.5 us)
Sparse Core Ops, SparseCore 0:
  9.6 83.4 all-gather.1
  153.1 98.0 reduce-scatter.1

commit v2 on v1

--- a/solution.py
+++ b/solution.py
@@ -58,37 +58,35 @@
     return out
 
 
-def forward_kernel(place_ref, x_ref, h_ref, taps_ref, skip_ref, tab_ref, mixed_ref, f_ref, filt_ref, xf, pf, pb, wide):
+def features_of(taps_ref, row, xf, i, begin):
+    total = taps_ref[row, 0:1] * xf[i, PAD + begin : PAD + begin + LTAPS]
+    for j in range(1, SHORT):
+        total = total + taps_ref[row, j : j + 1] * xf[i, PAD + begin - j : PAD + begin - j + LTAPS]
+    return total
+
+
+def forward_kernel(
+    place_ref, x_ref, h_ref, taps_ref, skip_ref, tab_ref, _, mixed_ref, f_ref, filt_ref, xf, pf, pb, wide
+):
     blocks, _, rows, _ = x_ref.shape
     tokens = blocks * rows
     per = tab_ref.shape[0] // LTAPS
-    xf[0, LTAPS : LTAPS + PAD] = h_ref[0:PAD].astype(F32)
-    for i in (1, 2):
-        begin = PAD + (i - 1) * (LTAPS + PAD)
-        xf[i, 0 : LTAPS + PAD] = h_ref[begin : begin + LTAPS + PAD].astype(F32)
     for i in range(3):
+        xf[i, 0:PAD] = h_ref[i * PAD : (i + 1) * PAD].astype(F32)
         for b in range(blocks):
-            begin = LTAPS + PAD + b * rows
+            begin = PAD + b * rows
             xf[i, begin : begin + rows] = x_ref[b, i].astype(F32)
-
-    def feature(i, base):
-        total = taps_ref[i, 0:1] * xf[i, PAD + base : PAD + base + LTAPS]
-        for j in range(1, SHORT):
-            total = total + taps_ref[i, j : j + 1] * xf[i, PAD + base - j : PAD + base - j + LTAPS]
-        return total
-
-    for n in range(tokens // LTAPS + 1):
-        base = n * LTAPS
-        own = slice(base - LTAPS, base)
-        f1 = feature(1, base)
-        f2 = feature(2, base)
+    pb[0:LTAPS] = h_ref[3 * PAD : 3 * PAD + LTAPS]
+    for begin in range(0, tokens, LTAPS):
+        own = slice(begin, begin + LTAPS)
+        f1 = features_of(taps_ref, 1, xf, 1, begin)
+        f2 = features_of(taps_ref, 2, xf, 2, begin)
         prod = f1 * f2
-        pb[base : base + LTAPS] = prod.astype(BF16)
-        if n:
-            f_ref[1, own] = f1
-            f_ref[2, own] = f2
-            f_ref[0, own] = feature(0, base)
-            pf[own] = prod
+        f_ref[1, own] = f1
+        f_ref[2, own] = f2
+        f_ref[0, own] = features_of(taps_ref, 0, xf, 0, begin)
+        pf[own] = prod
+        pb[LTAPS + begin : 2 * LTAPS + begin] = prod.astype(BF16)
     skip = skip_ref[...]
     for b in range(0, tokens // LTAPS, 2):
         low = b * LTAPS
@@ -103,7 +101,7 @@
             mixed_ref[:, pl.ds(there, LTAPS)] = mixed.T.astype(BF16)
 
 
-def forward(x, halo, short_taps, skip, table, place, chunk, chunks):
+def forward(x, halo, short_taps, skip, table, place, chunk, chunks, after):
     blocks, _, rows, cols = x.shape
     cols //= chunks
     tokens = blocks * rows
@@ -121,6 +119,7 @@
                 pl.BlockSpec((3, SHORT, LANES), lambda c, _: (0, 0, first + c)),
                 pl.BlockSpec((1, LANES), lambda c, _: (0, first + c)),
                 pl.BlockSpec((tab_rows, 2 * LTAPS), lambda c, _: (first + c, 0)),
+                pl.BlockSpec(memory_space=pl.ANY),
             ],
             out_specs=[
                 pl.BlockSpec((LANES, tokens), lambda c, _: (c, 0)),
@@ -128,7 +127,7 @@
                 pl.BlockSpec((tokens, LANES), lambda c, _: (0, c)),
             ],
             scratch_shapes=[
-                pltpu.VMEM((3, PAD + LTAPS + tokens, LANES), F32),
+                pltpu.VMEM((3, PAD + tokens, LANES), F32),
                 pltpu.VMEM((tokens, LANES), F32),
                 pltpu.VMEM((LTAPS + tokens, LANES), BF16),
                 pltpu.VMEM((tab_rows, 2 * LTAPS), F32),
@@ -141,7 +140,7 @@
         ],
         compiler_params=params(),
         name="forward",
-    )(place, x, halo, short_taps, skip, table)
+    )(place, x, halo, short_taps, skip, table, after)
 
 
 def sum_by_lag(gram):
@@ -449,64 +448,69 @@
     )(place, *cots, weights, after)
 
 
-def weight_grad_kernel(scale, chunks, a_ref, b_ref, *refs):
-    mixed, out = refs[:-2], refs[-1]
+def weight_grad_kernel(scale, a_ref, b_ref, *refs):
     steps, count, rows, tile = a_ref.shape
     tokens = count * rows
-    part = mixed[0].shape[0]
-    for h in range(chunks):
-        total = None
-        for step in range(steps):
-            for n, ref in enumerate((a_ref, b_ref)):
-                left = mixed[step * chunks + h][:, n * tokens : (n + 1) * tokens]
-                term = jnp.dot(left, ref[step].reshape(tokens, tile), preferred_element_type=F32)
-                total = term if total is None else total + term
-        out[h * part : (h + 1) * part] = (total * scale).astype(BF16)
-
-
-def weight_grad(cots, mixed, chunks, scale, after):
+    mixed, out = refs[:steps], refs[-1]
+    total = None
+    for step in range(steps):
+        for n, ref in enumerate((a_ref, b_ref)):
+            left = mixed[step][:, n * tokens : (n + 1) * tokens]
+            term = jnp.dot(left, ref[step].reshape(tokens, tile), preferred_element_type=F32)
+            total = term if total is None else total + term
+    out[...] = (total * scale).astype(BF16)
+
+
+def weight_grad(cots, mixed, chunk, chunks, scale, target, after):
     steps, count, rows, width = cots[0].shape
     part, tokens = mixed[0].shape
     tile = width // Z
     piece = pl.BlockSpec((steps, count, rows, tile), lambda i: (0, 0, 0, i))
-    return pl.pallas_call(
-        functools.partial(weight_grad_kernel, scale, chunks),
+    extra = [after] + ([] if target is None else [target])
+    return pl.pallas_call(
+        functools.partial(weight_grad_kernel, scale),
         grid=(Z,),
-        in_specs=[piece, piece] + [pl.BlockSpec((part, tokens), lambda i: (0, 0))] * len(mixed)
-        + [pl.BlockSpec(memory_space=pl.ANY)],
-        out_specs=pl.BlockSpec((part * chunks, tile), lambda i: (0, i)),
+        in_specs=[piece, piece]
+        + [pl.BlockSpec((part, tokens), lambda i: (0, 0))] * len(mixed)
+        + [pl.BlockSpec(memory_space=pl.ANY)] * len(extra),
+        out_specs=pl.BlockSpec((part, tile), lambda i: (chunk, i)),
         out_shape=jax.ShapeDtypeStruct((part * chunks, width), BF16),
+        input_output_aliases={} if target is None else {3 + len(mixed): 0},
         compiler_params=params(),
         name="weight_grad",
-    )(*cots, *mixed, after)
-
-
-def tail_kernel(x_ref, before_ref, *refs):
-    out_ref = refs[-1]
+    )(*cots, *mixed, *extra)
+
+
+def tail_kernel(x_ref, before_ref, taps_ref, *refs):
+    out_ref, xf = refs[-2:]
     rows = x_ref.shape[2]
-    out_ref[0:PAD] = x_ref[0, 0, rows - PAD :]
+    for i in range(3):
+        out_ref[i * PAD : (i + 1) * PAD] = x_ref[0, i, rows - PAD :]
     for i in (1, 2):
-        begin = PAD + (i - 1) * (PAD + rows)
-        out_ref[begin : begin + PAD] = before_ref[0, i, rows - PAD :]
-        out_ref[begin + PAD : begin + PAD + rows] = x_ref[0, i]
-
-
-def tail_of(x, after):
+        xf[i - 1, 0:PAD] = before_ref[0, i, rows - PAD :].astype(F32)
+        xf[i - 1, PAD:] = x_ref[0, i].astype(F32)
+    prod = features_of(taps_ref, 1, xf, 0, 0) * features_of(taps_ref, 2, xf, 1, 0)
+    out_ref[3 * PAD :] = prod.astype(BF16)
+
+
+def tail_of(x, short_taps, after):
     seq, _, rows, cols = x.shape
 
     def block(s):
-        return pl.BlockSpec((1, 3, rows, cols), lambda i: (s, 0, 0, 0))
-
-    out_rows = PAD + 2 * (PAD + rows)
+        return pl.BlockSpec((1, 3, rows, LANES), lambda c: (s, 0, 0, c))
+
+    out_rows = 3 * PAD + rows
     return pl.pallas_call(
         tail_kernel,
-        grid=(1,),
-        in_specs=[block(seq - 1), block(seq - 2)] + [pl.BlockSpec(memory_space=pl.ANY)] * len(after),
-        out_specs=pl.BlockSpec((out_rows, cols), lambda i: (0, 0)),
+        grid=(cols // LANES,),
+        in_specs=[block(seq - 1), block(seq - 2), pl.BlockSpec((3, SHORT, LANES), lambda c: (0, 0, c))]
+        + [pl.BlockSpec(memory_space=pl.ANY)] * len(after),
+        out_specs=pl.BlockSpec((out_rows, LANES), lambda c: (0, c)),
         out_shape=jax.ShapeDtypeStruct((out_rows, cols), BF16),
+        scratch_shapes=[pltpu.VMEM((2, PAD + rows, LANES), F32)],
         compiler_params=params(),
         name="tail",
-    )(x, x, *after)
+    )(x, x, short_taps, *after)
 
 
 def head_kernel(mo_ref, mr_ref, *refs):
@@ -570,9 +574,11 @@
     by_owner = pack((queries, keys, values), seq)
     x = lax.all_to_all(by_owner, "seq", split_axis=0, concat_axis=0, tiled=True)
     held = own_cotangent(cotangent, col_part, by_owner)
-    halo = along(tail_of(x, [fwd_table, held]), fsdp, 1)
-    mixers = [forward(x, halo, short_taps, skip, fwd_table, place, h, chunks) for h in range(chunks)]
-    cots = gather_cotangent(held, [mixer[0] for mixer in mixers])
+    halo = along(tail_of(x, short_taps, [fwd_table, held]), fsdp, 1)
+    mixers = [forward(x, halo, short_taps, skip, fwd_table, place, 0, chunks, held)]
+    cots = gather_cotangent(held, [mixers[0][0]])
+    for h in range(1, chunks):
+        mixers.append(forward(x, halo, short_taps, skip, fwd_table, place, h, chunks, cots[0]))
 
     parts, heads = [], []
     for step in range(1, ys):
@@ -586,10 +592,11 @@
     head = head_of(own_head, head_rest, mixers)
     later = along(head, fsdp, -1)
 
-    mixed_all = [
-        around(mixers[h][0], "y", step) if step else mixers[h][0] for step in range(ys) for h in range(chunks)
-    ]
-    weight_sum = weight_grad(cots, mixed_all, chunks, grad_scale, head)
+    weight_sum = None
+    for h in range(chunks):
+        mixed_all = [around(mixers[h][0], "y", step) if step else mixers[h][0] for step in range(ys)]
+        after = later if h == chunks - 1 else mixed_own
+        weight_sum = weight_grad(cots, mixed_all, h, chunks, grad_scale, weight_sum, after)
     weight_part = lax.psum_scatter(weight_sum, "z", scatter_dimension=1, tiled=True)
 
     grads, short_parts, long_parts = [], [], []

time: 279 us -> 268 us (0.961)
  starting transfers between devices: 62.4 us -> 48.3 us
  Pallas kernels: 90 us -> 96.1 us
  waiting for transfers between devices: 94.3 us -> 90.8 us
    ppermute x2, waiting for transfers between devices: 42.8 us -> 14.8 us  [along(): lax.ppermute(block, axis, [(i, i + distance) for i in range(size) if 0 <=...]
    ppermute x5, waiting for transfers between devices: 22.7 us -> 36.9 us  [around(): lax.ppermute(block, axis, [(i, (i + distance) % size) for i in range(size)])]
    ppermute x5, starting transfers between devices: 24.6 us -> 15.8 us  [around(): lax.ppermute(block, axis, [(i, (i + distance) % size) for i in range(size)])]
    pallas_call x2 -> x3, Pallas kernels: 10.6 us -> 17.5 us  [the longest x2 12 us: weight_grad(): pl.pallas_call(functools.partial(weight_grad_kernel, scale), grid=(Z,), i...]
    ppermute x5, waiting for transfers between devices: 15.1 us -> 21.2 us  [across(): lax.ppermute(block, axis, [(i, i ^ bit) for i in range(lax.axis_size(axis...]
    ppermute x5, starting transfers between devices: 21.2 us -> 15.9 us  [across(): lax.ppermute(block, axis, [(i, i ^ bit) for i in range(lax.axis_size(axis...]
    all_gather x1, waiting for transfers between devices: 0.01 us -> 4.23 us  [body(): weights = lax.all_gather(out_weight, 'z', axis=1, tiled=True)]
  transfers between devices with their start and end apart: 17 -> 17, of which waited for: 9 -> 12; matrix products, arithmetic and copies ran while one was open for 2% -> 2% of each run, Pallas kernels for 29% -> 31%
where the time goes in v2:
time: 268 us; the launch traced here: 266 us
  Pallas kernels  96.1 us (36%)
  waiting for transfers between devices  90.8 us (34%)
  starting transfers between devices  48.3 us (18%)
  between operations  14.2 us (5%)
  local copies, waits for them, and re-layouts  11.6 us (4%)
  other arithmetic  4.95 us (2%)
    ppermute x5, waiting for transfers between devices, around(): lax.ppermute(block, axis, [(i, (i + distance) % size) for i in range(size)])  36.9 us
    ppermute x5, waiting for transfers between devices, across(): lax.ppermute(block, axis, [(i, i ^ bit) for i in range(lax.axis_size(axis...  21.2 us
    pallas_call x2, Pallas kernels, backward(): pl.pallas_call(backward_kernel, grid=(tiles,), in_specs=[tok, tok, pl.Blo...  21.1 us
    ppermute x5, starting transfers between devices, across(): lax.ppermute(block, axis, [(i, i ^ bit) for i in range(lax.axis_size(axis...  15.9 us
    ppermute x5, starting transfers between devices, around(): lax.ppermute(block, axis, [(i, (i + distance) % size) for i in range(size)])  15.8 us
    pallas_call x2, Pallas kernels, forward(): pl.pallas_call(forward_kernel, grid_spec=pltpu.PrefetchScalarGridSpec(num...  14.8 us
    ppermute x2, waiting for transfers between devices, along(): lax.ppermute(block, axis, [(i, i + distance) for i in range(size) if 0 <=...  14.8 us
    pallas_call x2, Pallas kernels, mixed_grad(): pl.pallas_call(mixed_grad_kernel, grid_spec=pltpu.PrefetchScalarGridSpec(...  14.4 us
  transfers between devices with their start and end apart: 17, of which 12 were waited for; matrix products, arithmetic and copies ran while one was open for 2% of the time, Pallas kernels for 31%

profile of v2, /device:TPU:0, one launch (start us, length us, event | category | flops | bytes accessed | tf_op | source)
XLA Modules:
  0.0 265.9 jit_solution(10494571431067798365)
XLA Ops:
  7.9 4.2 %pack.1.refs_2_ = bf16[4,3,128,1024]{3,2,1,0:T(8,128)(2,1)} custom-call(bf16[128,4096]{1,0:T(8,128)(2,1)} %refs_0_.2, bf16[128,4096]{1,0:T(8,128)(2,1)} %refs_1_.2, bf16[128,4096]{1,0:T(8,128)(2,1)} %refs_2_.1), custom_call_target="tpu_custom_call" | custom-call | tf_op jit(solution)/shard_map/pack/pallas_call | solution.py:281
  12.1 4.2 %all-to-all-start = ((bf16[4,3,128,1024]{3,2,1,0:T(8,128)(2,1)}), bf16[4,3,128,1024]{3,2,1,0:T(8,128)(2,1)S(1)}, u32[]{:S(2)}, u32[]{:S(2)}) async-start(bf16[4,3,128,1024]{3,2,1,0:T(8,128)(2,1)} %pack.1.refs_2_), calls=%async_computation | async-start | bytes 6291456 | tf_op jit(solution)/shard_map/all_to_all | solution.py:575
  16.3 3.5 %split.1 = (bf16[128,2048]{1,0:T(8,128)(2,1)}, bf16[128,2048]{1,0:T(8,128)(2,1)}) custom-call(s32[1]{0:T(128)} %bitcast.y_ref, bf16[128,4096]{1,0:T(8,128)(2,1)} %refs_1_.3, bf16[128,4096]{1,0:T(8,128)(2,1)} %refs_1_.3, bf16[4,3,128,1024]{3,2,1,0:T(8,128)(2,1)} %pack.1.refs_2_), custom_call_target="tpu_custom_call" | custom-call | tf_op jit(solution)/shard_map/split/pallas_call | solution.py:353
  22.3 12.7 %collective-permute-done = bf16[128,2048]{1,0:T(8,128)(2,1)S(1)} collective-permute-done((bf16[128,2048]{1,0:T(8,128)(2,1)}, bf16[128,2048]{1,0:T(8,128)(2,1)S(1)}, u32[]{:S(2)}, u32[]{:S(2)}) %collective-permute-start) | collective-permute-done | bytes 524320 | tf_op jit(solution)/shard_map/ppermute | solution.py:322
  42.3 6.7 %tables.1 = (bf16[8192,256]{1,0:T(8,128)(2,1)}, bf16[8192,256]{1,0:T(8,128)(2,1)}) custom-call(f32[64,256]{1,0:T(8,128)} %pad.8.fwd_ref, f32[64,256]{1,0:T(8,128)} %pad.9.bwd_ref), custom_call_target="tpu_custom_call" | custom-call | tf_op jit(solution)/shard_map/tables/pallas_call | solution.py:41
  49.0 5.2 %all-to-all-done.x_ref.before_ref = bf16[4,3,128,1024]{3,2,1,0:T(8,128)(2,1)S(1)} async-done(((bf16[4,3,128,1024]{3,2,1,0:T(8,128)(2,1)}), bf16[4,3,128,1024]{3,2,1,0:T(8,128)(2,1)S(1)}, u32[]{:S(2)}, u32[]{:S(2)}) %all-to-all-start) | async-done | bytes 3145760 | tf_op jit(solution)/shard_map/all_to_all | solution.py:575
  55.8 5.4 %tail.1 = bf16[176,1024]{1,0:T(8,128)(2,1)} custom-call(bf16[4,3,128,1024]{3,2,1,0:T(8,128)(2,1)} %copy-done, bf16[4,3,128,1024]{3,2,1,0:T(8,128)(2,1)} %copy-done, f32[3,7,1024]{2,1,0:T(8,128)} %taps_ref.9, bf16[8192,256]{1,0:T(8,128)(2,1)} %get-tuple-element.32.refs_0_.tab_ref, bf16[2,1,128,2048]{3,2,1,0:T(8,128)(2,1)} %join.2.refs_1_._.refs_0_), custom_call_target="tpu_custom_call" | custom-call | tf_op jit(solution)/shard_map/tail/pallas_call | solution.py:503
  61.2 3.9 %collective-permute-start.2 = (bf16[176,1024]{1,0:T(8,128)(2,1)}, bf16[176,1024]{1,0:T(8,128)(2,1)S(1)}, u32[]{:S(2)}, u32[]{:S(2)}) collective-permute-start(bf16[176,1024]{1,0:T(8,128)(2,1)} %tail.1), channel_id=1, source_target_pairs={{0,4},{4,8},{8,12},{12,16},{16,20},{20,24},{24,28},{1,5},{5,9},{9,... | collective-permute-start | bytes 1081352 | tf_op jit(solution)/shard_map/ppermute | solution.py:317
  65.6 6.9 %collective-permute-done.2.h_ref = bf16[176,1024]{1,0:T(8,128)(2,1)S(1)} collective-permute-done((bf16[176,1024]{1,0:T(8,128)(2,1)}, bf16[176,1024]{1,0:T(8,128)(2,1)S(1)}, u32[]{:S(2)}, u32[]{:S(2)}) %collective-permute-start.2) | collective-permute-done | bytes 360480 | tf_op jit(solution)/shard_map/ppermute | solution.py:317
  73.3 7.4 %forward.2 = (bf16[512,512]{1,0:T(8,128)(2,1)}, f32[3,512,512]{2,1,0:T(8,128)}, f32[512,512]{1,0:T(8,128)}) custom-call(s32[4]{0:T(128)} %shift-left_add_fusion.place_ref._, bf16[4,3,128,1024]{3,2,1,0:T(8,128)(2,1)} %copy-done, bf16[176,1024]{1,0:T(8,128)(2,1)} %copy-done.7, f32[3,7,1024]{2,1,0:T(8,128)} %taps_ref.9, f32[1,1024]{1,0:T(1,128)} %bitcast.17, ...), custom_call_target="tpu_custom_call" | custom-call | tf_op jit(solution)/shard_map/forward/pallas_call | solution.py:111
  80.7 3.8 %join.3.a_ref._ = bf16[2,2,128,2048]{3,2,1,0:T(8,128)(2,1)} custom-call(bf16[2,1,128,2048]{3,2,1,0:T(8,128)(2,1)} %join.2.refs_1_._.refs_0_, bf16[2,1,128,2048]{3,2,1,0:T(8,128)(2,1)} %collective-permute-done.1.refs_1_, bf16[512,512]{1,0:T(8,128)(2,1)} %get-tuple-element.33.refs_2_.refs_0_), custom_call_target="tpu_custom_call" | custom-call | tf_op jit(solution)/shard_map/join/pallas_call | solution.py:383
  84.5 4.4 %collective-permute-done.3.b_ref = bf16[2,2,128,2048]{3,2,1,0:T(8,128)(2,1)S(1)} collective-permute-done((bf16[2,2,128,2048]{3,2,1,0:T(8,128)(2,1)}, bf16[2,2,128,2048]{3,2,1,0:T(8,128)(2,1)S(1)}, u32[]{:S(2)}, u32[]{:S(2)}) %collective-permute-start.3) | collective-permute-done | bytes 2097184 | tf_op jit(solution)/shard_map/ppermute | solution.py:326
  88.8 4.2 %all-gather.2.cloned.1.call-done.w_ref = bf16[1024,2048]{1,0:T(8,128)(2,1)} async-done(((bf16[1024,512]{1,0:T(8,128)(2,1)}), bf16[1024,2048]{1,0:T(8,128)(2,1)}) %all-gather.2.cloned.1.call-update) | async-done | bytes 4194320 | tf_op jit(solution)/shard_map/all_gather | solution.py:570
  93.1 7.0 %mixed_grad.2 = (bf16[512,1024]{1,0:T(8,128)(2,1)}, bf16[144,1024]{1,0:T(8,128)(2,1)}) custom-call(s32[4]{0:T(128)} %shift-left_add_fusion.place_ref._, bf16[2,2,128,2048]{3,2,1,0:T(8,128)(2,1)} %join.3.a_ref._, bf16[2,2,128,2048]{3,2,1,0:T(8,128)(2,1)} %copy-done.1, bf16[1024,2048]{1,0:T(8,128)(2,1)} %all-gather.2.cloned.1.call-done.w_ref, ...), custom_call_target="tpu_custom_call" | custom-call | tf_op jit(solution)/shard_map/mixed_grad/pallas_call | solution.py:425
  100.1 7.4 %collective-permute-start.5 = (bf16[144,1024]{1,0:T(8,128)(2,1)}, bf16[144,1024]{1,0:T(8,128)(2,1)S(1)}, u32[]{:S(2)}, u32[]{:S(2)}) collective-permute-start(bf16[144,1024]{1,0:T(8,128)(2,1)} %get-tuple-element.39), channel_id=1, source_target_pairs={{0,4},{4,0},{1,5},{5,1},{2,6},{6,2},{3,7},{7,3},{8,12},{12,8},{9,1... | collective-permute-start | bytes 884744 | tf_op jit(solution)/shard_map/ppermute | solution.py:322
  107.6 7.4 %forward.3 = (bf16[512,512]{1,0:T(8,128)(2,1)}, f32[3,512,512]{2,1,0:T(8,128)}, f32[512,512]{1,0:T(8,128)}) custom-call(s32[4]{0:T(128)} %shift-left_add_fusion.place_ref._, bf16[4,3,128,1024]{3,2,1,0:T(8,128)(2,1)} %copy-done, bf16[176,1024]{1,0:T(8,128)(2,1)} %copy-done.7, f32[3,7,1024]{2,1,0:T(8,128)} %taps_ref.9, f32[1,1024]{1,0:T(1,128)} %bitcast.18, ...), custom_call_target="tpu_custom_call" | custom-call | tf_op jit(solution)/shard_map/forward/pallas_call | solution.py:111
  116.9 7.3 %mixed_grad.3 = (f32[512,1024]{1,0:T(8,128)}, f32[144,1024]{1,0:T(8,128)}) custom-call(s32[4]{0:T(128)} %shift-left_add_fusion.place_ref._, bf16[2,2,128,2048]{3,2,1,0:T(8,128)(2,1)} %join.3.a_ref._, bf16[2,2,128,2048]{3,2,1,0:T(8,128)(2,1)} %copy-done.1, bf16[1024,2048]{1,0:T(8,128)(2,1)} %all-gather.2.cloned.1.call-done.w_ref, ...), custom_call_target="tpu_custom_call" | custom-call | tf_op jit(solution)/shard_map/mixed_grad/pallas_call | solution.py:425
  129.8 6.0 %weight_grad.2.refs_3_ = bf16[1024,2048]{1,0:T(8,128)(2,1)} custom-call(bf16[2,2,128,2048]{3,2,1,0:T(8,128)(2,1)} %join.3.a_ref._, bf16[2,2,128,2048]{3,2,1,0:T(8,128)(2,1)} %copy-done.1, bf16[512,512]{1,0:T(8,128)(2,1)} %get-tuple-element.33.refs_2_.refs_0_, bf16[512,512]{1,0:T(8,128)(2,1)} %copy-done.9, f32[512,1024]{1,0:T(8,128)} %get-tuple-element.35.mo_ref.refs_2_), custom_call_target="tpu_custom_call" | custom-call | tf_op jit(solution)/shard_map/weight_grad/pallas_call | solution.py:470
  138.0 7.9 %collective-permute-done.6.n_ref.refs_2_ = bf16[192,1024]{1,0:T(8,128)(2,1)S(1)} collective-permute-done((bf16[192,1024]{1,0:T(8,128)(2,1)}, bf16[192,1024]{1,0:T(8,128)(2,1)S(1)}, u32[]{:S(2)}, u32[]{:S(2)}) %collective-permute-start.6) | collective-permute-done | bytes 393248 | tf_op jit(solution)/shard_map/ppermute | solution.py:317
  146.7 6.0 %weight_grad.3 = bf16[1024,2048]{1,0:T(8,128)(2,1)} custom-call(bf16[2,2,128,2048]{3,2,1,0:T(8,128)(2,1)} %join.3.a_ref._, bf16[2,2,128,2048]{3,2,1,0:T(8,128)(2,1)} %copy-done.1, bf16[512,512]{1,0:T(8,128)(2,1)} %get-tuple-element.48.refs_0_, bf16[512,512]{1,0:T(8,128)(2,1)} %copy-done.11, ...), custom_call_target="tpu_custom_call", output_to_operand_aliasing={{}: (5, {})} | custom-call | tf_op jit(solution)/shard_map/weight_grad/pallas_call | solution.py:470
  154.0 3.8 %collective-permute-start.4 = (bf16[512,1024]{1,0:T(8,128)(2,1)S(1)}, bf16[512,1024]{1,0:T(8,128)(2,1)S(1)}, u32[]{:S(2)}, u32[]{:S(2)}) collective-permute-start(bf16[512,1024]{1,0:T(8,128)(2,1)S(1)} %copy-done.8), channel_id=1, source_target_pairs={{0,4},{4,0},{1,5},{5,1},{2,6},{6,2},{3,7},{7,3},{8,12},{12,8},{9,1... | collective-permute-start | bytes 3145736 | tf_op jit(solution)/shard_map/ppermute | solution.py:322
  157.8 22.0 %collective-permute-done.4.mr_ref = bf16[512,1024]{1,0:T(8,128)(2,1)S(1)} collective-permute-done((bf16[512,1024]{1,0:T(8,128)(2,1)S(1)}, bf16[512,1024]{1,0:T(8,128)(2,1)S(1)}, u32[]{:S(2)}, u32[]{:S(2)}) %collective-permute-start.4) | collective-permute-done | bytes 1048608 | tf_op jit(solution)/shard_map/ppermute | solution.py:322
  180.8 10.5 %backward.2 = (bf16[4,3,128,512]{3,2,1,0:T(8,128)(2,1)}, f32[3,8,512]{2,1,0:T(8,128)}, f32[32,128]{1,0:T(8,128)}) custom-call(f32[512,1024]{1,0:T(8,128)} %get-tuple-element.35.mo_ref.refs_2_, bf16[512,1024]{1,0:T(8,128)(2,1)} %copy-done.4, f32[3,512,512]{2,1,0:T(8,128)} %get-tuple-element.36.refs_0_.f_ref, f32[512,512]{1,0:T(8,128)} %get-tuple-element.37.refs_1_.filt_ref, ...), custom_call_target="tpu_custom_call" | custom-call | tf_op jit(solution)/shard_map/backward/pallas_call | solution.py:236
  191.2 3.6 %all-to-all-start.1 = ((bf16[4,3,128,512]{3,2,1,0:T(8,128)(2,1)}), bf16[4,3,128,512]{3,2,1,0:T(8,128)(2,1)S(1)}, u32[]{:S(2)}, u32[]{:S(2)}) async-start(bf16[4,3,128,512]{3,2,1,0:T(8,128)(2,1)} %get-tuple-element.43), calls=%async_computation.1 | async-start | bytes 3145728 | tf_op jit(solution)/shard_map/all_to_all | solution.py:608
  194.8 10.6 %backward.3 = (bf16[4,3,128,512]{3,2,1,0:T(8,128)(2,1)}, f32[3,8,512]{2,1,0:T(8,128)}, f32[32,128]{1,0:T(8,128)}) custom-call(f32[512,1024]{1,0:T(8,128)} %get-tuple-element.35.mo_ref.refs_2_, bf16[512,1024]{1,0:T(8,128)(2,1)} %copy-done.4, f32[3,512,512]{2,1,0:T(8,128)} %get-tuple-element.40.refs_2_.f_ref, f32[512,512]{1,0:T(8,128)} %get-tuple-element.41.refs_3_.filt_ref, ...), custom_call_target="tpu_custom_call" | custom-call | tf_op jit(solution)/shard_map/backward/pallas_call | solution.py:236
  207.0 7.9 %all-to-all-done.1.refs_0_ = bf16[4,3,128,512]{3,2,1,0:T(8,128)(2,1)S(1)} async-done(((bf16[4,3,128,512]{3,2,1,0:T(8,128)(2,1)}), bf16[4,3,128,512]{3,2,1,0:T(8,128)(2,1)S(1)}, u32[]{:S(2)}, u32[]{:S(2)}) %all-to-all-start.1) | async-done | bytes 1572896 | tf_op jit(solution)/shard_map/all_to_all | solution.py:608
  214.9 3.6 %all-to-all-start.2 = ((bf16[4,3,128,512]{3,2,1,0:T(8,128)(2,1)}), bf16[4,3,128,512]{3,2,1,0:T(8,128)(2,1)S(1)}, u32[]{:S(2)}, u32[]{:S(2)}) async-start(bf16[4,3,128,512]{3,2,1,0:T(8,128)(2,1)} %get-tuple-element.44), calls=%async_computation.2 | async-start | bytes 3145728 | tf_op jit(solution)/shard_map/all_to_all | solution.py:608
  220.3 4.1 %collective-permute-done.9 = f32[32,1024]{1,0:T(8,128)S(1)} collective-permute-done((f32[32,1024]{1,0:T(8,128)S(1)}, f32[32,1024]{1,0:T(8,128)S(1)}, u32[]{:S(2)}, u32[]{:S(2)}) %collective-permute-start.9) | collective-permute-done | bytes 131104 | tf_op jit(solution)/shard_map/ppermute | solution.py:326
  224.4 9.4 %collective-permute-start.10 = (f32[32,1024]{1,0:T(8,128)S(1)}, f32[32,1024]{1,0:T(8,128)S(1)}, u32[]{:S(2)}, u32[]{:S(2)}) collective-permute-start(f32[32,1024]{1,0:T(8,128)S(1)} %fusion), channel_id=1, source_target_pairs={{0,8},{8,0},{16,24},{24,16},{1,9},{9,1},{17,25},{25,17},{2,10},{10... | collective-permute-start | bytes 393224 | tf_op jit(solution)/shard_map/ppermute | solution.py:326
  233.8 6.6 %collective-permute-done.10 = f32[32,1024]{1,0:T(8,128)S(1)} collective-permute-done((f32[32,1024]{1,0:T(8,128)S(1)}, f32[32,1024]{1,0:T(8,128)S(1)}, u32[]{:S(2)}, u32[]{:S(2)}) %collective-permute-start.10) | collective-permute-done | bytes 131104 | tf_op jit(solution)/shard_map/ppermute | solution.py:326
  243.4 6.2 %collective-permute-done.11 = f32[32,1024]{1,0:T(8,128)S(1)} collective-permute-done((f32[32,1024]{1,0:T(8,128)S(1)}, f32[32,1024]{1,0:T(8,128)S(1)}, u32[]{:S(2)}, u32[]{:S(2)}) %collective-permute-start.11) | collective-permute-done | bytes 131104 | tf_op jit(solution)/shard_map/ppermute | solution.py:326
  252.0 4.2 %unpack.1 = (bf16[128,4096]{1,0:T(8,128)(2,1)}, bf16[128,4096]{1,0:T(8,128)(2,1)}, bf16[128,4096]{1,0:T(8,128)(2,1)}) custom-call(bf16[4,3,128,512]{3,2,1,0:T(8,128)(2,1)} %copy-done.2, bf16[4,3,128,512]{3,2,1,0:T(8,128)(2,1)} %copy-done.3), custom_call_target="tpu_custom_call" | custom-call | tf_op jit(solution)/shard_map/unpack/pallas_call | solution.py:304
  (70 shorter events, 37.9 us)
Async XLA Ops:
  7.2 85.9 %all-gather.2.cloned.1.call-start = ((), (), s32[]{:S(2)}) async-start(), calls=%async_computation.4 | async-start | bytes 5242880 | tf_op jit(solution)/shard_map/all_gather | solution.py:570
  12.1 42.0 %all-to-all-start = ((bf16[4,3,128,1024]{3,2,1,0:T(8,128)(2,1)}), bf16[4,3,128,1024]{3,2,1,0:T(8,128)(2,1)S(1)}, u32[]{:S(2)}, u32[]{:S(2)}) async-start(bf16[4,3,128,1024]{3,2,1,0:T(8,128)(2,1)} %pack.1.refs_2_), calls=%async_computation | async-start | bytes 6291456 | tf_op jit(solution)/shard_map/all_to_all | solution.py:575
  16.3 239.9 %reduce-scatter.2.cloned.1.call-start = ((), (), s32[]{:S(2)}) async-start(), calls=%async_computation.5 | async-start | bytes 5242880 | tf_op jit(solution)/shard_map/reduce_scatter | solution.py:600
  16.3 24.6 %copy-start.13 = (f32[128,64]{0,1:T(8,128)S(1)}, f32[128,64]{0,1:T(8,128)}, u32[]{:S(2)}) copy-start(f32[128,64]{0,1:T(8,128)} %param.14) | copy-start | bytes 98308
  19.8 15.2 %collective-permute-start = (bf16[128,2048]{1,0:T(8,128)(2,1)}, bf16[128,2048]{1,0:T(8,128)(2,1)S(1)}, u32[]{:S(2)}, u32[]{:S(2)}) collective-permute-start(bf16[128,2048]{1,0:T(8,128)(2,1)} %get-tuple-element.31), channel_id=1, source_target_pairs={{0,4},{4,0},{1,5},{5,1},{2,6},{6,2},{3,7},{7,3},{8,12},{12,8},{9,1... | collective-permute-start | bytes 1572872 | tf_op jit(solution)/shard_map/ppermute | solution.py:322
  35.0 0.8 copy-start.10
  39.2 41.5 %collective-permute-start.1 = (bf16[2,1,128,2048]{3,2,1,0:T(8,128)(2,1)}, bf16[2,1,128,2048]{3,2,1,0:T(8,128)(2,1)}, u32[]{:S(2)}, u32[]{:S(2)}) collective-permute-start(bf16[2,1,128,2048]{3,2,1,0:T(8,128)(2,1)} %join.2.refs_1_._.refs_0_), channel_id=1, source_target_pairs={{0,2},{1,3},{2,0},{3,1},{4,6},{5,7},{6,4},{7,5},{8,10},{9,11},{10,... | collective-permute-start | bytes 3145736 | tf_op jit(solution)/shard_map/ppermute | solution.py:326
  54.1 1.6 copy-start
  61.2 11.3 %collective-permute-start.2 = (bf16[176,1024]{1,0:T(8,128)(2,1)}, bf16[176,1024]{1,0:T(8,128)(2,1)S(1)}, u32[]{:S(2)}, u32[]{:S(2)}) collective-permute-start(bf16[176,1024]{1,0:T(8,128)(2,1)} %tail.1), channel_id=1, source_target_pairs={{0,4},{4,8},{8,12},{12,16},{16,20},{20,24},{24,28},{1,5},{5,9},{9,... | collective-permute-start | bytes 1081352 | tf_op jit(solution)/shard_map/ppermute | solution.py:317
  84.5 23.1 %copy-start.6 = (bf16[512,512]{1,0:T(8,128)(2,1)S(1)}, bf16[512,512]{1,0:T(8,128)(2,1)}, u32[]{:S(2)}) copy-start(bf16[512,512]{1,0:T(8,128)(2,1)} %get-tuple-element.33.refs_2_.refs_0_) | copy-start | bytes 1572868
  84.5 4.4 %collective-permute-start.3 = (bf16[2,2,128,2048]{3,2,1,0:T(8,128)(2,1)}, bf16[2,2,128,2048]{3,2,1,0:T(8,128)(2,1)S(1)}, u32[]{:S(2)}, u32[]{:S(2)}) collective-permute-start(bf16[2,2,128,2048]{3,2,1,0:T(8,128)(2,1)} %join.3.a_ref._), channel_id=1, source_target_pairs={{0,1},{1,0},{2,3},{3,2},{4,5},{5,4},{6,7},{7,6},{8,9},{9,8},{10,11... | collective-permute-start | bytes 6291464 | tf_op jit(solution)/shard_map/ppermute | solution.py:326
  88.8 4.2 %copy-start.1 = (bf16[2,2,128,2048]{3,2,1,0:T(8,128)(2,1)}, bf16[2,2,128,2048]{3,2,1,0:T(8,128)(2,1)S(1)}, u32[]{:S(2)}) copy-start(bf16[2,2,128,2048]{3,2,1,0:T(8,128)(2,1)S(1)} %collective-permute-done.3.b_ref) | copy-start | bytes 6291460
  100.1 24.2 %collective-permute-start.5 = (bf16[144,1024]{1,0:T(8,128)(2,1)}, bf16[144,1024]{1,0:T(8,128)(2,1)S(1)}, u32[]{:S(2)}, u32[]{:S(2)}) collective-permute-start(bf16[144,1024]{1,0:T(8,128)(2,1)} %get-tuple-element.39), channel_id=1, source_target_pairs={{0,4},{4,0},{1,5},{5,1},{2,6},{6,2},{3,7},{7,3},{8,12},{12,8},{9,1... | collective-permute-start | bytes 884744 | tf_op jit(solution)/shard_map/ppermute | solution.py:322
  107.5 21.4 %collective-permute-start.8 = (bf16[512,512]{1,0:T(8,128)(2,1)S(1)}, bf16[512,512]{1,0:T(8,128)(2,1)S(1)}, u32[]{:S(2)}, u32[]{:S(2)}) collective-permute-start(bf16[512,512]{1,0:T(8,128)(2,1)S(1)} %copy-done.6), channel_id=1, source_target_pairs={{0,4},{4,0},{1,5},{5,1},{2,6},{6,2},{3,7},{7,3},{8,12},{12,8},{9,1... | collective-permute-start | bytes 1572872 | tf_op jit(solution)/shard_map/ppermute | solution.py:322
  115.0 23.0 %collective-permute-start.7 = (bf16[512,512]{1,0:T(8,128)(2,1)}, bf16[512,512]{1,0:T(8,128)(2,1)S(1)}, u32[]{:S(2)}, u32[]{:S(2)}) collective-permute-start(bf16[512,512]{1,0:T(8,128)(2,1)} %get-tuple-element.48.refs_0_), channel_id=1, source_target_pairs={{0,4},{4,0},{1,5},{5,1},{2,6},{6,2},{3,7},{7,3},{8,12},{12,8},{9,1... | collective-permute-start | bytes 1572872 | tf_op jit(solution)/shard_map/ppermute | solution.py:322
  127.7 18.3 %collective-permute-start.6 = (bf16[192,1024]{1,0:T(8,128)(2,1)}, bf16[192,1024]{1,0:T(8,128)(2,1)S(1)}, u32[]{:S(2)}, u32[]{:S(2)}) collective-permute-start(bf16[192,1024]{1,0:T(8,128)(2,1)} %head.1), channel_id=1, source_target_pairs={{4,0},{8,4},{12,8},{16,12},{20,16},{24,20},{28,24},{5,1},{9,5},{13... | collective-permute-start | bytes 1179656 | tf_op jit(solution)/shard_map/ppermute | solution.py:317
  129.0 0.8 copy-start.9
  138.0 7.9 %copy-start.11 = (bf16[512,512]{1,0:T(8,128)(2,1)}, bf16[512,512]{1,0:T(8,128)(2,1)S(1)}, u32[]{:S(2)}) copy-start(bf16[512,512]{1,0:T(8,128)(2,1)S(1)} %collective-permute-done.7.refs_1_) | copy-start | bytes 1572868
  145.9 0.8 copy-start.5
  152.7 1.2 copy-start.8
  154.0 25.8 %collective-permute-start.4 = (bf16[512,1024]{1,0:T(8,128)(2,1)S(1)}, bf16[512,1024]{1,0:T(8,128)(2,1)S(1)}, u32[]{:S(2)}, u32[]{:S(2)}) collective-permute-start(bf16[512,1024]{1,0:T(8,128)(2,1)S(1)} %copy-done.8), channel_id=1, source_target_pairs={{0,4},{4,0},{1,5},{5,1},{2,6},{6,2},{3,7},{7,3},{8,12},{12,8},{9,1... | collective-permute-start | bytes 3145736 | tf_op jit(solution)/shard_map/ppermute | solution.py:322
  179.8 1.0 copy-start.4
  191.2 23.6 %all-to-all-start.1 = ((bf16[4,3,128,512]{3,2,1,0:T(8,128)(2,1)}), bf16[4,3,128,512]{3,2,1,0:T(8,128)(2,1)S(1)}, u32[]{:S(2)}, u32[]{:S(2)}) async-start(bf16[4,3,128,512]{3,2,1,0:T(8,128)(2,1)} %get-tuple-element.43), calls=%async_computation.1 | async-start | bytes 3145728 | tf_op jit(solution)/shard_map/all_to_all | solution.py:608
  194.8 10.6 %copy-start.16 = (f32[32,128]{1,0:T(8,128)S(1)}, f32[32,128]{1,0:T(8,128)}, u32[]{:S(2)}) copy-start(f32[32,128]{1,0:T(8,128)} %get-tuple-element.51) | copy-start | bytes 49156
  194.8 11.4 %copy-start.15 = (f32[3,8,512]{2,1,0:T(8,128)S(1)}, f32[3,8,512]{2,1,0:T(8,128)}, u32[]{:S(2)}) copy-start(f32[3,8,512]{2,1,0:T(8,128)} %get-tuple-element.49) | copy-start | bytes 147460
  214.9 36.0 %copy-start.2 = (bf16[4,3,128,512]{3,2,1,0:T(8,128)(2,1)}, bf16[4,3,128,512]{3,2,1,0:T(8,128)(2,1)S(1)}, u32[]{:S(2)}) copy-start(bf16[4,3,128,512]{3,2,1,0:T(8,128)(2,1)S(1)} %all-to-all-done.1.refs_0_) | copy-start | bytes 4718596
  214.9 36.0 %all-to-all-start.2 = ((bf16[4,3,128,512]{3,2,1,0:T(8,128)(2,1)}), bf16[4,3,128,512]{3,2,1,0:T(8,128)(2,1)S(1)}, u32[]{:S(2)}, u32[]{:S(2)}) async-start(bf16[4,3,128,512]{3,2,1,0:T(8,128)(2,1)} %get-tuple-element.44), calls=%async_computation.2 | async-start | bytes 3145728 | tf_op jit(solution)/shard_map/all_to_all | solution.py:608
  218.5 5.9 %collective-permute-start.9 = (f32[32,1024]{1,0:T(8,128)S(1)}, f32[32,1024]{1,0:T(8,128)S(1)}, u32[]{:S(2)}, u32[]{:S(2)}) collective-permute-start(f32[32,1024]{1,0:T(8,128)S(1)} %pad_maximum_fusion), channel_id=1, source_target_pairs={{0,4},{4,0},{1,5},{5,1},{2,6},{6,2},{3,7},{7,3},{8,12},{12,8},{9,1... | collective-permute-start | bytes 393224 | tf_op jit(solution)/shard_map/ppermute | solution.py:326
  224.4 15.9 %collective-permute-start.10 = (f32[32,1024]{1,0:T(8,128)S(1)}, f32[32,1024]{1,0:T(8,128)S(1)}, u32[]{:S(2)}, u32[]{:S(2)}) collective-permute-start(f32[32,1024]{1,0:T(8,128)S(1)} %fusion), channel_id=1, source_target_pairs={{0,8},{8,0},{16,24},{24,16},{1,9},{9,1},{17,25},{25,17},{2,10},{10... | collective-permute-start | bytes 393224 | tf_op jit(solution)/shard_map/ppermute | solution.py:326
  240.4 9.2 %collective-permute-start.11 = (f32[32,1024]{1,0:T(8,128)S(1)}, f32[32,1024]{1,0:T(8,128)S(1)}, u32[]{:S(2)}, u32[]{:S(2)}) collective-permute-start(f32[32,1024]{1,0:T(8,128)S(1)} %add.20), channel_id=1, source_target_pairs={{0,16},{8,24},{16,0},{24,8},{1,17},{9,25},{17,1},{25,9},{2,18},{10... | collective-permute-start | bytes 393224 | tf_op jit(solution)/shard_map/ppermute | solution.py:326
  250.2 8.8 %copy-start.14 = (f32[3,8,1024]{2,1,0:T(8,128)}, f32[3,8,1024]{2,1,0:T(8,128)S(1)}, u32[]{:S(2)}) copy-start(f32[3,8,1024]{2,1,0:T(8,128)S(1)} %slice_bitcast_fusion) | copy-start | bytes 294916
  250.9 1.2 copy-start.3
  (2 other events, 1.5 us)
Sparse Core Ops, SparseCore 0:
  9.6 83.4 all-gather.1
  152.9 86.5 reduce-scatter.1

commit v3 on v2

--- a/solution.py
+++ b/solution.py
@@ -466,7 +466,7 @@
     part, tokens = mixed[0].shape
     tile = width // Z
     piece = pl.BlockSpec((steps, count, rows, tile), lambda i: (0, 0, 0, i))
-    extra = [after] + ([] if target is None else [target])
+    extra = [*after] + ([] if target is None else [target])
     return pl.pallas_call(
         functools.partial(weight_grad_kernel, scale),
         grid=(Z,),
@@ -475,7 +475,7 @@
         + [pl.BlockSpec(memory_space=pl.ANY)] * len(extra),
         out_specs=pl.BlockSpec((part, tile), lambda i: (chunk, i)),
         out_shape=jax.ShapeDtypeStruct((part * chunks, width), BF16),
-        input_output_aliases={} if target is None else {3 + len(mixed): 0},
+        input_output_aliases={} if target is None else {2 + len(mixed) + len(after): 0},
         compiler_params=params(),
         name="weight_grad",
     )(*cots, *mixed, *extra)
@@ -486,28 +486,36 @@
     rows = x_ref.shape[2]
     for i in range(3):
         out_ref[i * PAD : (i + 1) * PAD] = x_ref[0, i, rows - PAD :]
-    for i in (1, 2):
-        xf[i - 1, 0:PAD] = before_ref[0, i, rows - PAD :].astype(F32)
-        xf[i - 1, PAD:] = x_ref[0, i].astype(F32)
-    prod = features_of(taps_ref, 1, xf, 0, 0) * features_of(taps_ref, 2, xf, 1, 0)
-    out_ref[3 * PAD :] = prod.astype(BF16)
+    for tile in range(x_ref.shape[3] // LANES):
+        cols = slice(tile * LANES, (tile + 1) * LANES)
+        taps = taps_ref[:, :, cols]
+        prod = None
+        for i in (1, 2):
+            xf[tile, i - 1, 0:PAD] = before_ref[0, i, :, cols].astype(F32)
+            xf[tile, i - 1, PAD:] = x_ref[0, i, :, cols].astype(F32)
+            feature = taps[i, 0:1] * xf[tile, i - 1, PAD : PAD + rows]
+            for j in range(1, SHORT):
+                feature = feature + taps[i, j : j + 1] * xf[tile, i - 1, PAD - j : PAD - j + rows]
+            prod = feature if prod is None else prod * feature
+        out_ref[3 * PAD :, cols] = prod.astype(BF16)
 
 
 def tail_of(x, short_taps, after):
     seq, _, rows, cols = x.shape
-
-    def block(s):
-        return pl.BlockSpec((1, 3, rows, LANES), lambda c: (s, 0, 0, c))
-
+    wide = min(cols, 4 * LANES)
     out_rows = 3 * PAD + rows
     return pl.pallas_call(
         tail_kernel,
-        grid=(cols // LANES,),
-        in_specs=[block(seq - 1), block(seq - 2), pl.BlockSpec((3, SHORT, LANES), lambda c: (0, 0, c))]
+        grid=(cols // wide,),
+        in_specs=[
+            pl.BlockSpec((1, 3, rows, wide), lambda c: (seq - 1, 0, 0, c)),
+            pl.BlockSpec((1, 3, PAD, wide), lambda c: (seq - 2, 0, rows // PAD - 1, c)),
+            pl.BlockSpec((3, SHORT, wide), lambda c: (0, 0, c)),
+        ]
         + [pl.BlockSpec(memory_space=pl.ANY)] * len(after),
-        out_specs=pl.BlockSpec((out_rows, LANES), lambda c: (0, c)),
+        out_specs=pl.BlockSpec((out_rows, wide), lambda c: (0, c)),
         out_shape=jax.ShapeDtypeStruct((out_rows, cols), BF16),
-        scratch_shapes=[pltpu.VMEM((2, PAD + rows, LANES), F32)],
+        scratch_shapes=[pltpu.VMEM((wide // LANES, 2, PAD + rows, LANES), F32)],
         compiler_params=params(),
         name="tail",
     )(x, x, short_taps, *after)
@@ -575,10 +583,10 @@
     x = lax.all_to_all(by_owner, "seq", split_axis=0, concat_axis=0, tiled=True)
     held = own_cotangent(cotangent, col_part, by_owner)
     halo = along(tail_of(x, short_taps, [fwd_table, held]), fsdp, 1)
-    mixers = [forward(x, halo, short_taps, skip, fwd_table, place, 0, chunks, held)]
-    cots = gather_cotangent(held, [mixers[0][0]])
-    for h in range(1, chunks):
-        mixers.append(forward(x, halo, short_taps, skip, fwd_table, place, h, chunks, cots[0]))
+    cots = gather_cotangent(held, [])
+    mixers = [
+        forward(x, halo, short_taps, skip, fwd_table, place, h, chunks, cots[1]) for h in range(chunks)
+    ]
 
     parts, heads = [], []
     for step in range(1, ys):
@@ -595,7 +603,7 @@
     weight_sum = None
     for h in range(chunks):
         mixed_all = [around(mixers[h][0], "y", step) if step else mixers[h][0] for step in range(ys)]
-        after = later if h == chunks - 1 else mixed_own
+        after = [later, *rest] if h == chunks - 1 else [mixed_own]
         weight_sum = weight_grad(cots, mixed_all, h, chunks, grad_scale, weight_sum, after)
     weight_part = lax.psum_scatter(weight_sum, "z", scatter_dimension=1, tiled=True)
 

time: 268 us -> 273 us (1.019)
  waiting for transfers between devices: 90.8 us -> 124 us
  starting transfers between devices: 48.3 us -> 25.5 us
    ppermute x5, waiting for transfers between devices: 21.2 us -> 58.2 us  [across(): lax.ppermute(block, axis, [(i, i ^ bit) for i in range(lax.axis_size(axis...]
    ppermute x5, waiting for transfers between devices: 36.9 us -> 12.1 us  [around(): lax.ppermute(block, axis, [(i, (i + distance) % size) for i in range(size)])]
    all_gather x1, waiting for transfers between devices: 4.23 us -> 23.6 us  [body(): weights = lax.all_gather(out_weight, 'z', axis=1, tiled=True)]
    ppermute x5, starting transfers between devices: 15.9 us -> 3.98 us  [across(): lax.ppermute(block, axis, [(i, i ^ bit) for i in range(lax.axis_size(axis...]
    ppermute x5, starting transfers between devices: 15.8 us -> 6.89 us  [around(): lax.ppermute(block, axis, [(i, (i + distance) % size) for i in range(size)])]
    ppermute x2, waiting for transfers between devices: 14.8 us -> 20.4 us  [along(): lax.ppermute(block, axis, [(i, i + distance) for i in range(size) if 0 <=...]
    all_to_all x1, waiting for transfers between devices: 5.15 us -> 0.01 us  [body(): x = lax.all_to_all(by_owner, 'seq', split_axis=0, concat_axis=0, tiled=True)]
    pallas_call x1, Pallas kernels: 5.44 us -> 2.33 us  [tail_of(): pl.pallas_call(tail_kernel, grid=(cols // wide,), in_specs=[pl.BlockSpec(...]
  transfers between devices with their start and end apart: 17 -> 17, of which waited for: 12 -> 11; matrix products, arithmetic and copies ran while one was open for 2% -> 2% of each run, Pallas kernels for 31% -> 32%
where the time goes in v3:
time: 273 us; the launch traced here: 271 us
  waiting for transfers between devices  124 us (45%)
  Pallas kernels  93.5 us (34%)
  starting transfers between devices  25.5 us (9%)
  between operations  14.2 us (5%)
  local copies, waits for them, and re-layouts  9.28 us (3%)
  other arithmetic  4.95 us (2%)
    ppermute x5, waiting for transfers between devices, across(): lax.ppermute(block, axis, [(i, i ^ bit) for i in range(lax.axis_size(axis...  58.2 us
    all_gather x1, waiting for transfers between devices, body(): weights = lax.all_gather(out_weight, 'z', axis=1, tiled=True)  23.6 us
    pallas_call x2, Pallas kernels, backward(): pl.pallas_call(backward_kernel, grid=(tiles,), in_specs=[tok, tok, pl.Blo...  21.5 us
    ppermute x2, waiting for transfers between devices, along(): lax.ppermute(block, axis, [(i, i + distance) for i in range(size) if 0 <=...  20.4 us
    pallas_call x2, Pallas kernels, forward(): pl.pallas_call(forward_kernel, grid_spec=pltpu.PrefetchScalarGridSpec(num...  14.8 us
    pallas_call x2, Pallas kernels, mixed_grad(): pl.pallas_call(mixed_grad_kernel, grid_spec=pltpu.PrefetchScalarGridSpec(...  14.4 us
    ppermute x5, waiting for transfers between devices, around(): lax.ppermute(block, axis, [(i, (i + distance) % size) for i in range(size)])  12.1 us
    pallas_call x2, Pallas kernels, weight_grad(): pl.pallas_call(functools.partial(weight_grad_kernel, scale), grid=(Z,), i...  12.1 us
  transfers between devices with their start and end apart: 17, of which 11 were waited for; matrix products, arithmetic and copies ran while one was open for 2% of the time, Pallas kernels for 32%

profile of v3, /device:TPU:0, one launch (start us, length us, event | category | flops | bytes accessed | tf_op | source)
XLA Modules:
  0.0 271.3 jit_solution(13259235557836211598)
XLA Ops:
  7.9 4.2 %pack.1.refs_2_ = bf16[4,3,128,1024]{3,2,1,0:T(8,128)(2,1)} custom-call(bf16[128,4096]{1,0:T(8,128)(2,1)} %refs_0_.2, bf16[128,4096]{1,0:T(8,128)(2,1)} %refs_1_.2, bf16[128,4096]{1,0:T(8,128)(2,1)} %refs_2_.1), custom_call_target="tpu_custom_call" | custom-call | tf_op jit(solution)/shard_map/pack/pallas_call | solution.py:281
  12.1 3.4 %split.1 = (bf16[128,2048]{1,0:T(8,128)(2,1)}, bf16[128,2048]{1,0:T(8,128)(2,1)}) custom-call(s32[1]{0:T(128)} %bitcast.y_ref, bf16[128,4096]{1,0:T(8,128)(2,1)} %refs_1_.3, bf16[128,4096]{1,0:T(8,128)(2,1)} %refs_1_.3, bf16[4,3,128,1024]{3,2,1,0:T(8,128)(2,1)} %pack.1.refs_2_), custom_call_target="tpu_custom_call" | custom-call | tf_op jit(solution)/shard_map/split/pallas_call | solution.py:353
  15.5 3.0 %collective-permute-start = (bf16[128,2048]{1,0:T(8,128)(2,1)}, bf16[128,2048]{1,0:T(8,128)(2,1)S(1)}, u32[]{:S(2)}, u32[]{:S(2)}) collective-permute-start(bf16[128,2048]{1,0:T(8,128)(2,1)} %get-tuple-element.31), channel_id=1, source_target_pairs={{0,4},{4,0},{1,5},{5,1},{2,6},{6,2},{3,7},{7,3},{8,12},{12,8},{9,1... | collective-permute-start | bytes 1572872 | tf_op jit(solution)/shard_map/ppermute | solution.py:322
  18.5 12.1 %collective-permute-done = bf16[128,2048]{1,0:T(8,128)(2,1)S(1)} collective-permute-done((bf16[128,2048]{1,0:T(8,128)(2,1)}, bf16[128,2048]{1,0:T(8,128)(2,1)S(1)}, u32[]{:S(2)}, u32[]{:S(2)}) %collective-permute-start) | collective-permute-done | bytes 524320 | tf_op jit(solution)/shard_map/ppermute | solution.py:322
  31.4 3.4 %join.2.refs_0_.refs_1_ = bf16[2,1,128,2048]{3,2,1,0:T(8,128)(2,1)} custom-call(bf16[1,1,128,2048]{3,2,1,0:T(8,128)(2,1)} %bitcast.12, bf16[1,1,128,2048]{3,2,1,0:T(8,128)(2,1)} %bitcast.13), custom_call_target="tpu_custom_call" | custom-call | tf_op jit(solution)/shard_map/join/pallas_call | solution.py:383
  36.5 3.7 %all-to-all-start = ((bf16[4,3,128,1024]{3,2,1,0:T(8,128)(2,1)}), bf16[4,3,128,1024]{3,2,1,0:T(8,128)(2,1)S(1)}, u32[]{:S(2)}, u32[]{:S(2)}) async-start(bf16[4,3,128,1024]{3,2,1,0:T(8,128)(2,1)} %pack.1.refs_2_), calls=%async_computation | async-start | bytes 6291456 | tf_op jit(solution)/shard_map/all_to_all | solution.py:583
  40.3 20.9 %collective-permute-done.1.refs_1_ = bf16[2,1,128,2048]{3,2,1,0:T(8,128)(2,1)} collective-permute-done((bf16[2,1,128,2048]{3,2,1,0:T(8,128)(2,1)}, bf16[2,1,128,2048]{3,2,1,0:T(8,128)(2,1)}, u32[]{:S(2)}, u32[]{:S(2)}) %collective-permute-start.1) | collective-permute-done | bytes 1048608 | tf_op jit(solution)/shard_map/ppermute | solution.py:326
  61.2 3.8 %join.3.a_ref = bf16[2,2,128,2048]{3,2,1,0:T(8,128)(2,1)} custom-call(bf16[2,1,128,2048]{3,2,1,0:T(8,128)(2,1)} %join.2.refs_0_.refs_1_, bf16[2,1,128,2048]{3,2,1,0:T(8,128)(2,1)} %collective-permute-done.1.refs_1_), custom_call_target="tpu_custom_call" | custom-call | tf_op jit(solution)/shard_map/join/pallas_call | solution.py:383
  65.5 4.0 %collective-permute-done.2.b_ref._ = bf16[2,2,128,2048]{3,2,1,0:T(8,128)(2,1)} collective-permute-done((bf16[2,2,128,2048]{3,2,1,0:T(8,128)(2,1)}, bf16[2,2,128,2048]{3,2,1,0:T(8,128)(2,1)}, u32[]{:S(2)}, u32[]{:S(2)}) %collective-permute-start.2) | collective-permute-done | bytes 2097184 | tf_op jit(solution)/shard_map/ppermute | solution.py:326
  69.5 23.6 %all-gather.2.cloned.1.call-done.w_ref = bf16[1024,2048]{1,0:T(8,128)(2,1)} async-done(((bf16[1024,512]{1,0:T(8,128)(2,1)}), bf16[1024,2048]{1,0:T(8,128)(2,1)}) %all-gather.2.cloned.1.call-update) | async-done | bytes 4194320 | tf_op jit(solution)/shard_map/all_gather | solution.py:578
  93.1 7.0 %mixed_grad.2 = (bf16[512,1024]{1,0:T(8,128)(2,1)}, bf16[144,1024]{1,0:T(8,128)(2,1)}) custom-call(s32[4]{0:T(128)} %shift-left_add_fusion.place_ref._, bf16[2,2,128,2048]{3,2,1,0:T(8,128)(2,1)} %join.3.a_ref, bf16[2,2,128,2048]{3,2,1,0:T(8,128)(2,1)} %collective-permute-done.2.b_ref._, bf16[1024,2048]{1,0:T(8,128)(2,1)} %all-gather.2.cloned.1.call-done.w_ref, ...), custom_call_target="tpu_custom_call" | custom-call | tf_op jit(solution)/shard_map/mixed_grad/pallas_call | solution.py:425
  103.0 6.7 %tables.1 = (bf16[8192,256]{1,0:T(8,128)(2,1)}, bf16[8192,256]{1,0:T(8,128)(2,1)}) custom-call(f32[64,256]{1,0:T(8,128)} %pad.8.fwd_ref, f32[64,256]{1,0:T(8,128)} %pad.9.bwd_ref), custom_call_target="tpu_custom_call" | custom-call | tf_op jit(solution)/shard_map/tables/pallas_call | solution.py:41
  113.7 2.5 collective-permute-start.4
  116.3 16.9 %collective-permute-done.4.h_ref = bf16[176,1024]{1,0:T(8,128)(2,1)S(1)} collective-permute-done((bf16[176,1024]{1,0:T(8,128)(2,1)}, bf16[176,1024]{1,0:T(8,128)(2,1)S(1)}, u32[]{:S(2)}, u32[]{:S(2)}) %collective-permute-start.4) | collective-permute-done | bytes 360480 | tf_op jit(solution)/shard_map/ppermute | solution.py:317
  133.9 7.4 %forward.2 = (bf16[512,512]{1,0:T(8,128)(2,1)}, f32[3,512,512]{2,1,0:T(8,128)}, f32[512,512]{1,0:T(8,128)}) custom-call(s32[4]{0:T(128)} %shift-left_add_fusion.place_ref._, bf16[4,3,128,1024]{3,2,1,0:T(8,128)(2,1)} %copy-done, bf16[176,1024]{1,0:T(8,128)(2,1)} %copy-done.4, f32[3,7,1024]{2,1,0:T(8,128)} %taps_ref.9, f32[1,1024]{1,0:T(1,128)} %bitcast.17, ...), custom_call_target="tpu_custom_call" | custom-call | tf_op jit(solution)/shard_map/forward/pallas_call | solution.py:111
  141.3 2.4 collective-permute-start.8
  143.7 7.4 %forward.3 = (bf16[512,512]{1,0:T(8,128)(2,1)}, f32[3,512,512]{2,1,0:T(8,128)}, f32[512,512]{1,0:T(8,128)}) custom-call(s32[4]{0:T(128)} %shift-left_add_fusion.place_ref._, bf16[4,3,128,1024]{3,2,1,0:T(8,128)(2,1)} %copy-done, bf16[176,1024]{1,0:T(8,128)(2,1)} %copy-done.4, f32[3,7,1024]{2,1,0:T(8,128)} %taps_ref.9, f32[1,1024]{1,0:T(1,128)} %bitcast.18, ...), custom_call_target="tpu_custom_call" | custom-call | tf_op jit(solution)/shard_map/forward/pallas_call | solution.py:111
  151.1 7.4 %mixed_grad.3 = (f32[512,1024]{1,0:T(8,128)}, f32[144,1024]{1,0:T(8,128)}) custom-call(s32[4]{0:T(128)} %shift-left_add_fusion.place_ref._, bf16[2,2,128,2048]{3,2,1,0:T(8,128)(2,1)} %join.3.a_ref, bf16[2,2,128,2048]{3,2,1,0:T(8,128)(2,1)} %collective-permute-done.2.b_ref._, bf16[1024,2048]{1,0:T(8,128)(2,1)} %all-gather.2.cloned.1.call-done.w_ref, ...), custom_call_target="tpu_custom_call" | custom-call | tf_op jit(solution)/shard_map/mixed_grad/pallas_call | solution.py:425
  159.2 2.7 head.1
  164.0 6.0 %weight_grad.2.refs_4_ = bf16[1024,2048]{1,0:T(8,128)(2,1)} custom-call(bf16[2,2,128,2048]{3,2,1,0:T(8,128)(2,1)} %join.3.a_ref, bf16[2,2,128,2048]{3,2,1,0:T(8,128)(2,1)} %collective-permute-done.2.b_ref._, bf16[512,512]{1,0:T(8,128)(2,1)} %get-tuple-element.48.refs_0_, bf16[512,512]{1,0:T(8,128)(2,1)} %copy-done.6, ...), custom_call_target="tpu_custom_call" | custom-call | tf_op jit(solution)/shard_map/weight_grad/pallas_call | solution.py:470
  170.0 3.5 %collective-permute-done.6.n_ref.refs_2_ = bf16[192,1024]{1,0:T(8,128)(2,1)S(1)} collective-permute-done((bf16[192,1024]{1,0:T(8,128)(2,1)}, bf16[192,1024]{1,0:T(8,128)(2,1)S(1)}, u32[]{:S(2)}, u32[]{:S(2)}) %collective-permute-start.6) | collective-permute-done | bytes 393248 | tf_op jit(solution)/shard_map/ppermute | solution.py:317
  174.3 6.1 %weight_grad.3 = bf16[1024,2048]{1,0:T(8,128)(2,1)} custom-call(bf16[2,2,128,2048]{3,2,1,0:T(8,128)(2,1)} %join.3.a_ref, bf16[2,2,128,2048]{3,2,1,0:T(8,128)(2,1)} %collective-permute-done.2.b_ref._, bf16[512,512]{1,0:T(8,128)(2,1)} %get-tuple-element.47.refs_0_, bf16[512,512]{1,0:T(8,128)(2,1)} %copy-done.5, ...), custom_call_target="tpu_custom_call", output_to_operand_aliasing={{}: (6, {})} | custom-call | tf_op jit(solution)/shard_map/weight_grad/pallas_call | solution.py:470
  180.4 11.0 %backward.3 = (bf16[4,3,128,512]{3,2,1,0:T(8,128)(2,1)}, f32[3,8,512]{2,1,0:T(8,128)}, f32[32,128]{1,0:T(8,128)}) custom-call(f32[512,1024]{1,0:T(8,128)} %get-tuple-element.33.mo_ref.refs_2_, bf16[512,1024]{1,0:T(8,128)(2,1)} %collective-permute-done.3.mr_ref.refs_3_, f32[3,512,512]{2,1,0:T(8,128)} %get-tuple-element.39.refs_2_.f_ref, ...), custom_call_target="tpu_custom_call" | custom-call | tf_op jit(solution)/shard_map/backward/pallas_call | solution.py:236
  191.4 3.6 %all-to-all-start.2 = ((bf16[4,3,128,512]{3,2,1,0:T(8,128)(2,1)}), bf16[4,3,128,512]{3,2,1,0:T(8,128)(2,1)S(1)}, u32[]{:S(2)}, u32[]{:S(2)}) async-start(bf16[4,3,128,512]{3,2,1,0:T(8,128)(2,1)} %get-tuple-element.43), calls=%async_computation.2 | async-start | bytes 3145728 | tf_op jit(solution)/shard_map/all_to_all | solution.py:616
  195.0 10.5 %backward.2 = (bf16[4,3,128,512]{3,2,1,0:T(8,128)(2,1)}, f32[3,8,512]{2,1,0:T(8,128)}, f32[32,128]{1,0:T(8,128)}) custom-call(f32[512,1024]{1,0:T(8,128)} %get-tuple-element.33.mo_ref.refs_2_, bf16[512,1024]{1,0:T(8,128)(2,1)} %collective-permute-done.3.mr_ref.refs_3_, f32[3,512,512]{2,1,0:T(8,128)} %get-tuple-element.35.refs_0_.f_ref, ...), custom_call_target="tpu_custom_call" | custom-call | tf_op jit(solution)/shard_map/backward/pallas_call | solution.py:236
  207.0 8.0 %all-to-all-done.2.refs_1_ = bf16[4,3,128,512]{3,2,1,0:T(8,128)(2,1)S(1)} async-done(((bf16[4,3,128,512]{3,2,1,0:T(8,128)(2,1)}), bf16[4,3,128,512]{3,2,1,0:T(8,128)(2,1)S(1)}, u32[]{:S(2)}, u32[]{:S(2)}) %all-to-all-start.2) | async-done | bytes 1572896 | tf_op jit(solution)/shard_map/all_to_all | solution.py:616
  215.0 3.6 %all-to-all-start.1 = ((bf16[4,3,128,512]{3,2,1,0:T(8,128)(2,1)}), bf16[4,3,128,512]{3,2,1,0:T(8,128)(2,1)S(1)}, u32[]{:S(2)}, u32[]{:S(2)}) async-start(bf16[4,3,128,512]{3,2,1,0:T(8,128)(2,1)} %get-tuple-element.42), calls=%async_computation.1 | async-start | bytes 3145728 | tf_op jit(solution)/shard_map/all_to_all | solution.py:616
  220.4 4.2 %collective-permute-done.9 = f32[32,1024]{1,0:T(8,128)S(1)} collective-permute-done((f32[32,1024]{1,0:T(8,128)S(1)}, f32[32,1024]{1,0:T(8,128)S(1)}, u32[]{:S(2)}, u32[]{:S(2)}) %collective-permute-start.9) | collective-permute-done | bytes 131104 | tf_op jit(solution)/shard_map/ppermute | solution.py:326
  225.0 11.3 %collective-permute-done.10 = f32[32,1024]{1,0:T(8,128)S(1)} collective-permute-done((f32[32,1024]{1,0:T(8,128)S(1)}, f32[32,1024]{1,0:T(8,128)S(1)}, u32[]{:S(2)}, u32[]{:S(2)}) %collective-permute-start.10) | collective-permute-done | bytes 131104 | tf_op jit(solution)/shard_map/ppermute | solution.py:326
  236.4 17.8 %collective-permute-done.11 = f32[32,1024]{1,0:T(8,128)S(1)} collective-permute-done((f32[32,1024]{1,0:T(8,128)S(1)}, f32[32,1024]{1,0:T(8,128)S(1)}, u32[]{:S(2)}, u32[]{:S(2)}) %collective-permute-start.11) | collective-permute-done | bytes 131104 | tf_op jit(solution)/shard_map/ppermute | solution.py:326
  256.6 4.2 %unpack.1 = (bf16[128,4096]{1,0:T(8,128)(2,1)}, bf16[128,4096]{1,0:T(8,128)(2,1)}, bf16[128,4096]{1,0:T(8,128)(2,1)}) custom-call(bf16[4,3,128,512]{3,2,1,0:T(8,128)(2,1)} %copy-done.2, bf16[4,3,128,512]{3,2,1,0:T(8,128)(2,1)} %copy-done.1), custom_call_target="tpu_custom_call" | custom-call | tf_op jit(solution)/shard_map/unpack/pallas_call | solution.py:304
  261.6 2.8 %convert_element_type.7 = f32[1024,512]{1,0:T(8,128)} convert(bf16[1024,512]{1,0:T(8,128)(2,1)} %reduce-scatter.2.cloned.1.call-done) | non-fusion elementwise | flops 524288 | bytes 3145728 | tf_op jit(solution)/shard_map/convert_element_type | solution.py:635
  (64 shorter events, 22.2 us)
Async XLA Ops:
  7.2 85.9 %all-gather.2.cloned.1.call-start = ((), (), s32[]{:S(2)}) async-start(), calls=%async_computation.4 | async-start | bytes 5242880 | tf_op jit(solution)/shard_map/all_gather | solution.py:578
  15.5 15.1 %collective-permute-start = (bf16[128,2048]{1,0:T(8,128)(2,1)}, bf16[128,2048]{1,0:T(8,128)(2,1)S(1)}, u32[]{:S(2)}, u32[]{:S(2)}) collective-permute-start(bf16[128,2048]{1,0:T(8,128)(2,1)} %get-tuple-element.31), channel_id=1, source_target_pairs={{0,4},{4,0},{1,5},{5,1},{2,6},{6,2},{3,7},{7,3},{8,12},{12,8},{9,1... | collective-permute-start | bytes 1572872 | tf_op jit(solution)/shard_map/ppermute | solution.py:322
  30.6 0.8 copy-start.7
  34.8 26.4 %collective-permute-start.1 = (bf16[2,1,128,2048]{3,2,1,0:T(8,128)(2,1)}, bf16[2,1,128,2048]{3,2,1,0:T(8,128)(2,1)}, u32[]{:S(2)}, u32[]{:S(2)}) collective-permute-start(bf16[2,1,128,2048]{3,2,1,0:T(8,128)(2,1)} %join.2.refs_0_.refs_1_), channel_id=1, source_target_pairs={{0,2},{1,3},{2,0},{3,1},{4,6},{5,7},{6,4},{7,5},{8,10},{9,11},{10,... | collective-permute-start | bytes 3145736 | tf_op jit(solution)/shard_map/ppermute | solution.py:326
  36.5 73.2 %all-to-all-start = ((bf16[4,3,128,1024]{3,2,1,0:T(8,128)(2,1)}), bf16[4,3,128,1024]{3,2,1,0:T(8,128)(2,1)S(1)}, u32[]{:S(2)}, u32[]{:S(2)}) async-start(bf16[4,3,128,1024]{3,2,1,0:T(8,128)(2,1)} %pack.1.refs_2_), calls=%async_computation | async-start | bytes 6291456 | tf_op jit(solution)/shard_map/all_to_all | solution.py:583
  40.3 221.3 %reduce-scatter.2.cloned.1.call-start = ((), (), s32[]{:S(2)}) async-start(), calls=%async_computation.5 | async-start | bytes 5242880 | tf_op jit(solution)/shard_map/reduce_scatter | solution.py:608
  65.0 4.5 %collective-permute-start.2 = (bf16[2,2,128,2048]{3,2,1,0:T(8,128)(2,1)}, bf16[2,2,128,2048]{3,2,1,0:T(8,128)(2,1)}, u32[]{:S(2)}, u32[]{:S(2)}) collective-permute-start(bf16[2,2,128,2048]{3,2,1,0:T(8,128)(2,1)} %join.3.a_ref), channel_id=1, source_target_pairs={{0,1},{1,0},{2,3},{3,2},{4,5},{5,4},{6,7},{7,6},{8,9},{9,8},{10,11... | collective-permute-start | bytes 6291464 | tf_op jit(solution)/shard_map/ppermute | solution.py:326
  65.5 36.1 %copy-start.9 = (f32[128,64]{0,1:T(8,128)S(1)}, f32[128,64]{0,1:T(8,128)}, u32[]{:S(2)}) copy-start(f32[128,64]{0,1:T(8,128)} %param.14) | copy-start | bytes 98308
  100.1 73.4 %collective-permute-start.3 = (bf16[512,1024]{1,0:T(8,128)(2,1)}, bf16[512,1024]{1,0:T(8,128)(2,1)}, u32[]{:S(2)}, u32[]{:S(2)}) collective-permute-start(bf16[512,1024]{1,0:T(8,128)(2,1)} %get-tuple-element.32._), channel_id=1, source_target_pairs={{0,4},{4,0},{1,5},{5,1},{2,6},{6,2},{3,7},{7,3},{8,12},{12,8},{9,1... | collective-permute-start | bytes 3145736 | tf_op jit(solution)/shard_map/ppermute | solution.py:322
  109.7 1.6 copy-start
  111.4 4.8 %copy-start.13 = (bf16[144,1024]{1,0:T(8,128)(2,1)S(1)}, bf16[144,1024]{1,0:T(8,128)(2,1)}, u32[]{:S(2)}) copy-start(bf16[144,1024]{1,0:T(8,128)(2,1)} %get-tuple-element.38) | copy-start | bytes 884740
  113.7 19.5 %collective-permute-start.4 = (bf16[176,1024]{1,0:T(8,128)(2,1)}, bf16[176,1024]{1,0:T(8,128)(2,1)S(1)}, u32[]{:S(2)}, u32[]{:S(2)}) collective-permute-start(bf16[176,1024]{1,0:T(8,128)(2,1)} %tail.1), channel_id=1, source_target_pairs={{0,4},{4,8},{8,12},{12,16},{16,20},{20,24},{24,28},{1,5},{5,9},{9,... | collective-permute-start | bytes 1081352 | tf_op jit(solution)/shard_map/ppermute | solution.py:317
  116.2 42.3 %collective-permute-start.5 = (bf16[144,1024]{1,0:T(8,128)(2,1)S(1)}, bf16[144,1024]{1,0:T(8,128)(2,1)S(1)}, u32[]{:S(2)}, u32[]{:S(2)}) collective-permute-start(bf16[144,1024]{1,0:T(8,128)(2,1)S(1)} %copy-done.13), channel_id=1, source_target_pairs={{0,4},{4,0},{1,5},{5,1},{2,6},{6,2},{3,7},{7,3},{8,12},{12,8},{9,1... | collective-permute-start | bytes 884744 | tf_op jit(solution)/shard_map/ppermute | solution.py:322
  133.2 0.7 copy-start.4
  141.3 21.9 %collective-permute-start.8 = (bf16[512,512]{1,0:T(8,128)(2,1)}, bf16[512,512]{1,0:T(8,128)(2,1)S(1)}, u32[]{:S(2)}, u32[]{:S(2)}) collective-permute-start(bf16[512,512]{1,0:T(8,128)(2,1)} %get-tuple-element.48.refs_0_), channel_id=1, source_target_pairs={{0,4},{4,0},{1,5},{5,1},{2,6},{6,2},{3,7},{7,3},{8,12},{12,8},{9,1... | collective-permute-start | bytes 1572872 | tf_op jit(solution)/shard_map/ppermute | solution.py:322
  151.1 18.9 %collective-permute-start.7 = (bf16[512,512]{1,0:T(8,128)(2,1)}, bf16[512,512]{1,0:T(8,128)(2,1)S(1)}, u32[]{:S(2)}, u32[]{:S(2)}) collective-permute-start(bf16[512,512]{1,0:T(8,128)(2,1)} %get-tuple-element.47.refs_0_), channel_id=1, source_target_pairs={{0,4},{4,0},{1,5},{5,1},{2,6},{6,2},{3,7},{7,3},{8,12},{12,8},{9,1... | collective-permute-start | bytes 1572872 | tf_op jit(solution)/shard_map/ppermute | solution.py:322
  158.5 0.7 copy-start.8
  161.9 11.6 %collective-permute-start.6 = (bf16[192,1024]{1,0:T(8,128)(2,1)}, bf16[192,1024]{1,0:T(8,128)(2,1)S(1)}, u32[]{:S(2)}, u32[]{:S(2)}) collective-permute-start(bf16[192,1024]{1,0:T(8,128)(2,1)} %head.1), channel_id=1, source_target_pairs={{4,0},{8,4},{12,8},{16,12},{20,16},{24,20},{28,24},{5,1},{9,5},{13... | collective-permute-start | bytes 1179656 | tf_op jit(solution)/shard_map/ppermute | solution.py:317
  163.2 0.8 copy-start.6
  170.0 3.5 %copy-start.5 = (bf16[512,512]{1,0:T(8,128)(2,1)}, bf16[512,512]{1,0:T(8,128)(2,1)S(1)}, u32[]{:S(2)}) copy-start(bf16[512,512]{1,0:T(8,128)(2,1)S(1)} %collective-permute-done.7.refs_1_) | copy-start | bytes 1572868
  173.5 0.8 copy-start.3
  191.4 23.6 %all-to-all-start.2 = ((bf16[4,3,128,512]{3,2,1,0:T(8,128)(2,1)}), bf16[4,3,128,512]{3,2,1,0:T(8,128)(2,1)S(1)}, u32[]{:S(2)}, u32[]{:S(2)}) async-start(bf16[4,3,128,512]{3,2,1,0:T(8,128)(2,1)} %get-tuple-element.43), calls=%async_computation.2 | async-start | bytes 3145728 | tf_op jit(solution)/shard_map/all_to_all | solution.py:616
  195.0 10.5 %copy-start.12 = (f32[32,128]{1,0:T(8,128)S(1)}, f32[32,128]{1,0:T(8,128)}, u32[]{:S(2)}) copy-start(f32[32,128]{1,0:T(8,128)} %get-tuple-element.52) | copy-start | bytes 49156
  195.0 11.3 %copy-start.11 = (f32[3,8,512]{2,1,0:T(8,128)S(1)}, f32[3,8,512]{2,1,0:T(8,128)}, u32[]{:S(2)}) copy-start(f32[3,8,512]{2,1,0:T(8,128)} %get-tuple-element.50) | copy-start | bytes 147460
  215.0 40.5 %copy-start.1 = (bf16[4,3,128,512]{3,2,1,0:T(8,128)(2,1)}, bf16[4,3,128,512]{3,2,1,0:T(8,128)(2,1)S(1)}, u32[]{:S(2)}) copy-start(bf16[4,3,128,512]{3,2,1,0:T(8,128)(2,1)S(1)} %all-to-all-done.2.refs_1_) | copy-start | bytes 4718596
  215.0 40.4 %all-to-all-start.1 = ((bf16[4,3,128,512]{3,2,1,0:T(8,128)(2,1)}), bf16[4,3,128,512]{3,2,1,0:T(8,128)(2,1)S(1)}, u32[]{:S(2)}, u32[]{:S(2)}) async-start(bf16[4,3,128,512]{3,2,1,0:T(8,128)(2,1)} %get-tuple-element.42), calls=%async_computation.1 | async-start | bytes 3145728 | tf_op jit(solution)/shard_map/all_to_all | solution.py:616
  218.6 5.9 %collective-permute-start.9 = (f32[32,1024]{1,0:T(8,128)S(1)}, f32[32,1024]{1,0:T(8,128)S(1)}, u32[]{:S(2)}, u32[]{:S(2)}) collective-permute-start(f32[32,1024]{1,0:T(8,128)S(1)} %pad_maximum_fusion), channel_id=1, source_target_pairs={{0,4},{4,0},{1,5},{5,1},{2,6},{6,2},{3,7},{7,3},{8,12},{12,8},{9,1... | collective-permute-start | bytes 393224 | tf_op jit(solution)/shard_map/ppermute | solution.py:326
  224.5 11.7 %collective-permute-start.10 = (f32[32,1024]{1,0:T(8,128)S(1)}, f32[32,1024]{1,0:T(8,128)S(1)}, u32[]{:S(2)}, u32[]{:S(2)}) collective-permute-start(f32[32,1024]{1,0:T(8,128)S(1)} %fusion), channel_id=1, source_target_pairs={{0,8},{8,0},{16,24},{24,16},{1,9},{9,1},{17,25},{25,17},{2,10},{10... | collective-permute-start | bytes 393224 | tf_op jit(solution)/shard_map/ppermute | solution.py:326
  236.3 17.9 %collective-permute-start.11 = (f32[32,1024]{1,0:T(8,128)S(1)}, f32[32,1024]{1,0:T(8,128)S(1)}, u32[]{:S(2)}, u32[]{:S(2)}) collective-permute-start(f32[32,1024]{1,0:T(8,128)S(1)} %add.20), channel_id=1, source_target_pairs={{0,16},{8,24},{16,0},{24,8},{1,17},{9,25},{17,1},{25,9},{2,18},{10... | collective-permute-start | bytes 393224 | tf_op jit(solution)/shard_map/ppermute | solution.py:326
  254.8 9.6 %copy-start.10 = (f32[3,8,1024]{2,1,0:T(8,128)}, f32[3,8,1024]{2,1,0:T(8,128)S(1)}, u32[]{:S(2)}) copy-start(f32[3,8,1024]{2,1,0:T(8,128)S(1)} %slice_bitcast_fusion) | copy-start | bytes 294916
  255.5 1.1 copy-start.2
Sparse Core Ops, SparseCore 0:
  9.6 83.4 all-gather.1
  180.5 81.0 reduce-scatter.1

commit v4 on v3

--- a/solution.py
+++ b/solution.py
@@ -582,17 +582,18 @@
     by_owner = pack((queries, keys, values), seq)
     x = lax.all_to_all(by_owner, "seq", split_axis=0, concat_axis=0, tiled=True)
     held = own_cotangent(cotangent, col_part, by_owner)
-    halo = along(tail_of(x, short_taps, [fwd_table, held]), fsdp, 1)
-    cots = gather_cotangent(held, [])
-    mixers = [
-        forward(x, halo, short_taps, skip, fwd_table, place, h, chunks, cots[1]) for h in range(chunks)
-    ]
+    tail = tail_of(x, short_taps, [fwd_table, held])
+    halo = along(tail, fsdp, 1)
+    cots = gather_cotangent(held, [tail])
+    mixers = [forward(x, halo, short_taps, skip, fwd_table, place, 0, chunks, cots[1])]
 
     parts, heads = [], []
     for step in range(1, ys):
-        part, head = mixed_grad(cots, weights, place, step, BF16, parts[-1] if parts else place)
+        part, head = mixed_grad(cots, weights, place, step, BF16, parts[-1] if parts else mixers[0][0])
         parts.append(part)
         heads.append(around(head, "y", -step))
+    for h in range(1, chunks):
+        mixers.append(forward(x, halo, short_taps, skip, fwd_table, place, h, chunks, parts[-1]))
     mixed_own, own_head = mixed_grad(cots, weights, place, 0, F32, parts[-1])
     rest = [around(parts[step - 1], "y", -step) for step in range(1, ys)]
     mixed_rest = rest[0] if len(rest) == 1 else sum(piece.astype(F32) for piece in rest)

time: 273 us -> 279 us (1.022)
  starting transfers between devices: 25.5 us -> 36.3 us
  waiting for transfers between devices: 124 us -> 117 us
    ppermute x5, waiting for transfers between devices: 12.1 us -> 44.5 us  [around(): lax.ppermute(block, axis, [(i, (i + distance) % size) for i in range(size)])]
    all_gather x1, waiting for transfers between devices: 23.6 us -> 0.01 us  [body(): weights = lax.all_gather(out_weight, 'z', axis=1, tiled=True)]
    ppermute x2, waiting for transfers between devices: 20.4 us -> 8.4 us  [along(): lax.ppermute(block, axis, [(i, i + distance) for i in range(size) if 0 <=...]
    ppermute x5, waiting for transfers between devices: 58.2 us -> 49.8 us  [across(): lax.ppermute(block, axis, [(i, i ^ bit) for i in range(lax.axis_size(axis...]
    all_to_all x1, waiting for transfers between devices: 0.01 us -> 5.15 us  [body(): x = lax.all_to_all(by_owner, 'seq', split_axis=0, concat_axis=0, tiled=True)]
    ppermute x5, starting transfers between devices: 3.98 us -> 8.54 us  [across(): lax.ppermute(block, axis, [(i, i ^ bit) for i in range(lax.axis_size(axis...]
    ppermute x5, starting transfers between devices: 6.89 us -> 10.8 us  [around(): lax.ppermute(block, axis, [(i, (i + distance) % size) for i in range(size)])]
    unnamed x28 -> x34, local copies, waits for them, and re-layouts: 6.58 us -> 8.27 us
  transfers between devices with their start and end apart: 17 -> 17, of which waited for: 11 -> 13; matrix products, arithmetic and copies ran while one was open for 2% -> 2% of each run, Pallas kernels for 32% -> 29%
where the time goes in v4:
time: 279 us; the launch traced here: 277 us
  waiting for transfers between devices  117 us (42%)
  Pallas kernels  93.1 us (33%)
  starting transfers between devices  36.3 us (13%)
  between operations  14.2 us (5%)
  local copies, waits for them, and re-layouts  11 us (4%)
  other arithmetic  4.95 us (2%)
    ppermute x5, waiting for transfers between devices, across(): lax.ppermute(block, axis, [(i, i ^ bit) for i in range(lax.axis_size(axis...  49.8 us
    ppermute x5, waiting for transfers between devices, around(): lax.ppermute(block, axis, [(i, (i + distance) % size) for i in range(size)])  44.5 us
    pallas_call x2, Pallas kernels, backward(): pl.pallas_call(backward_kernel, grid=(tiles,), in_specs=[tok, tok, pl.Blo...  21.1 us
    pallas_call x2, Pallas kernels, forward(): pl.pallas_call(forward_kernel, grid_spec=pltpu.PrefetchScalarGridSpec(num...  14.8 us
    pallas_call x2, Pallas kernels, mixed_grad(): pl.pallas_call(mixed_grad_kernel, grid_spec=pltpu.PrefetchScalarGridSpec(...  14.5 us
    pallas_call x2, Pallas kernels, weight_grad(): pl.pallas_call(functools.partial(weight_grad_kernel, scale), grid=(Z,), i...  12 us
    ppermute x5, starting transfers between devices, around(): lax.ppermute(block, axis, [(i, (i + distance) % size) for i in range(size)])  10.8 us
    ppermute x5, starting transfers between devices, across(): lax.ppermute(block, axis, [(i, i ^ bit) for i in range(lax.axis_size(axis...  8.54 us
  transfers between devices with their start and end apart: 17, of which 13 were waited for; matrix products, arithmetic and copies ran while one was open for 2% of the time, Pallas kernels for 29%

profile of v4, /device:TPU:0, one launch (start us, length us, event | category | flops | bytes accessed | tf_op | source)
XLA Modules:
  0.0 276.9 jit_solution(2621968875482219595)
XLA Ops:
  7.9 4.2 %pack.1.refs_2_ = bf16[4,3,128,1024]{3,2,1,0:T(8,128)(2,1)} custom-call(bf16[128,4096]{1,0:T(8,128)(2,1)} %refs_0_.2, bf16[128,4096]{1,0:T(8,128)(2,1)} %refs_1_.2, bf16[128,4096]{1,0:T(8,128)(2,1)} %refs_2_.1), custom_call_target="tpu_custom_call" | custom-call | tf_op jit(solution)/shard_map/pack/pallas_call | solution.py:281
  12.1 4.2 %all-to-all-start = ((bf16[4,3,128,1024]{3,2,1,0:T(8,128)(2,1)}), bf16[4,3,128,1024]{3,2,1,0:T(8,128)(2,1)S(1)}, u32[]{:S(2)}, u32[]{:S(2)}) async-start(bf16[4,3,128,1024]{3,2,1,0:T(8,128)(2,1)} %pack.1.refs_2_), calls=%async_computation | async-start | bytes 6291456 | tf_op jit(solution)/shard_map/all_to_all | solution.py:583
  16.3 3.5 %split.1 = (bf16[128,2048]{1,0:T(8,128)(2,1)}, bf16[128,2048]{1,0:T(8,128)(2,1)}) custom-call(s32[1]{0:T(128)} %bitcast.y_ref, bf16[128,4096]{1,0:T(8,128)(2,1)} %refs_1_.3, bf16[128,4096]{1,0:T(8,128)(2,1)} %refs_1_.3, bf16[4,3,128,1024]{3,2,1,0:T(8,128)(2,1)} %pack.1.refs_2_), custom_call_target="tpu_custom_call" | custom-call | tf_op jit(solution)/shard_map/split/pallas_call | solution.py:353
  22.3 12.7 %collective-permute-done = bf16[128,2048]{1,0:T(8,128)(2,1)S(1)} collective-permute-done((bf16[128,2048]{1,0:T(8,128)(2,1)}, bf16[128,2048]{1,0:T(8,128)(2,1)S(1)}, u32[]{:S(2)}, u32[]{:S(2)}) %collective-permute-start) | collective-permute-done | bytes 524320 | tf_op jit(solution)/shard_map/ppermute | solution.py:322
  35.8 3.4 %join.2.refs_1_.refs_0_ = bf16[2,1,128,2048]{3,2,1,0:T(8,128)(2,1)} custom-call(bf16[1,1,128,2048]{3,2,1,0:T(8,128)(2,1)} %bitcast.12, bf16[1,1,128,2048]{3,2,1,0:T(8,128)(2,1)} %bitcast.13), custom_call_target="tpu_custom_call" | custom-call | tf_op jit(solution)/shard_map/join/pallas_call | solution.py:383
  42.3 6.7 %tables.1 = (bf16[8192,256]{1,0:T(8,128)(2,1)}, bf16[8192,256]{1,0:T(8,128)(2,1)}) custom-call(f32[64,256]{1,0:T(8,128)} %pad.8.fwd_ref, f32[64,256]{1,0:T(8,128)} %pad.9.bwd_ref), custom_call_target="tpu_custom_call" | custom-call | tf_op jit(solution)/shard_map/tables/pallas_call | solution.py:41
  49.0 5.2 %all-to-all-done.x_ref.before_ref = bf16[4,3,128,1024]{3,2,1,0:T(8,128)(2,1)S(1)} async-done(((bf16[4,3,128,1024]{3,2,1,0:T(8,128)(2,1)}), bf16[4,3,128,1024]{3,2,1,0:T(8,128)(2,1)S(1)}, u32[]{:S(2)}, u32[]{:S(2)}) %all-to-all-start) | async-done | bytes 3145760 | tf_op jit(solution)/shard_map/all_to_all | solution.py:583
  58.1 17.8 %collective-permute-done.1.refs_1_ = bf16[2,1,128,2048]{3,2,1,0:T(8,128)(2,1)} collective-permute-done((bf16[2,1,128,2048]{3,2,1,0:T(8,128)(2,1)}, bf16[2,1,128,2048]{3,2,1,0:T(8,128)(2,1)}, u32[]{:S(2)}, u32[]{:S(2)}) %collective-permute-start.1) | collective-permute-done | bytes 1048608 | tf_op jit(solution)/shard_map/ppermute | solution.py:326
  75.9 3.8 %join.3.a_ref = bf16[2,2,128,2048]{3,2,1,0:T(8,128)(2,1)} custom-call(bf16[2,1,128,2048]{3,2,1,0:T(8,128)(2,1)} %join.2.refs_1_.refs_0_, bf16[2,1,128,2048]{3,2,1,0:T(8,128)(2,1)} %collective-permute-done.1.refs_1_, bf16[176,1024]{1,0:T(8,128)(2,1)} %tail.1.refs_2_), custom_call_target="tpu_custom_call" | custom-call | tf_op jit(solution)/shard_map/join/pallas_call | solution.py:383
  79.6 4.3 %collective-permute-start.3 = (bf16[176,1024]{1,0:T(8,128)(2,1)S(1)}, bf16[176,1024]{1,0:T(8,128)(2,1)S(1)}, u32[]{:S(2)}, u32[]{:S(2)}) collective-permute-start(bf16[176,1024]{1,0:T(8,128)(2,1)S(1)} %copy-done.8), channel_id=1, source_target_pairs={{0,4},{4,8},{8,12},{12,16},{16,20},{20,24},{24,28},{1,5},{5,9},{9,... | collective-permute-start | bytes 1081352 | tf_op jit(solution)/shard_map/ppermute | solution.py:317
  84.4 7.8 %collective-permute-done.3.h_ref = bf16[176,1024]{1,0:T(8,128)(2,1)S(1)} collective-permute-done((bf16[176,1024]{1,0:T(8,128)(2,1)S(1)}, bf16[176,1024]{1,0:T(8,128)(2,1)S(1)}, u32[]{:S(2)}, u32[]{:S(2)}) %collective-permute-start.3) | collective-permute-done | bytes 360480 | tf_op jit(solution)/shard_map/ppermute | solution.py:317
  93.6 7.4 %forward.2 = (bf16[512,512]{1,0:T(8,128)(2,1)}, f32[3,512,512]{2,1,0:T(8,128)}, f32[512,512]{1,0:T(8,128)}) custom-call(s32[4]{0:T(128)} %shift-left_add_fusion.place_ref, bf16[4,3,128,1024]{3,2,1,0:T(8,128)(2,1)} %copy-done, bf16[176,1024]{1,0:T(8,128)(2,1)} %copy-done.7, f32[3,7,1024]{2,1,0:T(8,128)} %taps_ref.9, f32[1,1024]{1,0:T(1,128)} %bitcast.17, ...), custom_call_target="tpu_custom_call" | custom-call | tf_op jit(solution)/shard_map/forward/pallas_call | solution.py:111
  101.1 7.2 %mixed_grad.2 = (bf16[512,1024]{1,0:T(8,128)(2,1)}, bf16[144,1024]{1,0:T(8,128)(2,1)}) custom-call(s32[4]{0:T(128)} %shift-left_add_fusion.place_ref, bf16[2,2,128,2048]{3,2,1,0:T(8,128)(2,1)} %join.3.a_ref, bf16[2,2,128,2048]{3,2,1,0:T(8,128)(2,1)} %copy-done.1, bf16[1024,2048]{1,0:T(8,128)(2,1)} %all-gather.2.cloned.1.call-done.w_ref, ...), custom_call_target="tpu_custom_call" | custom-call | tf_op jit(solution)/shard_map/mixed_grad/pallas_call | solution.py:425
  108.3 6.2 %collective-permute-start.4 = (bf16[512,1024]{1,0:T(8,128)(2,1)}, bf16[512,1024]{1,0:T(8,128)(2,1)S(1)}, u32[]{:S(2)}, u32[]{:S(2)}) collective-permute-start(bf16[512,1024]{1,0:T(8,128)(2,1)} %get-tuple-element.34._), channel_id=1, source_target_pairs={{0,4},{4,0},{1,5},{5,1},{2,6},{6,2},{3,7},{7,3},{8,12},{12,8},{9,1... | collective-permute-start | bytes 3145736 | tf_op jit(solution)/shard_map/ppermute | solution.py:322
  116.5 7.4 %forward.3 = (bf16[512,512]{1,0:T(8,128)(2,1)}, f32[3,512,512]{2,1,0:T(8,128)}, f32[512,512]{1,0:T(8,128)}) custom-call(s32[4]{0:T(128)} %shift-left_add_fusion.place_ref, bf16[4,3,128,1024]{3,2,1,0:T(8,128)(2,1)} %copy-done, bf16[176,1024]{1,0:T(8,128)(2,1)} %copy-done.7, f32[3,7,1024]{2,1,0:T(8,128)} %taps_ref.9, f32[1,1024]{1,0:T(1,128)} %bitcast.18, ...), custom_call_target="tpu_custom_call" | custom-call | tf_op jit(solution)/shard_map/forward/pallas_call | solution.py:111
  123.9 7.3 %mixed_grad.3 = (f32[512,1024]{1,0:T(8,128)}, f32[144,1024]{1,0:T(8,128)}) custom-call(s32[4]{0:T(128)} %shift-left_add_fusion.place_ref, bf16[2,2,128,2048]{3,2,1,0:T(8,128)(2,1)} %join.3.a_ref, bf16[2,2,128,2048]{3,2,1,0:T(8,128)(2,1)} %copy-done.1, bf16[1024,2048]{1,0:T(8,128)(2,1)} %all-gather.2.cloned.1.call-done.w_ref, ...), custom_call_target="tpu_custom_call" | custom-call | tf_op jit(solution)/shard_map/mixed_grad/pallas_call | solution.py:425
  131.3 13.7 %collective-permute-done.5.mr_ref = bf16[144,1024]{1,0:T(8,128)(2,1)S(1)} collective-permute-done((bf16[144,1024]{1,0:T(8,128)(2,1)}, bf16[144,1024]{1,0:T(8,128)(2,1)S(1)}, u32[]{:S(2)}, u32[]{:S(2)}) %collective-permute-start.5) | collective-permute-done | bytes 294944 | tf_op jit(solution)/shard_map/ppermute | solution.py:322
  149.7 14.5 %collective-permute-done.8.refs_1_ = bf16[512,512]{1,0:T(8,128)(2,1)S(1)} collective-permute-done((bf16[512,512]{1,0:T(8,128)(2,1)S(1)}, bf16[512,512]{1,0:T(8,128)(2,1)S(1)}, u32[]{:S(2)}, u32[]{:S(2)}) %collective-permute-start.8) | collective-permute-done | bytes 524320 | tf_op jit(solution)/shard_map/ppermute | solution.py:322
  165.0 6.0 %weight_grad.2.refs_4_ = bf16[1024,2048]{1,0:T(8,128)(2,1)} custom-call(bf16[2,2,128,2048]{3,2,1,0:T(8,128)(2,1)} %join.3.a_ref, bf16[2,2,128,2048]{3,2,1,0:T(8,128)(2,1)} %copy-done.1, bf16[512,512]{1,0:T(8,128)(2,1)} %get-tuple-element.33._.refs_0_, bf16[512,512]{1,0:T(8,128)(2,1)} %copy-done.10, f32[512,1024]{1,0:T(8,128)} %get-tuple-element.35.mo_ref.refs_2_), custom_call_target="tpu_custom_call" | custom-call | tf_op jit(solution)/shard_map/weight_grad/pallas_call | solution.py:470
  171.0 3.5 %collective-permute-done.7.refs_1_ = bf16[512,512]{1,0:T(8,128)(2,1)S(1)} collective-permute-done((bf16[512,512]{1,0:T(8,128)(2,1)}, bf16[512,512]{1,0:T(8,128)(2,1)S(1)}, u32[]{:S(2)}, u32[]{:S(2)}) %collective-permute-start.7) | collective-permute-done | bytes 524320 | tf_op jit(solution)/shard_map/ppermute | solution.py:322
  176.9 6.0 %weight_grad.3 = bf16[1024,2048]{1,0:T(8,128)(2,1)} custom-call(bf16[2,2,128,2048]{3,2,1,0:T(8,128)(2,1)} %join.3.a_ref, bf16[2,2,128,2048]{3,2,1,0:T(8,128)(2,1)} %copy-done.1, bf16[512,512]{1,0:T(8,128)(2,1)} %get-tuple-element.48.refs_0_, bf16[512,512]{1,0:T(8,128)(2,1)} %copy-done.9, ...), custom_call_target="tpu_custom_call", output_to_operand_aliasing={{}: (6, {})} | custom-call | tf_op jit(solution)/shard_map/weight_grad/pallas_call | solution.py:470
  183.0 10.6 %backward.3 = (bf16[4,3,128,512]{3,2,1,0:T(8,128)(2,1)}, f32[3,8,512]{2,1,0:T(8,128)}, f32[32,128]{1,0:T(8,128)}) custom-call(f32[512,1024]{1,0:T(8,128)} %get-tuple-element.35.mo_ref.refs_2_, bf16[512,1024]{1,0:T(8,128)(2,1)} %copy-done.2, f32[3,512,512]{2,1,0:T(8,128)} %get-tuple-element.40.refs_2_.f_ref, f32[512,512]{1,0:T(8,128)} %get-tuple-element.41.refs_3_.filt_ref, ...), custom_call_target="tpu_custom_call" | custom-call | tf_op jit(solution)/shard_map/backward/pallas_call | solution.py:236
  193.6 3.6 %all-to-all-start.2 = ((bf16[4,3,128,512]{3,2,1,0:T(8,128)(2,1)}), bf16[4,3,128,512]{3,2,1,0:T(8,128)(2,1)S(1)}, u32[]{:S(2)}, u32[]{:S(2)}) async-start(bf16[4,3,128,512]{3,2,1,0:T(8,128)(2,1)} %get-tuple-element.44), calls=%async_computation.2 | async-start | bytes 3145728 | tf_op jit(solution)/shard_map/all_to_all | solution.py:617
  197.2 10.5 %backward.2 = (bf16[4,3,128,512]{3,2,1,0:T(8,128)(2,1)}, f32[3,8,512]{2,1,0:T(8,128)}, f32[32,128]{1,0:T(8,128)}) custom-call(f32[512,1024]{1,0:T(8,128)} %get-tuple-element.35.mo_ref.refs_2_, bf16[512,1024]{1,0:T(8,128)(2,1)} %copy-done.2, f32[3,512,512]{2,1,0:T(8,128)} %get-tuple-element.36.refs_0_.f_ref, f32[512,512]{1,0:T(8,128)} %get-tuple-element.37.refs_1_.filt_ref, ...), custom_call_target="tpu_custom_call" | custom-call | tf_op jit(solution)/shard_map/backward/pallas_call | solution.py:236
  209.2 8.0 %all-to-all-done.2.refs_1_ = bf16[4,3,128,512]{3,2,1,0:T(8,128)(2,1)S(1)} async-done(((bf16[4,3,128,512]{3,2,1,0:T(8,128)(2,1)}), bf16[4,3,128,512]{3,2,1,0:T(8,128)(2,1)S(1)}, u32[]{:S(2)}, u32[]{:S(2)}) %all-to-all-start.2) | async-done | bytes 1572896 | tf_op jit(solution)/shard_map/all_to_all | solution.py:617
  217.2 3.6 %all-to-all-start.1 = ((bf16[4,3,128,512]{3,2,1,0:T(8,128)(2,1)}), bf16[4,3,128,512]{3,2,1,0:T(8,128)(2,1)S(1)}, u32[]{:S(2)}, u32[]{:S(2)}) async-start(bf16[4,3,128,512]{3,2,1,0:T(8,128)(2,1)} %get-tuple-element.43), calls=%async_computation.1 | async-start | bytes 3145728 | tf_op jit(solution)/shard_map/all_to_all | solution.py:617
  222.8 4.1 %collective-permute-done.9 = f32[32,1024]{1,0:T(8,128)S(1)} collective-permute-done((f32[32,1024]{1,0:T(8,128)S(1)}, f32[32,1024]{1,0:T(8,128)S(1)}, u32[]{:S(2)}, u32[]{:S(2)}) %collective-permute-start.9) | collective-permute-done | bytes 131104 | tf_op jit(solution)/shard_map/ppermute | solution.py:326
  226.9 3.6 %collective-permute-start.10 = (f32[32,1024]{1,0:T(8,128)S(1)}, f32[32,1024]{1,0:T(8,128)S(1)}, u32[]{:S(2)}, u32[]{:S(2)}) collective-permute-start(f32[32,1024]{1,0:T(8,128)S(1)} %fusion), channel_id=1, source_target_pairs={{0,8},{8,0},{16,24},{24,16},{1,9},{9,1},{17,25},{25,17},{2,10},{10... | collective-permute-start | bytes 393224 | tf_op jit(solution)/shard_map/ppermute | solution.py:326
  230.6 9.9 %collective-permute-done.10 = f32[32,1024]{1,0:T(8,128)S(1)} collective-permute-done((f32[32,1024]{1,0:T(8,128)S(1)}, f32[32,1024]{1,0:T(8,128)S(1)}, u32[]{:S(2)}, u32[]{:S(2)}) %collective-permute-start.10) | collective-permute-done | bytes 131104 | tf_op jit(solution)/shard_map/ppermute | solution.py:326
  241.7 18.0 %collective-permute-done.11 = f32[32,1024]{1,0:T(8,128)S(1)} collective-permute-done((f32[32,1024]{1,0:T(8,128)S(1)}, f32[32,1024]{1,0:T(8,128)S(1)}, u32[]{:S(2)}, u32[]{:S(2)}) %collective-permute-start.11) | collective-permute-done | bytes 131104 | tf_op jit(solution)/shard_map/ppermute | solution.py:326
  262.2 4.2 %unpack.1 = (bf16[128,4096]{1,0:T(8,128)(2,1)}, bf16[128,4096]{1,0:T(8,128)(2,1)}, bf16[128,4096]{1,0:T(8,128)(2,1)}) custom-call(bf16[4,3,128,512]{3,2,1,0:T(8,128)(2,1)} %copy-done.4, bf16[4,3,128,512]{3,2,1,0:T(8,128)(2,1)} %copy-done.3), custom_call_target="tpu_custom_call" | custom-call | tf_op jit(solution)/shard_map/unpack/pallas_call | solution.py:304
  267.3 2.8 %convert_element_type.7 = f32[1024,512]{1,0:T(8,128)} convert(bf16[1024,512]{1,0:T(8,128)(2,1)} %reduce-scatter.2.cloned.1.call-done) | non-fusion elementwise | flops 524288 | bytes 3145728 | tf_op jit(solution)/shard_map/convert_element_type | solution.py:636
  (70 shorter events, 31.2 us)
Async XLA Ops:
  7.2 93.9 %all-gather.2.cloned.1.call-start = ((), (), s32[]{:S(2)}) async-start(), calls=%async_computation.4 | async-start | bytes 5242880 | tf_op jit(solution)/shard_map/all_gather | solution.py:578
  12.1 42.0 %all-to-all-start = ((bf16[4,3,128,1024]{3,2,1,0:T(8,128)(2,1)}), bf16[4,3,128,1024]{3,2,1,0:T(8,128)(2,1)S(1)}, u32[]{:S(2)}, u32[]{:S(2)}) async-start(bf16[4,3,128,1024]{3,2,1,0:T(8,128)(2,1)} %pack.1.refs_2_), calls=%async_computation | async-start | bytes 6291456 | tf_op jit(solution)/shard_map/all_to_all | solution.py:583
  16.3 251.0 %reduce-scatter.2.cloned.1.call-start = ((), (), s32[]{:S(2)}) async-start(), calls=%async_computation.5 | async-start | bytes 5242880 | tf_op jit(solution)/shard_map/reduce_scatter | solution.py:609
  16.3 24.6 %copy-start.13 = (f32[128,64]{0,1:T(8,128)S(1)}, f32[128,64]{0,1:T(8,128)}, u32[]{:S(2)}) copy-start(f32[128,64]{0,1:T(8,128)} %param.14) | copy-start | bytes 98308
  19.8 15.2 %collective-permute-start = (bf16[128,2048]{1,0:T(8,128)(2,1)}, bf16[128,2048]{1,0:T(8,128)(2,1)S(1)}, u32[]{:S(2)}, u32[]{:S(2)}) collective-permute-start(bf16[128,2048]{1,0:T(8,128)(2,1)} %get-tuple-element.31), channel_id=1, source_target_pairs={{0,4},{4,0},{1,5},{5,1},{2,6},{6,2},{3,7},{7,3},{8,12},{12,8},{9,1... | collective-permute-start | bytes 1572872 | tf_op jit(solution)/shard_map/ppermute | solution.py:322
  35.0 0.8 copy-start.11
  39.2 36.7 %collective-permute-start.1 = (bf16[2,1,128,2048]{3,2,1,0:T(8,128)(2,1)}, bf16[2,1,128,2048]{3,2,1,0:T(8,128)(2,1)}, u32[]{:S(2)}, u32[]{:S(2)}) collective-permute-start(bf16[2,1,128,2048]{3,2,1,0:T(8,128)(2,1)} %join.2.refs_1_.refs_0_), channel_id=1, source_target_pairs={{0,2},{1,3},{2,0},{3,1},{4,6},{5,7},{6,4},{7,5},{8,10},{9,11},{10,... | collective-permute-start | bytes 3145736 | tf_op jit(solution)/shard_map/ppermute | solution.py:326
  54.1 1.6 copy-start
  58.1 21.6 %copy-start.8 = (bf16[176,1024]{1,0:T(8,128)(2,1)S(1)}, bf16[176,1024]{1,0:T(8,128)(2,1)}, u32[]{:S(2)}) copy-start(bf16[176,1024]{1,0:T(8,128)(2,1)} %tail.1.refs_2_) | copy-start | bytes 1081348
  79.6 12.6 %collective-permute-start.2 = (bf16[2,2,128,2048]{3,2,1,0:T(8,128)(2,1)}, bf16[2,2,128,2048]{3,2,1,0:T(8,128)(2,1)S(1)}, u32[]{:S(2)}, u32[]{:S(2)}) collective-permute-start(bf16[2,2,128,2048]{3,2,1,0:T(8,128)(2,1)} %join.3.a_ref), channel_id=1, source_target_pairs={{0,1},{1,0},{2,3},{3,2},{4,5},{5,4},{6,7},{7,6},{8,9},{9,8},{10,11... | collective-permute-start | bytes 6291464 | tf_op jit(solution)/shard_map/ppermute | solution.py:326
  79.6 12.6 %collective-permute-start.3 = (bf16[176,1024]{1,0:T(8,128)(2,1)S(1)}, bf16[176,1024]{1,0:T(8,128)(2,1)S(1)}, u32[]{:S(2)}, u32[]{:S(2)}) collective-permute-start(bf16[176,1024]{1,0:T(8,128)(2,1)S(1)} %copy-done.8), channel_id=1, source_target_pairs={{0,4},{4,8},{8,12},{12,16},{16,20},{20,24},{24,28},{1,5},{5,9},{9,... | collective-permute-start | bytes 1081352 | tf_op jit(solution)/shard_map/ppermute | solution.py:317
  92.2 1.4 copy-start.1
  101.1 13.5 %copy-start.6 = (bf16[512,512]{1,0:T(8,128)(2,1)S(1)}, bf16[512,512]{1,0:T(8,128)(2,1)}, u32[]{:S(2)}) copy-start(bf16[512,512]{1,0:T(8,128)(2,1)} %get-tuple-element.33._.refs_0_) | copy-start | bytes 1572868
  108.3 66.9 %collective-permute-start.4 = (bf16[512,1024]{1,0:T(8,128)(2,1)}, bf16[512,1024]{1,0:T(8,128)(2,1)S(1)}, u32[]{:S(2)}, u32[]{:S(2)}) collective-permute-start(bf16[512,1024]{1,0:T(8,128)(2,1)} %get-tuple-element.34._), channel_id=1, source_target_pairs={{0,4},{4,0},{1,5},{5,1},{2,6},{6,2},{3,7},{7,3},{8,12},{12,8},{9,1... | collective-permute-start | bytes 3145736 | tf_op jit(solution)/shard_map/ppermute | solution.py:322
  114.5 30.5 %collective-permute-start.5 = (bf16[144,1024]{1,0:T(8,128)(2,1)}, bf16[144,1024]{1,0:T(8,128)(2,1)S(1)}, u32[]{:S(2)}, u32[]{:S(2)}) collective-permute-start(bf16[144,1024]{1,0:T(8,128)(2,1)} %get-tuple-element.39), channel_id=1, source_target_pairs={{0,4},{4,0},{1,5},{5,1},{2,6},{6,2},{3,7},{7,3},{8,12},{12,8},{9,1... | collective-permute-start | bytes 884744 | tf_op jit(solution)/shard_map/ppermute | solution.py:322
  114.5 49.7 %collective-permute-start.8 = (bf16[512,512]{1,0:T(8,128)(2,1)S(1)}, bf16[512,512]{1,0:T(8,128)(2,1)S(1)}, u32[]{:S(2)}, u32[]{:S(2)}) collective-permute-start(bf16[512,512]{1,0:T(8,128)(2,1)S(1)} %copy-done.6), channel_id=1, source_target_pairs={{0,4},{4,0},{1,5},{5,1},{2,6},{6,2},{3,7},{7,3},{8,12},{12,8},{9,1... | collective-permute-start | bytes 1572872 | tf_op jit(solution)/shard_map/ppermute | solution.py:322
  123.9 50.7 %collective-permute-start.7 = (bf16[512,512]{1,0:T(8,128)(2,1)}, bf16[512,512]{1,0:T(8,128)(2,1)S(1)}, u32[]{:S(2)}, u32[]{:S(2)}) collective-permute-start(bf16[512,512]{1,0:T(8,128)(2,1)} %get-tuple-element.48.refs_0_), channel_id=1, source_target_pairs={{0,4},{4,0},{1,5},{5,1},{2,6},{6,2},{3,7},{7,3},{8,12},{12,8},{9,1... | collective-permute-start | bytes 1572872 | tf_op jit(solution)/shard_map/ppermute | solution.py:322
  148.4 26.8 %collective-permute-start.6 = (bf16[192,1024]{1,0:T(8,128)(2,1)}, bf16[192,1024]{1,0:T(8,128)(2,1)S(1)}, u32[]{:S(2)}, u32[]{:S(2)}) collective-permute-start(bf16[192,1024]{1,0:T(8,128)(2,1)} %head.1), channel_id=1, source_target_pairs={{4,0},{8,4},{12,8},{16,12},{20,16},{24,20},{28,24},{5,1},{9,5},{13... | collective-permute-start | bytes 1179656 | tf_op jit(solution)/shard_map/ppermute | solution.py:317
  164.2 0.8 copy-start.10
  174.5 0.8 copy-start.9
  175.2 0.8 copy-start.5
  176.0 1.0 copy-start.2
  193.6 23.6 %all-to-all-start.2 = ((bf16[4,3,128,512]{3,2,1,0:T(8,128)(2,1)}), bf16[4,3,128,512]{3,2,1,0:T(8,128)(2,1)S(1)}, u32[]{:S(2)}, u32[]{:S(2)}) async-start(bf16[4,3,128,512]{3,2,1,0:T(8,128)(2,1)} %get-tuple-element.44), calls=%async_computation.2 | async-start | bytes 3145728 | tf_op jit(solution)/shard_map/all_to_all | solution.py:617
  197.1 10.5 %copy-start.16 = (f32[32,128]{1,0:T(8,128)S(1)}, f32[32,128]{1,0:T(8,128)}, u32[]{:S(2)}) copy-start(f32[32,128]{1,0:T(8,128)} %get-tuple-element.52) | copy-start | bytes 49156
  197.2 11.3 %copy-start.15 = (f32[3,8,512]{2,1,0:T(8,128)S(1)}, f32[3,8,512]{2,1,0:T(8,128)}, u32[]{:S(2)}) copy-start(f32[3,8,512]{2,1,0:T(8,128)} %get-tuple-element.50) | copy-start | bytes 147460
  217.2 43.8 %copy-start.3 = (bf16[4,3,128,512]{3,2,1,0:T(8,128)(2,1)}, bf16[4,3,128,512]{3,2,1,0:T(8,128)(2,1)S(1)}, u32[]{:S(2)}) copy-start(bf16[4,3,128,512]{3,2,1,0:T(8,128)(2,1)S(1)} %all-to-all-done.2.refs_1_) | copy-start | bytes 4718596
  217.2 43.8 %all-to-all-start.1 = ((bf16[4,3,128,512]{3,2,1,0:T(8,128)(2,1)}), bf16[4,3,128,512]{3,2,1,0:T(8,128)(2,1)S(1)}, u32[]{:S(2)}, u32[]{:S(2)}) async-start(bf16[4,3,128,512]{3,2,1,0:T(8,128)(2,1)} %get-tuple-element.43), calls=%async_computation.1 | async-start | bytes 3145728 | tf_op jit(solution)/shard_map/all_to_all | solution.py:617
  220.8 6.1 %collective-permute-start.9 = (f32[32,1024]{1,0:T(8,128)S(1)}, f32[32,1024]{1,0:T(8,128)S(1)}, u32[]{:S(2)}, u32[]{:S(2)}) collective-permute-start(f32[32,1024]{1,0:T(8,128)S(1)} %pad_maximum_fusion), channel_id=1, source_target_pairs={{0,4},{4,0},{1,5},{5,1},{2,6},{6,2},{3,7},{7,3},{8,12},{12,8},{9,1... | collective-permute-start | bytes 393224 | tf_op jit(solution)/shard_map/ppermute | solution.py:326
  226.9 13.5 %collective-permute-start.10 = (f32[32,1024]{1,0:T(8,128)S(1)}, f32[32,1024]{1,0:T(8,128)S(1)}, u32[]{:S(2)}, u32[]{:S(2)}) collective-permute-start(f32[32,1024]{1,0:T(8,128)S(1)} %fusion), channel_id=1, source_target_pairs={{0,8},{8,0},{16,24},{24,16},{1,9},{9,1},{17,25},{25,17},{2,10},{10... | collective-permute-start | bytes 393224 | tf_op jit(solution)/shard_map/ppermute | solution.py:326
  240.4 19.3 %collective-permute-start.11 = (f32[32,1024]{1,0:T(8,128)S(1)}, f32[32,1024]{1,0:T(8,128)S(1)}, u32[]{:S(2)}, u32[]{:S(2)}) collective-permute-start(f32[32,1024]{1,0:T(8,128)S(1)} %add.20), channel_id=1, source_target_pairs={{0,16},{8,24},{16,0},{24,8},{1,17},{9,25},{17,1},{25,9},{2,18},{10... | collective-permute-start | bytes 393224 | tf_op jit(solution)/shard_map/ppermute | solution.py:326
  260.4 9.7 %copy-start.14 = (f32[3,8,1024]{2,1,0:T(8,128)}, f32[3,8,1024]{2,1,0:T(8,128)S(1)}, u32[]{:S(2)}) copy-start(f32[3,8,1024]{2,1,0:T(8,128)S(1)} %slice_bitcast_fusion) | copy-start | bytes 294916
  261.0 1.1 copy-start.4
  (2 other events, 1.5 us)
Sparse Core Ops, SparseCore 0:
  9.6 83.4 all-gather.1
  183.1 84.1 reduce-scatter.1

commit v5 on v4

--- a/solution.py
+++ b/solution.py
@@ -405,7 +405,8 @@
     return held, across(held, "seq", bits[0])
 
 
-def mixed_grad_kernel(place_ref, a_ref, b_ref, w_ref, _, out_ref, head_ref, found):
+def mixed_grad_kernel(place_ref, a_ref, b_ref, w_ref, _, out_ref, head_ref, *refs):
+    found = refs[-1]
     _, count, rows, _ = a_ref.shape
     tokens = count * rows
     pieces = jnp.concatenate([ref[...].reshape(tokens, -1) for ref in (a_ref, b_ref)], axis=0)
@@ -416,7 +417,7 @@
     head_ref[...] = out_ref[0 : LTAPS + PAD]
 
 
-def mixed_grad(cots, weights, place, step, dtype, after):
+def mixed_grad(cots, weights, place, step, dtype, after, passed=False):
     _, count, rows, width = cots[0].shape
     tokens = 2 * count * rows
     cols = weights.shape[0]
@@ -436,13 +437,16 @@
             out_specs=[
                 pl.BlockSpec((tokens, tile), lambda i, _: (0, i)),
                 pl.BlockSpec((LTAPS + PAD, tile), lambda i, _: (0, i)),
-            ],
+            ]
+            + [pl.BlockSpec(memory_space=pl.ANY)] * passed,
             scratch_shapes=[pltpu.VMEM((tokens, tile), F32)],
         ),
+        input_output_aliases={4: 2} if passed else {},
         out_shape=[
             jax.ShapeDtypeStruct((tokens, cols), dtype),
             jax.ShapeDtypeStruct((LTAPS + PAD, cols), dtype),
-        ],
+        ]
+        + [jax.ShapeDtypeStruct(after.shape, after.dtype)] * passed,
         compiler_params=params(),
         name="mixed_grad",
     )(place, *cots, weights, after)
@@ -584,17 +588,18 @@
     held = own_cotangent(cotangent, col_part, by_owner)
     tail = tail_of(x, short_taps, [fwd_table, held])
     halo = along(tail, fsdp, 1)
-    cots = gather_cotangent(held, [tail])
-    mixers = [forward(x, halo, short_taps, skip, fwd_table, place, 0, chunks, cots[1])]
+    cots = gather_cotangent(held, [halo])
+    mixers = []
+    for h in range(chunks):
+        after = mixers[-1][0] if mixers else cots[0]
+        mixers.append(forward(x, halo, short_taps, skip, fwd_table, place, h, chunks, after))
 
     parts, heads = [], []
     for step in range(1, ys):
-        part, head = mixed_grad(cots, weights, place, step, BF16, parts[-1] if parts else mixers[0][0])
+        part, head = mixed_grad(cots, weights, place, step, BF16, parts[-1] if parts else mixers[-1][0])
         parts.append(part)
         heads.append(around(head, "y", -step))
-    for h in range(1, chunks):
-        mixers.append(forward(x, halo, short_taps, skip, fwd_table, place, h, chunks, parts[-1]))
-    mixed_own, own_head = mixed_grad(cots, weights, place, 0, F32, parts[-1])
+    mixed_own, own_head, parts[-1] = mixed_grad(cots, weights, place, 0, F32, parts[-1], True)
     rest = [around(parts[step - 1], "y", -step) for step in range(1, ys)]
     mixed_rest = rest[0] if len(rest) == 1 else sum(piece.astype(F32) for piece in rest)
     head_rest = heads[0] if len(heads) == 1 else sum(piece.astype(F32) for piece in heads)
@@ -604,7 +609,7 @@
     weight_sum = None
     for h in range(chunks):
         mixed_all = [around(mixers[h][0], "y", step) if step else mixers[h][0] for step in range(ys)]
-        after = [later, *rest] if h == chunks - 1 else [mixed_own]
+        after = [later] if h == chunks - 1 else [head]
         weight_sum = weight_grad(cots, mixed_all, h, chunks, grad_scale, weight_sum, after)
     weight_part = lax.psum_scatter(weight_sum, "z", scatter_dimension=1, tiled=True)
 

time: 279 us -> 269 us (0.964)
  waiting for transfers between devices: 117 us -> 99.4 us
  starting transfers between devices: 36.3 us -> 42.7 us
    ppermute x5, waiting for transfers between devices: 49.8 us -> 32 us  [across(): lax.ppermute(block, axis, [(i, i ^ bit) for i in range(lax.axis_size(axis...]
    ppermute x5, waiting for transfers between devices: 44.5 us -> 52.9 us  [around(): lax.ppermute(block, axis, [(i, (i + distance) % size) for i in range(size)])]
    ppermute x2, waiting for transfers between devices: 8.4 us -> 0.74 us  [along(): lax.ppermute(block, axis, [(i, i + distance) for i in range(size) if 0 <=...]
    ppermute x5, starting transfers between devices: 8.54 us -> 15.3 us  [across(): lax.ppermute(block, axis, [(i, i ^ bit) for i in range(lax.axis_size(axis...]
    unnamed x34 -> x36, local copies, waits for them, and re-layouts: 8.27 us -> 10.2 us
  transfers between devices with their start and end apart: 17 -> 17, of which waited for: 13 -> 11; matrix products, arithmetic and copies ran while one was open for 2% -> 2% of each run, Pallas kernels for 29% -> 30%
where the time goes in v5:
time: 269 us; the launch traced here: 267 us
  waiting for transfers between devices  99.4 us (37%)
  Pallas kernels  93.1 us (35%)
  starting transfers between devices  42.7 us (16%)
  between operations  14.2 us (5%)
  local copies, waits for them, and re-layouts  12.9 us (5%)
  other arithmetic  4.95 us (2%)
    ppermute x5, waiting for transfers between devices, around(): lax.ppermute(block, axis, [(i, (i + distance) % size) for i in range(size)])  52.9 us
    ppermute x5, waiting for transfers between devices, across(): lax.ppermute(block, axis, [(i, i ^ bit) for i in range(lax.axis_size(axis...  32 us
    pallas_call x2, Pallas kernels, backward(): pl.pallas_call(backward_kernel, grid=(tiles,), in_specs=[tok, tok, pl.Blo...  21.1 us
    ppermute x5, starting transfers between devices, across(): lax.ppermute(block, axis, [(i, i ^ bit) for i in range(lax.axis_size(axis...  15.3 us
    pallas_call x2, Pallas kernels, forward(): pl.pallas_call(forward_kernel, grid_spec=pltpu.PrefetchScalarGridSpec(num...  14.8 us
    pallas_call x2, Pallas kernels, mixed_grad(): pl.pallas_call(mixed_grad_kernel, grid_spec=pltpu.PrefetchScalarGridSpec(...  14.5 us
    pallas_call x2, Pallas kernels, weight_grad(): pl.pallas_call(functools.partial(weight_grad_kernel, scale), grid=(Z,), i...  12.1 us
    ppermute x5, starting transfers between devices, around(): lax.ppermute(block, axis, [(i, (i + distance) % size) for i in range(size)])  10.9 us
  transfers between devices with their start and end apart: 17, of which 11 were waited for; matrix products, arithmetic and copies ran while one was open for 2% of the time, Pallas kernels for 30%

profile of v5, /device:TPU:0, one launch (start us, length us, event | category | flops | bytes accessed | tf_op | source)
XLA Modules:
  0.0 267.3 jit_solution(5200919263706937603)
XLA Ops:
  7.9 4.2 %pack.1.refs_2_ = bf16[4,3,128,1024]{3,2,1,0:T(8,128)(2,1)} custom-call(bf16[128,4096]{1,0:T(8,128)(2,1)} %refs_0_.2, bf16[128,4096]{1,0:T(8,128)(2,1)} %refs_1_.2, bf16[128,4096]{1,0:T(8,128)(2,1)} %refs_2_.1), custom_call_target="tpu_custom_call" | custom-call | tf_op jit(solution)/shard_map/pack/pallas_call | solution.py:281
  12.1 4.2 %all-to-all-start = ((bf16[4,3,128,1024]{3,2,1,0:T(8,128)(2,1)}), bf16[4,3,128,1024]{3,2,1,0:T(8,128)(2,1)S(1)}, u32[]{:S(2)}, u32[]{:S(2)}) async-start(bf16[4,3,128,1024]{3,2,1,0:T(8,128)(2,1)} %pack.1.refs_2_), calls=%async_computation | async-start | bytes 6291456 | tf_op jit(solution)/shard_map/all_to_all | solution.py:587
  16.3 3.5 %split.1 = (bf16[128,2048]{1,0:T(8,128)(2,1)}, bf16[128,2048]{1,0:T(8,128)(2,1)}) custom-call(s32[1]{0:T(128)} %bitcast.y_ref, bf16[128,4096]{1,0:T(8,128)(2,1)} %refs_1_.3, bf16[128,4096]{1,0:T(8,128)(2,1)} %refs_1_.3, bf16[4,3,128,1024]{3,2,1,0:T(8,128)(2,1)} %pack.1.refs_2_), custom_call_target="tpu_custom_call" | custom-call | tf_op jit(solution)/shard_map/split/pallas_call | solution.py:353
  22.3 12.7 %collective-permute-done = bf16[128,2048]{1,0:T(8,128)(2,1)S(1)} collective-permute-done((bf16[128,2048]{1,0:T(8,128)(2,1)}, bf16[128,2048]{1,0:T(8,128)(2,1)S(1)}, u32[]{:S(2)}, u32[]{:S(2)}) %collective-permute-start) | collective-permute-done | bytes 524320 | tf_op jit(solution)/shard_map/ppermute | solution.py:322
  35.8 3.4 %join.2.refs_1_.refs_0_ = bf16[2,1,128,2048]{3,2,1,0:T(8,128)(2,1)} custom-call(bf16[1,1,128,2048]{3,2,1,0:T(8,128)(2,1)} %bitcast.12, bf16[1,1,128,2048]{3,2,1,0:T(8,128)(2,1)} %bitcast.13), custom_call_target="tpu_custom_call" | custom-call | tf_op jit(solution)/shard_map/join/pallas_call | solution.py:383
  42.3 6.7 %tables.1 = (bf16[8192,256]{1,0:T(8,128)(2,1)}, bf16[8192,256]{1,0:T(8,128)(2,1)}) custom-call(f32[64,256]{1,0:T(8,128)} %pad.8.fwd_ref, f32[64,256]{1,0:T(8,128)} %pad.9.bwd_ref), custom_call_target="tpu_custom_call" | custom-call | tf_op jit(solution)/shard_map/tables/pallas_call | solution.py:41
  49.0 5.1 %all-to-all-done.x_ref.before_ref = bf16[4,3,128,1024]{3,2,1,0:T(8,128)(2,1)S(1)} async-done(((bf16[4,3,128,1024]{3,2,1,0:T(8,128)(2,1)}), bf16[4,3,128,1024]{3,2,1,0:T(8,128)(2,1)S(1)}, u32[]{:S(2)}, u32[]{:S(2)}) %all-to-all-start) | async-done | bytes 3145760 | tf_op jit(solution)/shard_map/all_to_all | solution.py:587
  58.0 3.9 %collective-permute-start.2 = (bf16[176,1024]{1,0:T(8,128)(2,1)}, bf16[176,1024]{1,0:T(8,128)(2,1)S(1)}, u32[]{:S(2)}, u32[]{:S(2)}) collective-permute-start(bf16[176,1024]{1,0:T(8,128)(2,1)} %tail.1), channel_id=1, source_target_pairs={{0,4},{4,8},{8,12},{12,16},{16,20},{20,24},{24,28},{1,5},{5,9},{9,... | collective-permute-start | bytes 1081352 | tf_op jit(solution)/shard_map/ppermute | solution.py:317
  62.0 13.9 %collective-permute-done.1.refs_1_ = bf16[2,1,128,2048]{3,2,1,0:T(8,128)(2,1)} collective-permute-done((bf16[2,1,128,2048]{3,2,1,0:T(8,128)(2,1)}, bf16[2,1,128,2048]{3,2,1,0:T(8,128)(2,1)}, u32[]{:S(2)}, u32[]{:S(2)}) %collective-permute-start.1) | collective-permute-done | bytes 1048608 | tf_op jit(solution)/shard_map/ppermute | solution.py:326
  76.6 3.8 %join.3._.a_ref = bf16[2,2,128,2048]{3,2,1,0:T(8,128)(2,1)} custom-call(bf16[2,1,128,2048]{3,2,1,0:T(8,128)(2,1)} %join.2.refs_1_.refs_0_, bf16[2,1,128,2048]{3,2,1,0:T(8,128)(2,1)} %collective-permute-done.1.refs_1_, bf16[176,1024]{1,0:T(8,128)(2,1)} %copy-done.6), custom_call_target="tpu_custom_call" | custom-call | tf_op jit(solution)/shard_map/join/pallas_call | solution.py:383
  80.9 7.4 %forward.2 = (bf16[512,512]{1,0:T(8,128)(2,1)}, f32[3,512,512]{2,1,0:T(8,128)}, f32[512,512]{1,0:T(8,128)}) custom-call(s32[4]{0:T(128)} %shift-left_add_fusion.place_ref, bf16[4,3,128,1024]{3,2,1,0:T(8,128)(2,1)} %copy-done, bf16[176,1024]{1,0:T(8,128)(2,1)} %copy-done.6, f32[3,7,1024]{2,1,0:T(8,128)} %taps_ref.9, f32[1,1024]{1,0:T(1,128)} %bitcast.17, ...), custom_call_target="tpu_custom_call" | custom-call | tf_op jit(solution)/shard_map/forward/pallas_call | solution.py:111
  88.3 7.4 %forward.3 = (bf16[512,512]{1,0:T(8,128)(2,1)}, f32[3,512,512]{2,1,0:T(8,128)}, f32[512,512]{1,0:T(8,128)}) custom-call(s32[4]{0:T(128)} %shift-left_add_fusion.place_ref, bf16[4,3,128,1024]{3,2,1,0:T(8,128)(2,1)} %copy-done, bf16[176,1024]{1,0:T(8,128)(2,1)} %copy-done.6, f32[3,7,1024]{2,1,0:T(8,128)} %taps_ref.9, f32[1,1024]{1,0:T(1,128)} %bitcast.18, ...), custom_call_target="tpu_custom_call" | custom-call | tf_op jit(solution)/shard_map/forward/pallas_call | solution.py:111
  97.1 7.2 %mixed_grad.2 = (bf16[512,1024]{1,0:T(8,128)(2,1)}, bf16[144,1024]{1,0:T(8,128)(2,1)}) custom-call(s32[4]{0:T(128)} %shift-left_add_fusion.place_ref, bf16[2,2,128,2048]{3,2,1,0:T(8,128)(2,1)} %join.3._.a_ref, bf16[2,2,128,2048]{3,2,1,0:T(8,128)(2,1)} %copy-done.1, bf16[1024,2048]{1,0:T(8,128)(2,1)} %all-gather.2.cloned.1.call-done.w_ref, ...), custom_call_target="tpu_custom_call" | custom-call | tf_op jit(solution)/shard_map/mixed_grad/pallas_call | solution.py:426
  104.3 3.8 %collective-permute-start.5 = (bf16[144,1024]{1,0:T(8,128)(2,1)}, bf16[144,1024]{1,0:T(8,128)(2,1)S(1)}, u32[]{:S(2)}, u32[]{:S(2)}) collective-permute-start(bf16[144,1024]{1,0:T(8,128)(2,1)} %get-tuple-element.42), channel_id=1, source_target_pairs={{0,4},{4,0},{1,5},{5,1},{2,6},{6,2},{3,7},{7,3},{8,12},{12,8},{9,1... | collective-permute-start | bytes 884744 | tf_op jit(solution)/shard_map/ppermute | solution.py:322
  110.1 7.4 %mixed_grad.3 = (f32[512,1024]{1,0:T(8,128)}, f32[144,1024]{1,0:T(8,128)}, bf16[512,1024]{1,0:T(8,128)(2,1)}) custom-call(s32[4]{0:T(128)} %shift-left_add_fusion.place_ref, bf16[2,2,128,2048]{3,2,1,0:T(8,128)(2,1)} %join.3._.a_ref, bf16[2,2,128,2048]{3,2,1,0:T(8,128)(2,1)} %copy-done.1, ...), custom_call_target="tpu_custom_call", output_to_operand_aliasing={{2}: (4, {})} | custom-call | tf_op jit(solution)/shard_map/mixed_grad/pallas_call | solution.py:426
  122.2 5.2 %collective-permute-done.8.refs_1_ = bf16[512,512]{1,0:T(8,128)(2,1)S(1)} collective-permute-done((bf16[512,512]{1,0:T(8,128)(2,1)S(1)}, bf16[512,512]{1,0:T(8,128)(2,1)S(1)}, u32[]{:S(2)}, u32[]{:S(2)}) %collective-permute-start.8) | collective-permute-done | bytes 524320 | tf_op jit(solution)/shard_map/ppermute | solution.py:322
  128.2 6.0 %weight_grad.2.refs_3_ = bf16[1024,2048]{1,0:T(8,128)(2,1)} custom-call(bf16[2,2,128,2048]{3,2,1,0:T(8,128)(2,1)} %join.3._.a_ref, bf16[2,2,128,2048]{3,2,1,0:T(8,128)(2,1)} %copy-done.1, bf16[512,512]{1,0:T(8,128)(2,1)} %get-tuple-element.34._.refs_0_, bf16[512,512]{1,0:T(8,128)(2,1)} %copy-done.10, bf16[192,1024]{1,0:T(8,128)(2,1)} %head.1.refs_2_), custom_call_target="tpu_custom_call" | custom-call | tf_op jit(solution)/shard_map/weight_grad/pallas_call | solution.py:474
  134.2 11.9 %collective-permute-done.7.refs_1_ = bf16[512,512]{1,0:T(8,128)(2,1)S(1)} collective-permute-done((bf16[512,512]{1,0:T(8,128)(2,1)S(1)}, bf16[512,512]{1,0:T(8,128)(2,1)S(1)}, u32[]{:S(2)}, u32[]{:S(2)}) %collective-permute-start.7) | collective-permute-done | bytes 524320 | tf_op jit(solution)/shard_map/ppermute | solution.py:322
  147.7 6.1 %weight_grad.3 = bf16[1024,2048]{1,0:T(8,128)(2,1)} custom-call(bf16[2,2,128,2048]{3,2,1,0:T(8,128)(2,1)} %join.3._.a_ref, bf16[2,2,128,2048]{3,2,1,0:T(8,128)(2,1)} %copy-done.1, bf16[512,512]{1,0:T(8,128)(2,1)} %get-tuple-element.35._.refs_0_, bf16[512,512]{1,0:T(8,128)(2,1)} %copy-done.12, ...), custom_call_target="tpu_custom_call", output_to_operand_aliasing={{}: (5, {})} | custom-call | tf_op jit(solution)/shard_map/weight_grad/pallas_call | solution.py:474
  157.5 23.1 %collective-permute-done.4.mr_ref = bf16[512,1024]{1,0:T(8,128)(2,1)S(1)} collective-permute-done((bf16[512,1024]{1,0:T(8,128)(2,1)S(1)}, bf16[512,1024]{1,0:T(8,128)(2,1)S(1)}, u32[]{:S(2)}, u32[]{:S(2)}) %collective-permute-start.4) | collective-permute-done | bytes 1048608 | tf_op jit(solution)/shard_map/ppermute | solution.py:322
  181.5 10.6 %backward.3 = (bf16[4,3,128,512]{3,2,1,0:T(8,128)(2,1)}, f32[3,8,512]{2,1,0:T(8,128)}, f32[32,128]{1,0:T(8,128)}) custom-call(f32[512,1024]{1,0:T(8,128)} %get-tuple-element.37.mo_ref, bf16[512,1024]{1,0:T(8,128)(2,1)} %copy-done.4, f32[3,512,512]{2,1,0:T(8,128)} %get-tuple-element.43.refs_2_.f_ref, f32[512,512]{1,0:T(8,128)} %get-tuple-element.44.refs_3_.filt_ref, ...), custom_call_target="tpu_custom_call" | custom-call | tf_op jit(solution)/shard_map/backward/pallas_call | solution.py:236
  192.1 3.6 %all-to-all-start.2 = ((bf16[4,3,128,512]{3,2,1,0:T(8,128)(2,1)}), bf16[4,3,128,512]{3,2,1,0:T(8,128)(2,1)S(1)}, u32[]{:S(2)}, u32[]{:S(2)}) async-start(bf16[4,3,128,512]{3,2,1,0:T(8,128)(2,1)} %get-tuple-element.47), calls=%async_computation.2 | async-start | bytes 3145728 | tf_op jit(solution)/shard_map/all_to_all | solution.py:622
  195.7 10.5 %backward.2 = (bf16[4,3,128,512]{3,2,1,0:T(8,128)(2,1)}, f32[3,8,512]{2,1,0:T(8,128)}, f32[32,128]{1,0:T(8,128)}) custom-call(f32[512,1024]{1,0:T(8,128)} %get-tuple-element.37.mo_ref, bf16[512,1024]{1,0:T(8,128)(2,1)} %copy-done.4, f32[3,512,512]{2,1,0:T(8,128)} %get-tuple-element.39.refs_0_.f_ref, f32[512,512]{1,0:T(8,128)} %get-tuple-element.40.refs_1_.filt_ref, ...), custom_call_target="tpu_custom_call" | custom-call | tf_op jit(solution)/shard_map/backward/pallas_call | solution.py:236
  207.8 8.0 %all-to-all-done.2.refs_1_ = bf16[4,3,128,512]{3,2,1,0:T(8,128)(2,1)S(1)} async-done(((bf16[4,3,128,512]{3,2,1,0:T(8,128)(2,1)}), bf16[4,3,128,512]{3,2,1,0:T(8,128)(2,1)S(1)}, u32[]{:S(2)}, u32[]{:S(2)}) %all-to-all-start.2) | async-done | bytes 1572896 | tf_op jit(solution)/shard_map/all_to_all | solution.py:622
  215.7 3.6 %all-to-all-start.1 = ((bf16[4,3,128,512]{3,2,1,0:T(8,128)(2,1)}), bf16[4,3,128,512]{3,2,1,0:T(8,128)(2,1)S(1)}, u32[]{:S(2)}, u32[]{:S(2)}) async-start(bf16[4,3,128,512]{3,2,1,0:T(8,128)(2,1)} %get-tuple-element.46), calls=%async_computation.1 | async-start | bytes 3145728 | tf_op jit(solution)/shard_map/all_to_all | solution.py:622
  221.1 4.1 %collective-permute-done.9 = f32[32,1024]{1,0:T(8,128)S(1)} collective-permute-done((f32[32,1024]{1,0:T(8,128)S(1)}, f32[32,1024]{1,0:T(8,128)S(1)}, u32[]{:S(2)}, u32[]{:S(2)}) %collective-permute-start.9) | collective-permute-done | bytes 131104 | tf_op jit(solution)/shard_map/ppermute | solution.py:326
  225.3 8.8 %collective-permute-start.10 = (f32[32,1024]{1,0:T(8,128)S(1)}, f32[32,1024]{1,0:T(8,128)S(1)}, u32[]{:S(2)}, u32[]{:S(2)}) collective-permute-start(f32[32,1024]{1,0:T(8,128)S(1)} %fusion), channel_id=1, source_target_pairs={{0,8},{8,0},{16,24},{24,16},{1,9},{9,1},{17,25},{25,17},{2,10},{10... | collective-permute-start | bytes 393224 | tf_op jit(solution)/shard_map/ppermute | solution.py:326
  234.0 7.6 %collective-permute-done.10 = f32[32,1024]{1,0:T(8,128)S(1)} collective-permute-done((f32[32,1024]{1,0:T(8,128)S(1)}, f32[32,1024]{1,0:T(8,128)S(1)}, u32[]{:S(2)}, u32[]{:S(2)}) %collective-permute-start.10) | collective-permute-done | bytes 131104 | tf_op jit(solution)/shard_map/ppermute | solution.py:326
  241.7 3.0 %collective-permute-start.11 = (f32[32,1024]{1,0:T(8,128)S(1)}, f32[32,1024]{1,0:T(8,128)S(1)}, u32[]{:S(2)}, u32[]{:S(2)}) collective-permute-start(f32[32,1024]{1,0:T(8,128)S(1)} %add.20), channel_id=1, source_target_pairs={{0,16},{8,24},{16,0},{24,8},{1,17},{9,25},{17,1},{25,9},{2,18},{10... | collective-permute-start | bytes 393224 | tf_op jit(solution)/shard_map/ppermute | solution.py:326
  244.7 6.3 %collective-permute-done.11 = f32[32,1024]{1,0:T(8,128)S(1)} collective-permute-done((f32[32,1024]{1,0:T(8,128)S(1)}, f32[32,1024]{1,0:T(8,128)S(1)}, u32[]{:S(2)}, u32[]{:S(2)}) %collective-permute-start.11) | collective-permute-done | bytes 131104 | tf_op jit(solution)/shard_map/ppermute | solution.py:326
  253.5 4.2 %unpack.1 = (bf16[128,4096]{1,0:T(8,128)(2,1)}, bf16[128,4096]{1,0:T(8,128)(2,1)}, bf16[128,4096]{1,0:T(8,128)(2,1)}) custom-call(bf16[4,3,128,512]{3,2,1,0:T(8,128)(2,1)} %copy-done.3, bf16[4,3,128,512]{3,2,1,0:T(8,128)(2,1)} %copy-done.2), custom_call_target="tpu_custom_call" | custom-call | tf_op jit(solution)/shard_map/unpack/pallas_call | solution.py:304
  257.6 2.8 %convert_element_type.7 = f32[1024,512]{1,0:T(8,128)} convert(bf16[1024,512]{1,0:T(8,128)(2,1)} %reduce-scatter.2.cloned.1.call-done) | non-fusion elementwise | flops 524288 | bytes 3145728 | tf_op jit(solution)/shard_map/convert_element_type | solution.py:641
  (72 shorter events, 33.4 us)
Async XLA Ops:
  7.2 88.6 %all-gather.2.cloned.1.call-start = ((), (), s32[]{:S(2)}) async-start(), calls=%async_computation.4 | async-start | bytes 5242880 | tf_op jit(solution)/shard_map/all_gather | solution.py:582
  12.1 42.0 %all-to-all-start = ((bf16[4,3,128,1024]{3,2,1,0:T(8,128)(2,1)}), bf16[4,3,128,1024]{3,2,1,0:T(8,128)(2,1)S(1)}, u32[]{:S(2)}, u32[]{:S(2)}) async-start(bf16[4,3,128,1024]{3,2,1,0:T(8,128)(2,1)} %pack.1.refs_2_), calls=%async_computation | async-start | bytes 6291456 | tf_op jit(solution)/shard_map/all_to_all | solution.py:587
  16.3 241.4 %reduce-scatter.2.cloned.1.call-start = ((), (), s32[]{:S(2)}) async-start(), calls=%async_computation.5 | async-start | bytes 5242880 | tf_op jit(solution)/shard_map/reduce_scatter | solution.py:614
  16.3 24.6 %copy-start.14 = (f32[128,64]{0,1:T(8,128)S(1)}, f32[128,64]{0,1:T(8,128)}, u32[]{:S(2)}) copy-start(f32[128,64]{0,1:T(8,128)} %param.14) | copy-start | bytes 98308
  19.7 15.2 %collective-permute-start = (bf16[128,2048]{1,0:T(8,128)(2,1)}, bf16[128,2048]{1,0:T(8,128)(2,1)S(1)}, u32[]{:S(2)}, u32[]{:S(2)}) collective-permute-start(bf16[128,2048]{1,0:T(8,128)(2,1)} %get-tuple-element.32), channel_id=1, source_target_pairs={{0,4},{4,0},{1,5},{5,1},{2,6},{6,2},{3,7},{7,3},{8,12},{12,8},{9,1... | collective-permute-start | bytes 1572872 | tf_op jit(solution)/shard_map/ppermute | solution.py:322
  35.0 0.8 copy-start.11
  39.2 36.7 %collective-permute-start.1 = (bf16[2,1,128,2048]{3,2,1,0:T(8,128)(2,1)}, bf16[2,1,128,2048]{3,2,1,0:T(8,128)(2,1)}, u32[]{:S(2)}, u32[]{:S(2)}) collective-permute-start(bf16[2,1,128,2048]{3,2,1,0:T(8,128)(2,1)} %join.2.refs_1_.refs_0_), channel_id=1, source_target_pairs={{0,2},{1,3},{2,0},{3,1},{4,6},{5,7},{6,4},{7,5},{8,10},{9,11},{10,... | collective-permute-start | bytes 3145736 | tf_op jit(solution)/shard_map/ppermute | solution.py:326
  54.1 1.6 copy-start
  58.0 17.8 %collective-permute-start.2 = (bf16[176,1024]{1,0:T(8,128)(2,1)}, bf16[176,1024]{1,0:T(8,128)(2,1)S(1)}, u32[]{:S(2)}, u32[]{:S(2)}) collective-permute-start(bf16[176,1024]{1,0:T(8,128)(2,1)} %tail.1), channel_id=1, source_target_pairs={{0,4},{4,8},{8,12},{12,16},{16,20},{20,24},{24,28},{1,5},{5,9},{9,... | collective-permute-start | bytes 1081352 | tf_op jit(solution)/shard_map/ppermute | solution.py:317
  80.4 15.3 %collective-permute-start.3 = (bf16[2,2,128,2048]{3,2,1,0:T(8,128)(2,1)}, bf16[2,2,128,2048]{3,2,1,0:T(8,128)(2,1)S(1)}, u32[]{:S(2)}, u32[]{:S(2)}) collective-permute-start(bf16[2,2,128,2048]{3,2,1,0:T(8,128)(2,1)} %join.3._.a_ref), channel_id=1, source_target_pairs={{0,1},{1,0},{2,3},{3,2},{4,5},{5,4},{6,7},{7,6},{8,9},{9,8},{10,11... | collective-permute-start | bytes 6291464 | tf_op jit(solution)/shard_map/ppermute | solution.py:326
  95.7 1.4 copy-start.1
  97.1 11.0 %copy-start.8 = (bf16[512,512]{1,0:T(8,128)(2,1)S(1)}, bf16[512,512]{1,0:T(8,128)(2,1)}, u32[]{:S(2)}) copy-start(bf16[512,512]{1,0:T(8,128)(2,1)} %get-tuple-element.34._.refs_0_) | copy-start | bytes 1572868
  97.1 11.1 %copy-start.7 = (bf16[512,512]{1,0:T(8,128)(2,1)S(1)}, bf16[512,512]{1,0:T(8,128)(2,1)}, u32[]{:S(2)}) copy-start(bf16[512,512]{1,0:T(8,128)(2,1)} %get-tuple-element.35._.refs_0_) | copy-start | bytes 1572868
  104.3 13.2 %collective-permute-start.5 = (bf16[144,1024]{1,0:T(8,128)(2,1)}, bf16[144,1024]{1,0:T(8,128)(2,1)S(1)}, u32[]{:S(2)}, u32[]{:S(2)}) collective-permute-start(bf16[144,1024]{1,0:T(8,128)(2,1)} %get-tuple-element.42), channel_id=1, source_target_pairs={{0,4},{4,0},{1,5},{5,1},{2,6},{6,2},{3,7},{7,3},{8,12},{12,8},{9,1... | collective-permute-start | bytes 884744 | tf_op jit(solution)/shard_map/ppermute | solution.py:322
  108.1 19.3 %collective-permute-start.8 = (bf16[512,512]{1,0:T(8,128)(2,1)S(1)}, bf16[512,512]{1,0:T(8,128)(2,1)S(1)}, u32[]{:S(2)}, u32[]{:S(2)}) collective-permute-start(bf16[512,512]{1,0:T(8,128)(2,1)S(1)} %copy-done.8), channel_id=1, source_target_pairs={{0,4},{4,0},{1,5},{5,1},{2,6},{6,2},{3,7},{7,3},{8,12},{12,8},{9,1... | collective-permute-start | bytes 1572872 | tf_op jit(solution)/shard_map/ppermute | solution.py:322
  108.2 38.0 %collective-permute-start.7 = (bf16[512,512]{1,0:T(8,128)(2,1)S(1)}, bf16[512,512]{1,0:T(8,128)(2,1)S(1)}, u32[]{:S(2)}, u32[]{:S(2)}) collective-permute-start(bf16[512,512]{1,0:T(8,128)(2,1)S(1)} %copy-done.7), channel_id=1, source_target_pairs={{0,4},{4,0},{1,5},{5,1},{2,6},{6,2},{3,7},{7,3},{8,12},{12,8},{9,1... | collective-permute-start | bytes 1572872 | tf_op jit(solution)/shard_map/ppermute | solution.py:322
  120.9 26.0 %collective-permute-start.6 = (bf16[192,1024]{1,0:T(8,128)(2,1)}, bf16[192,1024]{1,0:T(8,128)(2,1)S(1)}, u32[]{:S(2)}, u32[]{:S(2)}) collective-permute-start(bf16[192,1024]{1,0:T(8,128)(2,1)} %head.1.refs_2_), channel_id=1, source_target_pairs={{4,0},{8,4},{12,8},{16,12},{20,16},{24,20},{28,24},{5,1},{9,5},{13... | collective-permute-start | bytes 1179656 | tf_op jit(solution)/shard_map/ppermute | solution.py:317
  127.4 0.8 copy-start.10
  146.2 0.8 copy-start.12
  153.8 1.2 copy-start.9
  155.0 25.5 %collective-permute-start.4 = (bf16[512,1024]{1,0:T(8,128)(2,1)S(1)}, bf16[512,1024]{1,0:T(8,128)(2,1)S(1)}, u32[]{:S(2)}, u32[]{:S(2)}) collective-permute-start(bf16[512,1024]{1,0:T(8,128)(2,1)S(1)} %copy-done.9), channel_id=1, source_target_pairs={{0,4},{4,0},{1,5},{5,1},{2,6},{6,2},{3,7},{7,3},{8,12},{12,8},{9,1... | collective-permute-start | bytes 3145736 | tf_op jit(solution)/shard_map/ppermute | solution.py:322
  180.5 1.0 copy-start.4
  192.1 23.6 %all-to-all-start.2 = ((bf16[4,3,128,512]{3,2,1,0:T(8,128)(2,1)}), bf16[4,3,128,512]{3,2,1,0:T(8,128)(2,1)S(1)}, u32[]{:S(2)}, u32[]{:S(2)}) async-start(bf16[4,3,128,512]{3,2,1,0:T(8,128)(2,1)} %get-tuple-element.47), calls=%async_computation.2 | async-start | bytes 3145728 | tf_op jit(solution)/shard_map/all_to_all | solution.py:622
  195.7 10.5 %copy-start.17 = (f32[32,128]{1,0:T(8,128)S(1)}, f32[32,128]{1,0:T(8,128)}, u32[]{:S(2)}) copy-start(f32[32,128]{1,0:T(8,128)} %get-tuple-element.54) | copy-start | bytes 49156
  195.7 11.3 %copy-start.16 = (f32[3,8,512]{2,1,0:T(8,128)S(1)}, f32[3,8,512]{2,1,0:T(8,128)}, u32[]{:S(2)}) copy-start(f32[3,8,512]{2,1,0:T(8,128)} %get-tuple-element.52) | copy-start | bytes 147460
  215.7 36.6 %copy-start.2 = (bf16[4,3,128,512]{3,2,1,0:T(8,128)(2,1)}, bf16[4,3,128,512]{3,2,1,0:T(8,128)(2,1)S(1)}, u32[]{:S(2)}) copy-start(bf16[4,3,128,512]{3,2,1,0:T(8,128)(2,1)S(1)} %all-to-all-done.2.refs_1_) | copy-start | bytes 4718596
  215.7 36.6 %all-to-all-start.1 = ((bf16[4,3,128,512]{3,2,1,0:T(8,128)(2,1)}), bf16[4,3,128,512]{3,2,1,0:T(8,128)(2,1)S(1)}, u32[]{:S(2)}, u32[]{:S(2)}) async-start(bf16[4,3,128,512]{3,2,1,0:T(8,128)(2,1)} %get-tuple-element.46), calls=%async_computation.1 | async-start | bytes 3145728 | tf_op jit(solution)/shard_map/all_to_all | solution.py:622
  219.3 5.9 %collective-permute-start.9 = (f32[32,1024]{1,0:T(8,128)S(1)}, f32[32,1024]{1,0:T(8,128)S(1)}, u32[]{:S(2)}, u32[]{:S(2)}) collective-permute-start(f32[32,1024]{1,0:T(8,128)S(1)} %pad_maximum_fusion), channel_id=1, source_target_pairs={{0,4},{4,0},{1,5},{5,1},{2,6},{6,2},{3,7},{7,3},{8,12},{12,8},{9,1... | collective-permute-start | bytes 393224 | tf_op jit(solution)/shard_map/ppermute | solution.py:326
  225.3 16.4 %collective-permute-start.10 = (f32[32,1024]{1,0:T(8,128)S(1)}, f32[32,1024]{1,0:T(8,128)S(1)}, u32[]{:S(2)}, u32[]{:S(2)}) collective-permute-start(f32[32,1024]{1,0:T(8,128)S(1)} %fusion), channel_id=1, source_target_pairs={{0,8},{8,0},{16,24},{24,16},{1,9},{9,1},{17,25},{25,17},{2,10},{10... | collective-permute-start | bytes 393224 | tf_op jit(solution)/shard_map/ppermute | solution.py:326
  241.7 9.3 %collective-permute-start.11 = (f32[32,1024]{1,0:T(8,128)S(1)}, f32[32,1024]{1,0:T(8,128)S(1)}, u32[]{:S(2)}, u32[]{:S(2)}) collective-permute-start(f32[32,1024]{1,0:T(8,128)S(1)} %add.20), channel_id=1, source_target_pairs={{0,16},{8,24},{16,0},{24,8},{1,17},{9,25},{17,1},{25,9},{2,18},{10... | collective-permute-start | bytes 393224 | tf_op jit(solution)/shard_map/ppermute | solution.py:326
  251.1 9.4 %copy-start.15 = (f32[3,8,1024]{2,1,0:T(8,128)}, f32[3,8,1024]{2,1,0:T(8,128)S(1)}, u32[]{:S(2)}) copy-start(f32[3,8,1024]{2,1,0:T(8,128)S(1)} %slice_bitcast_fusion) | copy-start | bytes 294916
  252.3 1.1 copy-start.3
  (3 other events, 2.2 us)
Sparse Core Ops, SparseCore 0:
  9.6 83.4 all-gather.1
  153.9 87.4 reduce-scatter.1
